TPU v7x, 32 devices: a whole 2x2x4 slice. The times are simulated.
32 devices in a mesh: wn: 16 (over z, y, core), tile: 2 (over x).
Axes of the slice: x: 2, y: 2, z: 4, core: 2. Of those that a mesh axis runs over, the one named last changes fastest.
Arguments:
- divergence: float32 [2048, 128, 128], P('wn', 'tile'), may hold values from -6 to 6
- basis: bfloat16 [2048, 2048], P('wn'), may hold values from -0.125 to 0.125
- eigen: float32 [2048], P('wn'), may hold values from 0.1 to 4
- plane_level: int32 [2048], P('wn'), may hold values from 0 to 15
- spacing: float32 [16], replicated, may hold values from 0.3 to 3
- solid: int32 [128, 128], P('tile'), may hold values 0 or 1
Outputs:
- pressure: float32 [2048, 128, 128], P('wn', 'tile')
All inputs are finite; a program needn't handle non-finite values. No bound on the sum of `solid` on one device may be relied on, other than what follows from the above.
Results may differ from a plain program's by a relative error of at most 0.0042.
Values may be sent and summed in bfloat16 or wider, within the bound.
No kernel may reach another device: no remote copies, remote signals or barrier semaphores. Data moves between devices by JAX's collectives and lax.ppermute only.
A program may use at most 64 MiB of HBM per device.

v0:
```python
import math

import jax
import jax.numpy as jnp
from jax import lax
from jax.sharding import PartitionSpec as P

SWEEPS = 4


def with_halo(cells, sides, width):
    for axis, dim in sides:
        count = lax.axis_size(axis)
        head = lax.slice_in_dim(cells, 0, width, axis=dim)
        tail = lax.slice_in_dim(cells, cells.shape[dim] - width, cells.shape[dim], axis=dim)
        cells = jnp.concatenate(
            [
                lax.ppermute(tail, axis, [(i, (i + 1) % count) for i in range(count)]),
                cells,
                lax.ppermute(head, axis, [((i + 1) % count, i) for i in range(count)]),
            ],
            axis=dim,
        )
    return cells


def beside_z(field):
    return jnp.roll(field, 1, 2) + jnp.roll(field, -1, 2)


def local(divergence, basis, eigen, plane_level, spacing, solid):
    planes, width, depth = divergence.shape
    levels = spacing.shape[0]
    onehot = (plane_level[:, None] == jnp.arange(levels, dtype=jnp.int32)[None, :]).astype(
        jnp.float32
    )
    weight = jnp.sum(onehot * spacing[None, :], axis=1)
    scaled = (
        (weight[:, None, None] * divergence).astype(jnp.bfloat16).reshape(planes, width * depth)
    )
    columns = lax.all_to_all(scaled, "wn", split_axis=1, concat_axis=0, tiled=True)
    spectral = lax.dot_general(
        lax.all_gather(basis, "wn", axis=0, tiled=True),
        columns,
        (((0,), (0,)), ((), ())),
        preferred_element_type=jnp.float32,
    )
    spectral = spectral.astype(jnp.bfloat16)
    modes = (
        lax.all_to_all(spectral, "wn", split_axis=0, concat_axis=1, tiled=True)
        .astype(jnp.float32)
        .reshape(planes, width, depth)
    )
    fluid = (1 - solid).astype(jnp.float32)
    diag = eigen[:, None, None] + 4.0
    spread = 4.0 / diag
    field = jnp.zeros((planes, width, depth), jnp.float32)
    for step in range(SWEEPS):
        angle = math.cos(math.pi * (2 * step + 1) / (2 * SWEEPS))
        omega = 1.0 / (1.0 + spread * angle)
        if step == 0:
            remain = modes
        else:
            padded = with_halo(field, (("tile", 1),), 1)
            beside = padded[:, 2:] + padded[:, :-2] + beside_z(field)
            remain = modes - (diag * field - beside)
        field = fluid[None] * (field + omega * remain / diag)
    solved = field.astype(jnp.bfloat16).reshape(planes, width * depth)
    solved_columns = lax.all_to_all(solved, "wn", split_axis=1, concat_axis=0, tiled=True)
    physical = jnp.dot(
        lax.all_gather(basis, "wn", axis=0, tiled=True),
        solved_columns,
        preferred_element_type=jnp.float32,
    )
    pressure = lax.all_to_all(physical, "wn", split_axis=0, concat_axis=1, tiled=True)
    return pressure.reshape(planes, width, depth)


def solution(mesh):
    return jax.shard_map(
        local,
        mesh=mesh,
        in_specs=(P("wn", "tile", None), P("wn", None), P("wn"), P("wn"), P(), P("tile", None)),
        out_specs=P("wn", "tile", None),
        check_vma=False,
    )
```

profile of v0, /device:TPU:0, one launch (start us, length us, event | category | flops | bytes accessed | tf_op | source)
XLA Modules:
  0.0 388.8 jit_solution(9788526915895039521)
XLA Ops:
  6.5 0.0 all-gather.2.cloned.1.call-start
  6.5 0.7 all-gather.2.cloned.1.call-update
  7.3 0.0 copy-start.2
  7.3 0.0 copy-start.3
  7.3 5.4 %copy.22 = f32[128,64,128]{0,2,1:T(8,128)} copy(f32[128,64,128]{2,1,0:T(8,128)} %param.6) | data formatting | bytes 8388608 | tf_op args[0]
  12.7 0.0 copy-done.2
  12.7 0.0 copy-done.3
  12.7 0.1 select_reduce_fusion
  12.8 2.7 multiply_convert_fusion.1
  15.5 95.4 %all_to_all.67 = bf16[128,16,512]{0,2,1:T(8,128)(2,1)S(1)} all-to-all(bf16[128,16,512]{0,2,1:T(8,128)(2,1)S(1)} %bitcast.36), channel_id=1, replica_groups=mesh['wn'=16,'tile'=2] {'wn'}, dimensions={1} | all-to-all | bytes 4194304 | tf_op jit(solution)/shard_map/all_to_all | solution.py:41
  110.9 2.6 copy.23
  113.5 8.4 %all-gather.2.cloned.1.call-done = bf16[2048,2048]{1,0:T(8,128)(2,1)} async-done(((bf16[128,2048]{1,0:T(8,128)(2,1)}), bf16[2048,2048]{1,0:T(8,128)(2,1)}) %all-gather.2.cloned.1.call-update) | async-done | bytes 8388624 | tf_op jit(solution)/shard_map/all_gather | solution.py:71
  121.9 8.6 %fusion.23 = bf16[64,16,8,128]{3,2,1,0:T(8,128)(2,1)S(1)} fusion(bf16[2048,512]{1,0:T(8,128)(2,1)} %bitcast.39, bf16[2048,2048]{1,0:T(8,128)(2,1)} %all-gather.2.cloned.1.call-done), kind=kOutput, calls=%fused_computation.39 | convolution fusion | flops 4296015872 | bytes 12582912 | tf_op jit(solution)/shard_map/dot_general | solution.py:42
  130.5 0.0 copy-start.1
  130.5 0.0 copy-start
  130.5 1.9 copy.33
  132.4 3.9 %all-to-all-start.1 = ((bf16[16,128,512]{1,2,0:T(8,128)(2,1)}), bf16[16,128,512]{1,2,0:T(8,128)(2,1)S(1)}, u32[]{:S(2)}, u32[]{:S(2)}) async-start(bf16[16,128,512]{1,2,0:T(8,128)(2,1)} %bitcast.37), calls=%async_computation.1 | async-start | bytes 4194304 | tf_op jit(solution)/shard_map/all_to_all | solution.py:50
  136.3 0.0 copy-done.1
  136.3 0.0 copy-done
  136.4 40.8 %all-to-all-done.1 = bf16[16,128,512]{1,2,0:T(8,128)(2,1)S(1)} async-done(((bf16[16,128,512]{1,2,0:T(8,128)(2,1)}), bf16[16,128,512]{1,2,0:T(8,128)(2,1)S(1)}, u32[]{:S(2)}, u32[]{:S(2)}) %all-to-all-start.1) | async-done | bytes 2097184 | tf_op jit(solution)/shard_map/all_to_all | solution.py:50
  177.1 0.4 convert_element_type.35
  177.6 1.4 divide_multiply_fusion
  179.0 1.2 fusion.32
  180.1 1.5 collective-permute-start
  181.7 0.6 collective-permute-start.1
  182.3 2.9 collective-permute-done
  185.2 1.2 collective-permute-done.1
  186.4 3.9 fusion.21
  190.3 1.2 fusion.29
  191.4 1.5 collective-permute-start.2
  193.0 0.6 collective-permute-start.3
  193.6 2.8 collective-permute-done.2
  196.3 0.9 collective-permute-done.3
  197.2 3.9 fusion.22
  201.2 1.2 fusion.26
  202.3 1.1 collective-permute-start.4
  203.4 1.0 collective-permute-start.5
  204.5 2.2 collective-permute-done.4
  206.7 1.0 collective-permute-done.5
  207.7 3.9 %multiply_convert_fusion = bf16[128,64,128]{0,2,1:T(8,128)(2,1)S(1)} fusion(f32[128,64,128]{0,2,1:T(8,128)S(1)} %fusion.22, f32[128,64,128]{0,2,1:T(8,128)S(1)} %bitcast.32, f32[128,64,1]{0,2,1:T(1,128)S(1)} %get-tuple-element.10, f32[128,64,127]{0,2,1:T(8,128)S(1)} %get-tuple-element.12, f32[128,64,127]{0,2,1:T(8,128)S(1)} %get-tuple-element.11, ...), kind=kLoop, calls=%fused_computation.31 | loop fusion | flops 15728640 | bytes 19039232 | tf_op jit(solution)/shard_map/convert_element_type | solution.py:68
  211.6 2.6 copy.25
  214.2 57.7 %all_to_all.68 = bf16[128,16,512]{2,0,1:T(8,128)(2,1)S(1)} all-to-all(bf16[128,16,512]{2,0,1:T(8,128)(2,1)} %copy.25), channel_id=1, replica_groups=mesh['wn'=16,'tile'=2] {'wn'}, dimensions={1} | all-to-all | bytes 4194304 | tf_op jit(solution)/shard_map/all_to_all | solution.py:69
  271.9 7.1 %convolution_bitcast_fusion = f32[64,16,8,128]{3,2,1,0:T(8,128)S(1)} fusion(bf16[2048,512]{1,0:T(8,128)(2,1)S(1)} %bitcast.40, bf16[2048,2048]{1,0:T(8,128)(2,1)} %all-gather.2.cloned.1.call-done), kind=kOutput, calls=%fused_computation.37 | convolution fusion | flops 4294967296 | bytes 14680064 | tf_op jit(solution)/shard_map/dot_general | solution.py:70
  279.0 0.4 copy.32
  279.4 97.3 %all_to_all.69 = f32[16,128,512]{1,2,0:T(8,128)} all-to-all(f32[16,128,512]{1,2,0:T(8,128)S(1)} %bitcast.33), channel_id=1, replica_groups=mesh['wn'=16,'tile'=2] {'wn'}, dimensions={0} | all-to-all | bytes 8388608 | tf_op jit(solution)/shard_map/all_to_all | solution.py:75
  376.7 5.3 %copy.27 = f32[128,64,128]{2,1,0:T(8,128)} copy(f32[128,64,128]{0,2,1:T(8,128)} %bitcast.34) | data formatting | bytes 8388608 | tf_op jit(solution)/shard_map/reshape | solution.py:76
  (9 shorter events, 0.2 us)
Async XLA Ops:
  6.5 115.4 %all-gather.2.cloned.1.call-start = ((), (), s32[]{:S(2)}) async-start(), calls=%async_computation.4 | async-start | bytes 8912896 | tf_op jit(solution)/shard_map/all_gather | solution.py:71
  7.3 5.4 %copy-start.2 = (f32[16]{0:T(128)S(1)}, f32[16]{0:T(128)}, u32[]{:S(2)}) copy-start(f32[16]{0:T(128)} %param.10) | copy-start | bytes 196
  7.3 5.4 %copy-start.3 = (s32[128]{0:T(128)S(1)}, s32[128]{0:T(128)}, u32[]{:S(2)}) copy-start(s32[128]{0:T(128)} %param.9) | copy-start | bytes 1540
  130.5 5.8 %copy-start.1 = (f32[128]{0:T(128)S(1)}, f32[128]{0:T(128)}, u32[]{:S(2)}) copy-start(f32[128]{0:T(128)} %param.8) | copy-start | bytes 1540
  130.5 5.8 %copy-start = (s32[64,128]{1,0:T(8,128)S(1)}, s32[64,128]{1,0:T(8,128)}, u32[]{:S(2)}) copy-start(s32[64,128]{1,0:T(8,128)} %param.11) | copy-start | bytes 98308
  132.4 44.8 %all-to-all-start.1 = ((bf16[16,128,512]{1,2,0:T(8,128)(2,1)}), bf16[16,128,512]{1,2,0:T(8,128)(2,1)S(1)}, u32[]{:S(2)}, u32[]{:S(2)}) async-start(bf16[16,128,512]{1,2,0:T(8,128)(2,1)} %bitcast.37), calls=%async_computation.1 | async-start | bytes 4194304 | tf_op jit(solution)/shard_map/all_to_all | solution.py:50
  180.1 5.0 %collective-permute-start = (f32[128,1,128]{0,2,1:T(8,128)S(1)}, f32[128,1,128]{0,2,1:T(8,128)S(1)}, u32[]{:S(2)}, u32[]{:S(2)}) collective-permute-start(f32[128,1,128]{0,2,1:T(8,128)S(1)} %get-tuple-element.19), channel_id=1, source_target_pairs={{1,0},{0,1},{3,2},{2,3},{5,4},{4,5},{7,6},{6,7},{9,8},{8,9},{11,10... | collective-permute-start | bytes 196616 | tf_op jit(solution)/shard_map/ppermute | solution.py:20
  181.7 4.7 %collective-permute-start.1 = (f32[128,1,128]{0,2,1:T(8,128)S(1)}, f32[128,1,128]{0,2,1:T(8,128)S(1)}, u32[]{:S(2)}, u32[]{:S(2)}) collective-permute-start(f32[128,1,128]{0,2,1:T(8,128)S(1)} %get-tuple-element.20), channel_id=1, source_target_pairs={{0,1},{1,0},{2,3},{3,2},{4,5},{5,4},{6,7},{7,6},{8,9},{9,8},{10,11... | collective-permute-start | bytes 196616 | tf_op jit(solution)/shard_map/ppermute | solution.py:18
  191.4 4.9 %collective-permute-start.2 = (f32[128,1,128]{0,2,1:T(8,128)S(1)}, f32[128,1,128]{0,2,1:T(8,128)S(1)}, u32[]{:S(2)}, u32[]{:S(2)}) collective-permute-start(f32[128,1,128]{0,2,1:T(8,128)S(1)} %get-tuple-element.13), channel_id=1, source_target_pairs={{1,0},{0,1},{3,2},{2,3},{5,4},{4,5},{7,6},{6,7},{9,8},{8,9},{11,10... | collective-permute-start | bytes 196616 | tf_op jit(solution)/shard_map/ppermute | solution.py:20
  193.0 4.3 %collective-permute-start.3 = (f32[128,1,128]{0,2,1:T(8,128)S(1)}, f32[128,1,128]{0,2,1:T(8,128)S(1)}, u32[]{:S(2)}, u32[]{:S(2)}) collective-permute-start(f32[128,1,128]{0,2,1:T(8,128)S(1)} %get-tuple-element.14), channel_id=1, source_target_pairs={{0,1},{1,0},{2,3},{3,2},{4,5},{5,4},{6,7},{7,6},{8,9},{9,8},{10,11... | collective-permute-start | bytes 196616 | tf_op jit(solution)/shard_map/ppermute | solution.py:18
  202.3 4.3 %collective-permute-start.4 = (f32[128,1,128]{0,2,1:T(8,128)S(1)}, f32[128,1,128]{0,2,1:T(8,128)S(1)}, u32[]{:S(2)}, u32[]{:S(2)}) collective-permute-start(f32[128,1,128]{0,2,1:T(8,128)S(1)} %get-tuple-element.7), channel_id=1, source_target_pairs={{1,0},{0,1},{3,2},{2,3},{5,4},{4,5},{7,6},{6,7},{9,8},{8,9},{11,10... | collective-permute-start | bytes 196616 | tf_op jit(solution)/shard_map/ppermute | solution.py:20
  203.4 4.3 %collective-permute-start.5 = (f32[128,1,128]{0,2,1:T(8,128)S(1)}, f32[128,1,128]{0,2,1:T(8,128)S(1)}, u32[]{:S(2)}, u32[]{:S(2)}) collective-permute-start(f32[128,1,128]{0,2,1:T(8,128)S(1)} %get-tuple-element.8), channel_id=1, source_target_pairs={{0,1},{1,0},{2,3},{3,2},{4,5},{5,4},{6,7},{7,6},{8,9},{9,8},{10,11... | collective-permute-start | bytes 196616 | tf_op jit(solution)/shard_map/ppermute | solution.py:18
Sparse Core Ops, SparseCore 0:
  9.5 112.3 all-gather.1
where the time goes:
time: 390 us; the launch traced here: 389 us
  blocking collectives  250 us (64%)
  waiting for transfers between devices  60.9 us (16%)
  local copies, waits for them, and re-layouts  21.9 us (6%)
  other arithmetic  16.3 us (4%)
  matrix products  15.6 us (4%)
  between operations  13.6 us (3%)
  starting transfers between devices  10.2 us (3%)
    all_to_all x1, blocking collectives, local(): lax.all_to_all(physical, 'wn', split_axis=0, concat_axis=1, tiled=True)  97.3 us
    all_to_all x1, blocking collectives, local(): lax.all_to_all(scaled, 'wn', split_axis=1, concat_axis=0, tiled=True)  95.4 us
    all_to_all x1, blocking collectives, local(): lax.all_to_all(solved, 'wn', split_axis=1, concat_axis=0, tiled=True)  57.7 us
    all_to_all x1, waiting for transfers between devices, local(): lax.all_to_all(spectral, 'wn', split_axis=0, concat_axis=1, tiled=True)  40.8 us
    mul x3, other arithmetic, local(): field = fluid[None] * (field + omega * remain / diag)  9.16 us
    dot_general x1, matrix products, local(): lax.dot_general(lax.all_gather(basis, 'wn', axis=0, tiled=True), columns,...  8.58 us
    all_gather x1, waiting for transfers between devices, local(): lax.all_gather(basis, 'wn', axis=0, tiled=True)  8.43 us
    ppermute x3, waiting for transfers between devices, with_halo(): lax.ppermute(head, axis, [((i + 1) % count, i) for i in range(count)])  7.83 us
  transfers between devices with their start and end apart: 8, of which 8 were waited for; matrix products, arithmetic and copies ran while one was open for 3% of the time, Pallas kernels for 0%

commit v1 on v0

v1 whole, which is shorter than its diff:
```python
import functools
import math

import jax
import jax.numpy as jnp
from jax import lax
from jax.experimental import pallas as pl
from jax.experimental.pallas import tpu as pltpu
from jax.sharding import PartitionSpec as P

SWEEPS = 4
HALO = SWEEPS - 1
CHUNKS = 2
MIB = 1024 * 1024
F32, BF16 = jnp.float32, jnp.bfloat16


def params(mib):
    return pltpu.CompilerParams(vmem_limit_bytes=mib * MIB)


def cost(flops, nbytes):
    return pl.CostEstimate(flops=int(flops), bytes_accessed=int(nbytes), transcendentals=0)


def scale_body(table, w_ref, e_ref, x_ref, a_ref, b_ref):
    rows = x_ref.shape[1] // 2
    wide = x_ref.shape[2]
    swap = table[1] != 0
    w = w_ref[...]
    for r in range(rows):
        low = (x_ref[:, r, :] * w).T.astype(BF16)
        high = (x_ref[:, rows + r, :] * w).T.astype(BF16)
        a_ref[r * wide : (r + 1) * wide, :] = jnp.where(swap, high, low)
        b_ref[r * wide : (r + 1) * wide, :] = jnp.where(swap, low, high)
    a_ref[rows * wide :, :] = e_ref[...]
    b_ref[rows * wide :, :] = e_ref[...]


def scale_pair(table, weight, extra, divergence, rows):
    planes, _, wide = divergence.shape
    tall = rows * wide + extra.shape[0]
    out = jax.ShapeDtypeStruct((tall, planes), BF16)
    spec = pl.BlockSpec((tall, planes), lambda i, t: (0, 0))
    return pl.pallas_call(
        scale_body,
        grid_spec=pltpu.PrefetchScalarGridSpec(
            num_scalar_prefetch=1,
            grid=(1,),
            in_specs=[
                pl.BlockSpec((planes, 1), lambda i, t: (0, 0)),
                pl.BlockSpec(extra.shape, lambda i, t: (0, 0)),
                pl.BlockSpec((planes, 2 * rows, wide), lambda i, t: (0, t[0], 0)),
            ],
            out_specs=[spec, spec],
        ),
        out_shape=[out, out],
        compiler_params=params(12),
        cost_estimate=cost(planes * rows * wide * 2, planes * rows * wide * 12),
    )(table, weight, extra, divergence)


def place_body(table, *refs):
    a_ref, b_ref, o_ref = refs[0], refs[1], refs[-1]
    rows = o_ref.shape[1] // 2
    wide = o_ref.shape[2]
    swap = table[1] != 0
    for r in range(rows):
        a = a_ref[r * wide : (r + 1) * wide, :].astype(F32)
        b = b_ref[r * wide : (r + 1) * wide, :].astype(F32)
        o_ref[:, r, :] = jnp.where(swap, b, a).T
        o_ref[:, rows + r, :] = jnp.where(swap, a, b).T


def place_pair(table, a, b, out, shape, rows):
    planes, _, wide = shape
    spec = pl.BlockSpec((rows * wide, planes), lambda i, t: (0, 0))
    ins, specs, alias = [a, b], [spec, spec], {}
    if out is not None:
        ins.append(out)
        specs.append(pl.BlockSpec(memory_space=pl.ANY))
        alias = {3: 0}
    return pl.pallas_call(
        place_body,
        grid_spec=pltpu.PrefetchScalarGridSpec(
            num_scalar_prefetch=1,
            grid=(1,),
            in_specs=specs,
            out_specs=pl.BlockSpec((planes, 2 * rows, wide), lambda i, t: (0, t[0], 0)),
        ),
        out_shape=jax.ShapeDtypeStruct(shape, F32),
        input_output_aliases=alias,
        compiler_params=params(12),
        cost_estimate=cost(planes * rows * wide * 2, planes * rows * wide * 12),
    )(table, *ins)


def join_body(layout, blocks, planes, cells, half_ref, *refs):
    n, m = len(layout), len(blocks)
    b_refs, x_refs = refs[:n], refs[n : n + m]
    out_b, out_x, out_e, sem = refs[-4:]
    part = planes // 2
    half = half_ref[0]
    copies = []
    for ref, (kind, ids) in zip(b_refs, layout):
        for j, s in enumerate(ids):
            if kind == "whole":
                src, dst = ref, out_b.at[pl.ds(s * planes, planes), :]
            else:
                side = half if kind == "mine" else 1 - half
                start = pl.multiple_of(s * planes + side * part, part)
                src, dst = ref.at[pl.ds(j * part, part), :], out_b.at[pl.ds(start, part), :]
            copies.append((src, dst))
    for ref, s in zip(x_refs, blocks):
        tail = ref.shape[0] - cells
        copies.append((ref.at[pl.ds(cells, tail), :], out_e.at[s]))
        copies.append((ref.at[pl.ds(0, cells), :], out_x.at[s]))
    handles = [pltpu.make_async_copy(p, q, sem.at[k]) for k, (p, q) in enumerate(copies)]
    for h in handles:
        h.start()
    for h in handles:
        h.wait()


def join(half, pieces, layout, xs, blocks, shapes, held):
    planes, modes, cells, chips = shapes
    count = sum(len(ids) for _, ids in layout) + 2 * len(xs)
    out = [
        jax.ShapeDtypeStruct((chips * planes, modes), BF16),
        jax.ShapeDtypeStruct((chips, cells, planes), BF16),
        jax.ShapeDtypeStruct((chips, 16, planes), BF16),
    ]
    ins = [*pieces, *xs]
    anywhere = pl.BlockSpec(memory_space=pl.ANY)
    specs = [pl.BlockSpec(memory_space=pltpu.SMEM)] + [pl.BlockSpec(memory_space=pltpu.VMEM)] * len(ins)
    alias = {}
    if held is not None:
        alias = {1 + len(ins) + k: k for k in range(3)}
        specs += [anywhere] * 3
        ins += held
    return pl.pallas_call(
        functools.partial(join_body, layout, blocks, planes, cells),
        in_specs=specs,
        out_specs=[anywhere] * 3,
        out_shape=out,
        input_output_aliases=alias,
        scratch_shapes=[pltpu.SemaphoreType.DMA((count,))],
        compiler_params=params(12),
        cost_estimate=cost(0, 4 * sum(v.size for v in [*pieces, *xs])),
    )(half, *ins)


def forward_body(table, x_ref, b_ref, o_ref):
    x = jnp.concatenate([x_ref[k] for k in range(x_ref.shape[0])], axis=1)
    o_ref[...] = jnp.dot(x, b_ref[...], preferred_element_type=F32)


def forward(table, x, basis, modes, tile):
    chips, cells, planes = x.shape
    depth = chips * planes
    return pl.pallas_call(
        forward_body,
        grid_spec=pltpu.PrefetchScalarGridSpec(
            num_scalar_prefetch=1,
            grid=(modes // tile,),
            in_specs=[
                pl.BlockSpec((chips, cells, planes), lambda j, t: (0, 0, 0)),
                pl.BlockSpec((depth, tile), lambda j, t: (0, t[0] + j)),
            ],
            out_specs=pl.BlockSpec((cells, tile), lambda j, t: (0, j)),
        ),
        out_shape=jax.ShapeDtypeStruct((cells, modes), F32),
        compiler_params=params(20),
        cost_estimate=cost(2 * cells * depth * modes, 2 * cells * depth + 2 * depth * modes + 4 * cells * modes),
    )(table, x, basis)


def sweep_body(eigen_ref, fluid_ref, up_ref, own_ref, down_ref, o_ref, rhs, ua, ub):
    rows = own_ref.shape[0]
    ext = rows + 2 * HALO
    diag = eigen_ref[...] + 4.0
    spread = 4.0 / diag
    keep, gain = [], []
    for step in range(SWEEPS):
        omega = 1.0 / (1.0 + spread * math.cos(math.pi * (2 * step + 1) / (2 * SWEEPS)))
        keep.append(1.0 - omega)
        gain.append(omega / diag)

    def load(ref, first):
        def body(r, _):
            s = ref[r].astype(F32)
            rhs[first + r] = s
            ua[first + r] = fluid_ref[first + r] * (gain[0] * s)
            return 0

        lax.fori_loop(0, ref.shape[0], body, 0)

    load(up_ref, 0)
    load(own_ref, HALO)
    load(down_ref, HALO + rows)
    src, dst = ua, ub
    for step in range(1, SWEEPS):
        last = step == SWEEPS - 1

        def body(r, _, src=src, dst=dst, step=step, last=last):
            c = src[r]
            wide = c.shape[0]
            beside = src[r - 1] + src[r + 1] + (pltpu.roll(c, 1, 0) + pltpu.roll(c, wide - 1, 0))
            new = fluid_ref[r] * (keep[step] * c + gain[step] * (rhs[r] + beside))
            if last:
                o_ref[r - HALO] = new.astype(BF16)
            else:
                dst[r] = new
            return 0

        lax.fori_loop(step, ext - step, body, 0)
        src, dst = dst, src


def sweep(eigen, fluid, up, own, down):
    rows, wide, modes = own.shape
    ext, lanes = rows + 2 * HALO, 128
    block = lambda n: pl.BlockSpec((n, wide, lanes), lambda j: (0, 0, j))
    return pl.pallas_call(
        sweep_body,
        grid=(modes // lanes,),
        in_specs=[
            pl.BlockSpec((1, lanes), lambda j: (0, j)),
            pl.BlockSpec((ext, wide, lanes), lambda j: (0, 0, 0)),
            block(HALO),
            block(rows),
            block(HALO),
        ],
        out_specs=block(rows),
        out_shape=jax.ShapeDtypeStruct((rows, wide, modes), BF16),
        scratch_shapes=[pltpu.VMEM((ext, wide, lanes), F32)] * 3,
        compiler_params=params(16),
        cost_estimate=cost(modes * wide * ext * 400, 4 * modes * wide * ext),
    )(eigen, fluid, up, own, down)


def inverse_body(table, *refs):
    parts, b_ref, o_refs = refs[:-3], refs[-3], refs[-2:]
    wide = parts[0].shape[1]
    total = None
    for k, part in enumerate(parts):
        cols = pl.ds(pl.multiple_of(table[k] * wide, wide), wide)
        term = lax.dot_general(
            part[...], b_ref[:, cols], (((1,), (1,)), ((), ())), preferred_element_type=F32
        )
        total = term if total is None else total + term
    planes = b_ref.shape[0] // 2
    o_refs[0][...] = total[:, :planes].astype(BF16)
    o_refs[1][...] = total[:, planes:].astype(BF16)


def inverse(table, parts, basis, pair, planes):
    cells, wide = parts[0].shape
    modes = basis.shape[1]
    tile = min(cells, 512)
    out = jax.ShapeDtypeStruct((cells, planes), BF16)
    return pl.pallas_call(
        inverse_body,
        grid_spec=pltpu.PrefetchScalarGridSpec(
            num_scalar_prefetch=1,
            grid=(cells // tile,),
            in_specs=[pl.BlockSpec((tile, wide), lambda i, t: (i, 0))] * len(parts)
            + [pl.BlockSpec((2 * planes, modes), lambda i, t: (pair, 0))],
            out_specs=[pl.BlockSpec((tile, planes), lambda i, t: (i, 0))] * 2,
        ),
        out_shape=[out, out],
        compiler_params=params(20),
        cost_estimate=cost(4 * cells * modes * planes, 2 * cells * modes + 4 * planes * modes),
    )(table, *parts, basis)


def local(divergence, basis, eigen, plane_level, spacing, solid):
    planes, width, wide = divergence.shape
    wn, tiles = lax.axis_size("wn"), lax.axis_size("tile")
    chips = wn // 2
    rows = width // chips
    cells = rows * wide
    modes = basis.shape[1]
    mine = modes // 2
    me, t = lax.axis_index("wn"), lax.axis_index("tile")
    core, chip = me % 2, me // 2
    z, y, odd = chip // 2, chip % 2, t % 2
    i32 = lambda *v: jnp.stack([jnp.asarray(x, jnp.int32) for x in v])

    flip = lambda s: [(i, i ^ (2 * s)) for i in range(wn)]
    chip_swap = lambda v, s: lax.ppermute(v, "wn", flip(s))
    core_swap = lambda v: lax.ppermute(v, "wn", [(i, i ^ 1) for i in range(wn)])
    tile_swap = lambda v: lax.ppermute(v, "tile", [(i, i ^ 1) for i in range(tiles)])

    def pair_table(i):
        pz = z ^ i
        block = jnp.where(odd == 0, pz, chips // 2 - 1 - pz)
        return i32(block, y ^ (pz % 2) ^ odd)

    tables = [pair_table(i) for i in range(chips // 2)]
    order = lambda g: (g // 2) * 2 + ((g % 2) ^ ((g // 2) % 2))

    def device(tt, g):
        return order(g if tt % 2 == 0 else chips - 1 - g)

    snake = [(tt, device(tt, g)) for tt in range(tiles) for g in range(chips)]
    onward = [
        ((qa * 2 + c) * tiles + ta, (qb * 2 + c) * tiles + tb)
        for (ta, qa), (tb, qb) in zip(snake, snake[1:] + snake[:1])
        for c in range(2)
    ]
    backward = [(b, a) for a, b in onward]

    onehot = (plane_level[:, None] == jnp.arange(spacing.shape[0], dtype=jnp.int32)[None, :]).astype(F32)
    weight = jnp.sum(onehot * spacing[None, :], axis=1)[:, None]

    sibling = core_swap(eigen)
    both = jnp.stack([jnp.where(core == 0, eigen, sibling), jnp.where(core == 0, sibling, eigen)])
    high = lax.reduce_precision(both, 8, 7)
    middle = lax.reduce_precision(both - high, 8, 7)
    low = both - high - middle
    extra = jnp.concatenate([high, middle, low, jnp.zeros((10, planes), F32)]).astype(BF16)

    divergence = pltpu.with_memory_space_constraint(divergence, pltpu.HBM)
    send = [None] * chips
    for i in range(chips // 2):
        send[2 * i], send[2 * i + 1] = scale_pair(tables[i], weight, extra, divergence, rows)
    got = [send[0]] + [None] * (chips - 1)

    half = planes // 2
    steps = (chips // 2).bit_length()
    spread = list(range(1, chips))
    shares = [spread[k * len(spread) // steps : (k + 1) * len(spread) // steps] for k in range(steps)]
    if chips == 8:
        shares = [[1, 3, 5], [4, 6], [7, 2]]
    shares = [[]] + shares
    shapes = (planes, modes, cells, chips)
    state = {"held": None, "pieces": [(basis, ("whole", (0,)))], "blocks": [0]}

    def lay():
        pieces, blocks = state["pieces"], state["blocks"]
        state["pieces"], state["blocks"] = [], []
        state["held"] = join(
            i32(odd), [p for p, _ in pieces], tuple(q for _, q in pieces), [got[s] for s in blocks], blocks, shapes, state["held"]
        )

    def stage(k, *arrived):
        done = [got[s] for s in shares[k - 1]]
        before = state["held"] if k > 1 else send
        arrived, done, before = lax.optimization_barrier((arrived, done, list(before)))
        if k > 1:
            state["held"] = before
        else:
            send[:] = before
            got[0] = send[0]
        for s, v in zip(shares[k - 1], done):
            got[s] = v
            state["blocks"].append(s)
        for s in shares[k]:
            got[s] = chip_swap(send[s], s)
        return arrived

    own = lax.dynamic_slice_in_dim(basis, odd * half, half, 0)
    ids, held = [0], own
    bit, k = chips // 2, 0
    while bit > 1:
        new = chip_swap(held, bit)
        new_ids = [s ^ bit for s in ids]
        k += 1
        held, new = stage(k, held, new)
        state["pieces"].append((new, ("mine", tuple(new_ids))))
        lay()
        held, ids = jnp.concatenate([held, new], 0), ids + new_ids
        bit //= 2
    over_y = chip_swap(held, 1)
    over_x = tile_swap(held[half:])
    over_y, over_x = stage(k + 1, over_y, over_x)
    y_ids, x_ids = [s ^ 1 for s in ids], ids[1:]
    cut = len(ids) // 2
    corner_x = tile_swap(over_y[: cut * half])
    corner_y = chip_swap(over_x[(cut - 1) * half :], 1)
    state["pieces"] += [(over_y, ("mine", tuple(y_ids))), (over_x, ("other", tuple(x_ids)))]
    lay()
    state["pieces"] += [(corner_x, ("other", tuple(y_ids[:cut]))), (corner_y, ("other", tuple(y_ids[cut:])))]
    state["blocks"] += shares[k + 1]
    lay()
    full, x, tails = state["held"]

    inside = (1 - solid).astype(F32)
    ring = jnp.concatenate(
        [
            lax.ppermute(inside[width - HALO :], "tile", [(i, (i + 1) % tiles) for i in range(tiles)]),
            inside,
            lax.ppermute(inside[:HALO], "tile", [((i + 1) % tiles, i) for i in range(tiles)]),
        ]
    )
    e = 2 * z + (y ^ (z % 2))
    g = jnp.where(odd == 0, e, chips - 1 - e)
    fluid = lax.dynamic_slice_in_dim(ring, g * rows, rows + 2 * HALO, 0)
    fluid = jnp.broadcast_to(fluid[:, :, None], fluid.shape + (128,))

    tails = tails.astype(F32)
    values = tails[:, 0:2] + tails[:, 2:4] + tails[:, 4:6]
    want = (core * (chips // 2) + jnp.arange(chips // 2, dtype=jnp.int32)) ^ chip
    pick = want[:, None] == jnp.arange(chips, dtype=jnp.int32)[None, :]
    eigens = jnp.sum(jnp.where(pick[:, :, None, None], values[None], 0.0), axis=1).reshape(1, mine)

    size = mine // CHUNKS
    tile = min(256, size)
    per = size // tile
    halos, solved = [], []
    for j in range(CHUNKS):
        start = i32(((1 - core) * CHUNKS + j) * per, (core * CHUNKS + j) * per)
        if j:
            start, _ = lax.optimization_barrier((start, halos[-1][1]))
        theirs = core_swap(forward(start[:1], x, full, size, tile))
        part = forward(start[1:], x, full, size, tile)
        spectral = (part + theirs).astype(BF16).reshape(rows, wide, size)
        up = lax.ppermute(spectral[rows - HALO :], ("wn", "tile"), onward)
        down = lax.ppermute(spectral[:HALO], ("wn", "tile"), backward)
        halos.append((up, spectral, down))
    others = []
    for j in range(CHUNKS):
        up, spectral, down = halos[j]
        u = sweep(eigens[:, j * size : (j + 1) * size], fluid, up, spectral, down).reshape(cells, size)
        solved.append(u)
        others.append(core_swap(u))

    columns = i32(
        *[core * CHUNKS + j for j in range(CHUNKS)], *[(1 - core) * CHUNKS + j for j in range(CHUNKS)]
    )
    home = [None] * chips
    for i in reversed(range(chips // 2)):
        a, b = inverse(columns, solved + others, full, i, planes)
        columns, a, b = lax.optimization_barrier((columns, a, b))
        home[2 * i + 1] = chip_swap(b, 2 * i + 1)
        home[2 * i] = a if i == 0 else chip_swap(a, 2 * i)

    out = None
    for i in [chips // 2 - 1, *reversed(range(chips // 2 - 2)), chips // 2 - 2]:
        out = place_pair(tables[i], home[2 * i], home[2 * i + 1], out, divergence.shape, rows)
    return out


def solution(mesh):
    return jax.shard_map(
        local,
        mesh=mesh,
        in_specs=(P("wn", "tile", None), P("wn", None), P("wn"), P("wn"), P(), P("tile", None)),
        out_specs=P("wn", "tile", None),
        check_vma=False,
    )
```

time: 390 us -> 202 us (0.52)
  blocking collectives: 250 us -> 0 us
  Pallas kernels: 0 us -> 51.4 us
  starting transfers between devices: 10.2 us -> 54.6 us
  matrix products: 15.6 us -> 0 us
  between operations: 13.6 us -> 0.36 us
  other arithmetic: 16.3 us -> 6.15 us
  waiting for transfers between devices: 60.9 us -> 69.4 us
    all_to_all x3 -> x0, blocking collectives: 250 us -> none  [the longest x1 97.3 us: local(): lax.all_to_all(physical, 'wn', split_axis=0, concat_axis=1, tiled=True)]
    ppermute x6 -> x31, waiting for transfers between devices: 11 us -> 69.4 us  [the longest x18 60.5 us: local(): chip_swap = lambda v, s: lax.ppermute(v, 'wn', flip(s))]
    pallas_call x0 -> x22, Pallas kernels: none -> 51.4 us  [the longest x4 11.2 us: scale_pair(): pl.pallas_call(scale_body, grid_spec=pltpu.PrefetchScalarGridSpec(num_sca...]
    ppermute x6 -> x31, starting transfers between devices: 6.27 us -> 54.6 us  [the longest x18 43.7 us: local(): chip_swap = lambda v, s: lax.ppermute(v, 'wn', flip(s))]
    all_to_all x1 -> x0, waiting for transfers between devices: 40.8 us -> none  [local(): lax.all_to_all(spectral, 'wn', split_axis=0, concat_axis=1, tiled=True)]
    dot_general x2 -> x0, matrix products: 15.6 us -> none  [the longest x1 8.58 us: local(): lax.dot_general(lax.all_gather(basis, 'wn', axis=0, tiled=True), columns,...]
    unnamed x9 -> x30, local copies, waits for them, and re-layouts: 5.43 us -> 14.9 us
    mul x3 -> x0, other arithmetic: 9.16 us -> none  [local(): field = fluid[None] * (field + omega * remain / diag)]
  transfers between devices with their start and end apart: 8 -> 31, of which waited for: 8 -> 16; matrix products, arithmetic and copies ran while one was open for 3% -> 3% of each run, Pallas kernels for 0% -> 20%
where the time goes in v1:
time: 202 us; the launch traced here: 201 us
  waiting for transfers between devices  69.4 us (34%)
  starting transfers between devices  54.6 us (27%)
  Pallas kernels  51.4 us (25%)
  local copies, waits for them, and re-layouts  19 us (9%)
  other arithmetic  6.15 us (3%)
    ppermute x18, waiting for transfers between devices, local(): chip_swap = lambda v, s: lax.ppermute(v, 'wn', flip(s))  60.5 us
    ppermute x18, starting transfers between devices, local(): chip_swap = lambda v, s: lax.ppermute(v, 'wn', flip(s))  43.7 us
    unnamed x30, local copies, waits for them, and re-layouts  14.9 us
    pallas_call x4, Pallas kernels, scale_pair(): pl.pallas_call(scale_body, grid_spec=pltpu.PrefetchScalarGridSpec(num_sca...  11.2 us
    pallas_call x2, Pallas kernels, sweep(): pl.pallas_call(sweep_body, grid=(modes // lanes,), in_specs=[pl.BlockSpec...  10.9 us
    pallas_call x4, Pallas kernels, forward(): pl.pallas_call(forward_body, grid_spec=pltpu.PrefetchScalarGridSpec(num_s...  10.2 us
    pallas_call x4, Pallas kernels, place_pair(): pl.pallas_call(place_body, grid_spec=pltpu.PrefetchScalarGridSpec(num_sca...  8.68 us
    pallas_call x4, Pallas kernels, inverse(): pl.pallas_call(inverse_body, grid_spec=pltpu.PrefetchScalarGridSpec(num_s...  8.32 us
  transfers between devices with their start and end apart: 31, of which 16 were waited for; matrix products, arithmetic and copies ran while one was open for 3% of the time, Pallas kernels for 20%

profile of v1, /device:TPU:0, one launch (start us, length us, event | category | flops | bytes accessed | tf_op | source)
XLA Modules:
  0.0 200.9 jit_solution(12186256817249092192)
XLA Ops:
  0.0 1.0 constant_dynamic-slice_fusion
  1.0 4.1 %collective-permute-start = (bf16[64,2048]{1,0:T(8,128)(2,1)S(1)}, bf16[64,2048]{1,0:T(8,128)(2,1)S(1)}, u32[]{:S(2)}, u32[]{:S(2)}) collective-permute-start(bf16[64,2048]{1,0:T(8,128)(2,1)S(1)} %constant_dynamic-slice_fusion), channel_id=1, source_target_pairs={{0,16},{2,18},{4,20},{6,22},{8,24},{10,26},{12,28},{14,30},{16,0},... | collective-permute-start | bytes 786440 | tf_op jit(solution)/shard_map/ppermute | solution.py:291
  5.1 0.8 select_reduce_fusion.1
  7.1 2.5 %shard_map.64 = (bf16[1040,128]{1,0:T(8,128)(2,1)S(1)}, bf16[1040,128]{1,0:T(8,128)(2,1)S(1)}) custom-call(s32[2]{0:T(128)S(1)} %get-tuple-element.151.table, f32[128,1]{1,0:T(8,128)S(1)} %copy.23.w_ref, bf16[16,128]{1,0:T(8,128)(2,1)S(1)} %maximum_maximum_fusion.e_ref, f32[128,64,128]{2,1,0:T(8,128)} %x_ref.7), custom_call_target="tpu_custom_call" | custom-call | flops 262144 | bytes 1572864 | tf_op jit(solution)/shard_map/pallas_call | solution.py:45
  9.5 3.2 %shard_map.65 = (bf16[1040,128]{1,0:T(8,128)(2,1)}, bf16[1040,128]{1,0:T(8,128)(2,1)S(1)}) custom-call(s32[2]{0:T(128)S(1)} %get-tuple-element.152.table, f32[128,1]{1,0:T(8,128)S(1)} %copy.23.w_ref, bf16[16,128]{1,0:T(8,128)(2,1)S(1)} %maximum_maximum_fusion.e_ref, f32[128,64,128]{2,1,0:T(8,128)} %x_ref.7), custom_call_target="tpu_custom_call" | custom-call | flops 262144 | bytes 1572864 | tf_op jit(solution)/shard_map/pallas_call | solution.py:45
  12.7 2.5 %shard_map.66 = (bf16[1040,128]{1,0:T(8,128)(2,1)S(1)}, bf16[1040,128]{1,0:T(8,128)(2,1)S(1)}) custom-call(s32[2]{0:T(128)S(1)} %get-tuple-element.150.table, f32[128,1]{1,0:T(8,128)S(1)} %copy.23.w_ref, bf16[16,128]{1,0:T(8,128)(2,1)S(1)} %maximum_maximum_fusion.e_ref, f32[128,64,128]{2,1,0:T(8,128)} %x_ref.7), custom_call_target="tpu_custom_call" | custom-call | flops 262144 | bytes 1572864 | tf_op jit(solution)/shard_map/pallas_call | solution.py:45
  15.2 3.1 %shard_map.67 = (bf16[1040,128]{1,0:T(8,128)(2,1)S(1)}, bf16[1040,128]{1,0:T(8,128)(2,1)}) custom-call(s32[2]{0:T(128)S(1)} %get-tuple-element.153.table, f32[128,1]{1,0:T(8,128)S(1)} %copy.23.w_ref, bf16[16,128]{1,0:T(8,128)(2,1)S(1)} %maximum_maximum_fusion.e_ref, f32[128,64,128]{2,1,0:T(8,128)} %x_ref.7), custom_call_target="tpu_custom_call" | custom-call | flops 262144 | bytes 1572864 | tf_op jit(solution)/shard_map/pallas_call | solution.py:45
  18.4 1.7 collective-permute-start.2
  20.0 1.5 collective-permute-start.3
  21.9 1.8 collective-permute-start.5
  23.8 10.3 %collective-permute-done.3.refs_1_ = bf16[1040,128]{1,0:T(8,128)(2,1)S(1)} collective-permute-done((bf16[1040,128]{1,0:T(8,128)(2,1)S(1)}, bf16[1040,128]{1,0:T(8,128)(2,1)S(1)}, u32[]{:S(2)}, u32[]{:S(2)}) %collective-permute-start.3) | collective-permute-done | bytes 266272 | tf_op jit(solution)/shard_map/ppermute | solution.py:291
  34.1 10.9 %collective-permute-done.4.refs_2_ = bf16[1040,128]{1,0:T(8,128)(2,1)S(1)} collective-permute-done((bf16[1040,128]{1,0:T(8,128)(2,1)S(1)}, bf16[1040,128]{1,0:T(8,128)(2,1)S(1)}, u32[]{:S(2)}, u32[]{:S(2)}) %collective-permute-start.4) | collective-permute-done | bytes 266272 | tf_op jit(solution)/shard_map/ppermute | solution.py:291
  45.7 1.6 collective-permute-start.7
  47.3 2.5 %collective-permute-start.8 = (bf16[1040,128]{1,0:T(8,128)(2,1)S(1)}, bf16[1040,128]{1,0:T(8,128)(2,1)S(1)}, u32[]{:S(2)}, u32[]{:S(2)}) collective-permute-start(bf16[1040,128]{1,0:T(8,128)(2,1)S(1)} %get-tuple-element.89), channel_id=1, source_target_pairs={{0,16},{2,18},{4,20},{6,22},{8,24},{10,26},{12,28},{14,30},{16,0},... | collective-permute-start | bytes 798728 | tf_op jit(solution)/shard_map/ppermute | solution.py:291
  49.8 1.5 collective-permute-start.9
  51.4 2.0 copy-done
  53.4 14.4 %collective-permute-done.8.refs_2_ = bf16[1040,128]{1,0:T(8,128)(2,1)S(1)} collective-permute-done((bf16[1040,128]{1,0:T(8,128)(2,1)S(1)}, bf16[1040,128]{1,0:T(8,128)(2,1)S(1)}, u32[]{:S(2)}, u32[]{:S(2)}) %collective-permute-start.8) | collective-permute-done | bytes 266272 | tf_op jit(solution)/shard_map/ppermute | solution.py:291
  67.9 1.9 collective-permute-done.6.refs_0_
  69.8 0.8 slice.61
  70.6 1.5 collective-permute-start.10
  72.1 0.9 slice.62
  73.5 2.4 %collective-permute-start.12 = (bf16[1040,128]{1,0:T(8,128)(2,1)}, bf16[1040,128]{1,0:T(8,128)(2,1)}, u32[]{:S(2)}, u32[]{:S(2)}) collective-permute-start(bf16[1040,128]{1,0:T(8,128)(2,1)} %get-tuple-element.102), channel_id=1, source_target_pairs={{0,28},{2,30},{4,24},{6,26},{8,20},{10,22},{12,16},{14,18},{16,12}... | collective-permute-start | bytes 798728 | tf_op jit(solution)/shard_map/ppermute | solution.py:291
  75.9 1.6 collective-permute-start.13
  77.5 2.2 %copy-done.1 = bf16[1024,2048]{1,0:T(8,128)(2,1)S(1)} copy-done((bf16[1024,2048]{1,0:T(8,128)(2,1)S(1)}, bf16[1024,2048]{1,0:T(8,128)(2,1)}, u32[]{:S(2)}) %copy-start.1) | copy-done | bytes 4194328
  79.7 1.1 copy-done.9
  80.9 0.9 copy-done.12
  82.1 3.7 %collective-permute-done.12.refs_2_ = bf16[1040,128]{1,0:T(8,128)(2,1)} collective-permute-done((bf16[1040,128]{1,0:T(8,128)(2,1)}, bf16[1040,128]{1,0:T(8,128)(2,1)}, u32[]{:S(2)}, u32[]{:S(2)}) %collective-permute-start.12) | collective-permute-done | bytes 266272 | tf_op jit(solution)/shard_map/ppermute | solution.py:291
  85.8 2.4 %collective-permute-done.13.refs_3_ = bf16[1040,128]{1,0:T(8,128)(2,1)} collective-permute-done((bf16[1040,128]{1,0:T(8,128)(2,1)}, bf16[1040,128]{1,0:T(8,128)(2,1)}, u32[]{:S(2)}, u32[]{:S(2)}) %collective-permute-start.13) | collective-permute-done | bytes 266272 | tf_op jit(solution)/shard_map/ppermute | solution.py:291
  88.1 3.0 %collective-permute-done.11.refs_1_ = bf16[128,2048]{1,0:T(8,128)(2,1)} collective-permute-done((bf16[128,2048]{1,0:T(8,128)(2,1)}, bf16[128,2048]{1,0:T(8,128)(2,1)}, u32[]{:S(2)}, u32[]{:S(2)}) %collective-permute-start.11) | collective-permute-done | bytes 524320 | tf_op jit(solution)/shard_map/ppermute | solution.py:291
  91.2 1.6 shard_map.71
  92.8 2.0 copy-done.2
  94.8 2.2 %copy-done.3 = bf16[1024,2048]{1,0:T(8,128)(2,1)S(1)} copy-done((bf16[1024,2048]{1,0:T(8,128)(2,1)S(1)}, bf16[1024,2048]{1,0:T(8,128)(2,1)}, u32[]{:S(2)}) %copy-start.3) | copy-done | bytes 4194328
  97.0 2.7 %shard_map.73 = f32[1024,512]{1,0:T(8,128)} custom-call(s32[1]{0:T(128)} %bitcast.18.table, bf16[8,1024,128]{2,1,0:T(8,128)(2,1)S(1)} %get-tuple-element.113.x_ref, bf16[1024,2048]{1,0:T(8,128)(2,1)S(1)} %copy-done.3), custom_call_target="tpu_custom_call" | custom-call | flops 1073741824 | bytes 5242880 | tf_op jit(solution)/shard_map/pallas_call | solution.py:161
  99.7 2.2 %copy-done.4 = bf16[1024,2048]{1,0:T(8,128)(2,1)S(1)} copy-done((bf16[1024,2048]{1,0:T(8,128)(2,1)S(1)}, bf16[1024,2048]{1,0:T(8,128)(2,1)}, u32[]{:S(2)}) %copy-start.4) | copy-done | bytes 4194328
  101.9 1.7 shard_map.72
  104.1 2.2 %add_convert_fusion.1 = bf16[1024,512]{1,0:T(8,128)(2,1)S(1)} fusion(f32[1024,512]{1,0:T(8,128)S(1)} %shard_map.72, f32[1024,512]{1,0:T(8,128)} %collective-permute-done.16), kind=kLoop, calls=%fused_computation.1 | loop fusion | flops 1048576 | bytes 5242880 | tf_op jit(solution)/shard_map/convert_element_type | solution.py:418
  106.3 0.7 fusion.9
  107.0 3.4 %shard_map.76 = f32[1024,512]{1,0:T(8,128)} custom-call(s32[1]{0:T(128)} %get-tuple-element.148.table, bf16[8,1024,128]{2,1,0:T(8,128)(2,1)S(1)} %get-tuple-element.113.x_ref, bf16[1024,2048]{1,0:T(8,128)(2,1)S(1)} %copy-done.5), custom_call_target="tpu_custom_call" | custom-call | flops 1073741824 | bytes 5242880 | tf_op jit(solution)/shard_map/pallas_call | solution.py:161
  111.0 1.5 collective-permute-start.15
  112.6 1.5 collective-permute-done.14
  115.3 1.5 collective-permute-start.18
  116.8 2.2 %copy-done.6 = bf16[1024,2048]{1,0:T(8,128)(2,1)S(1)} copy-done((bf16[1024,2048]{1,0:T(8,128)(2,1)S(1)}, bf16[1024,2048]{1,0:T(8,128)(2,1)}, u32[]{:S(2)}) %copy-start.6) | copy-done | bytes 4194328
  119.0 2.5 %shard_map.75 = f32[1024,512]{1,0:T(8,128)S(1)} custom-call(s32[1]{0:T(128)} %get-tuple-element.149.table, bf16[8,1024,128]{2,1,0:T(8,128)(2,1)S(1)} %get-tuple-element.113.x_ref, bf16[1024,2048]{1,0:T(8,128)(2,1)S(1)} %copy-done.6), custom_call_target="tpu_custom_call" | custom-call | flops 1073741824 | bytes 5242880 | tf_op jit(solution)/shard_map/pallas_call | solution.py:161
  121.4 1.9 add_convert_fusion
  123.4 3.5 %collective-permute-start.20 = (bf16[3,128,512]{2,1,0:T(8,128)(2,1)S(1)}, bf16[3,128,512]{2,1,0:T(8,128)(2,1)S(1)}, u32[]{:S(2)}, u32[]{:S(2)}) collective-permute-start(bf16[3,128,512]{2,1,0:T(8,128)(2,1)S(1)} %bitcast.46), channel_id=1, source_target_pairs={{0,4},{2,6},{4,12},{6,14},{12,8},{14,10},{8,16},{10,18},{16,20},{1... | collective-permute-start | bytes 1179656 | tf_op jit(solution)/shard_map/ppermute | solution.py:419
  127.1 1.3 collective-permute-done.18.down_ref
  128.7 5.4 %shard_map.74 = bf16[8,128,512]{2,1,0:T(8,128)(2,1)S(1)} custom-call(f32[1,512]{1,0:T(1,128)S(1)} %get-tuple-element.142.eigen_ref, f32[14,128,128]{2,1,0:T(8,128)S(1)} %broadcast_in_dim.44.fluid_ref, bf16[3,128,512]{2,1,0:T(8,128)(2,1)S(1)} %collective-permute-done.17.up_ref, bf16[8,128,512]{2,1,0:T(8,128)(2,1)S(1)} %bitcast.41, ...), custom_call_target="tpu_custom_call" | custom-call | flops 367001600 | bytes 3670016 | tf_op jit(solution)/shard_map/pallas_call | solution.py:224
  134.2 2.4 %collective-permute-done.21.down_ref = bf16[3,128,512]{2,1,0:T(8,128)(2,1)S(1)} collective-permute-done((bf16[3,128,512]{2,1,0:T(8,128)(2,1)S(1)}, bf16[3,128,512]{2,1,0:T(8,128)(2,1)S(1)}, u32[]{:S(2)}, u32[]{:S(2)}) %collective-permute-start.21) | collective-permute-done | bytes 393248 | tf_op jit(solution)/shard_map/ppermute | solution.py:420
  136.7 5.4 %shard_map.77 = bf16[8,128,512]{2,1,0:T(8,128)(2,1)S(1)} custom-call(f32[1,512]{1,0:T(1,128)S(1)} %get-tuple-element.141.eigen_ref, f32[14,128,128]{2,1,0:T(8,128)S(1)} %broadcast_in_dim.44.fluid_ref, bf16[3,128,512]{2,1,0:T(8,128)(2,1)S(1)} %collective-permute-done.20.up_ref, bf16[8,128,512]{2,1,0:T(8,128)(2,1)S(1)} %bitcast.42, ...), custom_call_target="tpu_custom_call" | custom-call | flops 367001600 | bytes 3670016 | tf_op jit(solution)/shard_map/pallas_call | solution.py:224
  142.2 2.6 %collective-permute-done.23.refs_3_ = bf16[1024,512]{1,0:T(8,128)(2,1)S(1)} collective-permute-done((bf16[1024,512]{1,0:T(8,128)(2,1)S(1)}, bf16[1024,512]{1,0:T(8,128)(2,1)S(1)}, u32[]{:S(2)}, u32[]{:S(2)}) %collective-permute-start.23) | collective-permute-done | bytes 1048608 | tf_op jit(solution)/shard_map/ppermute | solution.py:292
  144.8 2.1 %shard_map.78 = (bf16[1024,128]{1,0:T(8,128)(2,1)S(1)}, bf16[1024,128]{1,0:T(8,128)(2,1)S(1)}) custom-call(s32[4]{0:T(128)S(1)} %pad_add_fusion.1.table, bf16[1024,512]{1,0:T(8,128)(2,1)S(1)} %bitcast.32, bf16[1024,512]{1,0:T(8,128)(2,1)S(1)} %bitcast.37, bf16[1024,512]{1,0:T(8,128)(2,1)S(1)} %collective-permute-done.22.refs_2_, ...), custom_call_target="tpu_custom_call" | custom-call | flops 1073741824 | bytes 5242880 | tf_op jit(solution)/shard_map/pallas_call | solution.py:262
  147.0 5.0 %collective-permute-start.30 = (bf16[1024,128]{1,0:T(8,128)(2,1)S(1)}, bf16[1024,128]{1,0:T(8,128)(2,1)S(1)}, u32[]{:S(2)}, u32[]{:S(2)}) collective-permute-start(bf16[1024,128]{1,0:T(8,128)(2,1)S(1)} %get-tuple-element.134), channel_id=1, source_target_pairs={{0,28},{2,30},{4,24},{6,26},{8,20},{10,22},{12,16},{14,18},{16,12}... | collective-permute-start | bytes 786440 | tf_op jit(solution)/shard_map/ppermute | solution.py:291
  152.0 2.1 %shard_map.79 = (bf16[1024,128]{1,0:T(8,128)(2,1)S(1)}, bf16[1024,128]{1,0:T(8,128)(2,1)S(1)}) custom-call(s32[4]{0:T(128)S(1)} %pad_add_fusion.1.table, bf16[1024,512]{1,0:T(8,128)(2,1)S(1)} %bitcast.33, bf16[1024,512]{1,0:T(8,128)(2,1)S(1)} %bitcast.38, bf16[1024,512]{1,0:T(8,128)(2,1)S(1)} %collective-permute-done.22.refs_2_, ...), custom_call_target="tpu_custom_call" | custom-call | flops 1073741824 | bytes 5242880 | tf_op jit(solution)/shard_map/pallas_call | solution.py:262
  154.1 2.1 %shard_map.80 = (bf16[1024,128]{1,0:T(8,128)(2,1)S(1)}, bf16[1024,128]{1,0:T(8,128)(2,1)S(1)}) custom-call(s32[4]{0:T(128)S(1)} %pad_add_fusion.1.table, bf16[1024,512]{1,0:T(8,128)(2,1)S(1)} %bitcast.34, bf16[1024,512]{1,0:T(8,128)(2,1)S(1)} %bitcast.39, bf16[1024,512]{1,0:T(8,128)(2,1)S(1)} %collective-permute-done.22.refs_2_, ...), custom_call_target="tpu_custom_call" | custom-call | flops 1073741824 | bytes 5242880 | tf_op jit(solution)/shard_map/pallas_call | solution.py:262
  156.1 2.1 %shard_map.81 = (bf16[1024,128]{1,0:T(8,128)(2,1)S(1)}, bf16[1024,128]{1,0:T(8,128)(2,1)S(1)}) custom-call(s32[4]{0:T(128)S(1)} %pad_add_fusion.1.table, bf16[1024,512]{1,0:T(8,128)(2,1)S(1)} %bitcast.35, bf16[1024,512]{1,0:T(8,128)(2,1)S(1)} %bitcast.40, bf16[1024,512]{1,0:T(8,128)(2,1)S(1)} %collective-permute-done.22.refs_2_, ...), custom_call_target="tpu_custom_call" | custom-call | flops 1073741824 | bytes 5242880 | tf_op jit(solution)/shard_map/pallas_call | solution.py:262
  158.6 3.2 %collective-permute-start.28 = (bf16[1024,128]{1,0:T(8,128)(2,1)S(1)}, bf16[1024,128]{1,0:T(8,128)(2,1)S(1)}, u32[]{:S(2)}, u32[]{:S(2)}) collective-permute-start(bf16[1024,128]{1,0:T(8,128)(2,1)S(1)} %get-tuple-element.132), channel_id=1, source_target_pairs={{0,12},{2,14},{4,8},{6,10},{8,4},{10,6},{12,0},{14,2},{16,28},{18,... | collective-permute-start | bytes 786440 | tf_op jit(solution)/shard_map/ppermute | solution.py:291
  161.8 6.0 %collective-permute-start.24 = (bf16[1024,128]{1,0:T(8,128)(2,1)S(1)}, bf16[1024,128]{1,0:T(8,128)(2,1)S(1)}, u32[]{:S(2)}, u32[]{:S(2)}) collective-permute-start(bf16[1024,128]{1,0:T(8,128)(2,1)S(1)} %get-tuple-element.121), channel_id=1, source_target_pairs={{0,16},{2,18},{4,20},{6,22},{8,24},{10,26},{12,28},{14,30},{16,0},... | collective-permute-start | bytes 786440 | tf_op jit(solution)/shard_map/ppermute | solution.py:291
  167.8 10.5 %collective-permute-start.25 = (bf16[1024,128]{1,0:T(8,128)(2,1)S(1)}, bf16[1024,128]{1,0:T(8,128)(2,1)S(1)}, u32[]{:S(2)}, u32[]{:S(2)}) collective-permute-start(bf16[1024,128]{1,0:T(8,128)(2,1)S(1)} %get-tuple-element.122), channel_id=1, source_target_pairs={{0,20},{2,22},{4,16},{6,18},{8,28},{10,30},{12,24},{14,26},{16,4},... | collective-permute-start | bytes 786440 | tf_op jit(solution)/shard_map/ppermute | solution.py:291
  178.3 2.2 %shard_map.82.refs_2_ = f32[128,64,128]{2,1,0:T(8,128)} custom-call(s32[2]{0:T(128)S(1)} %get-tuple-element.153.table, bf16[1024,128]{1,0:T(8,128)(2,1)S(1)} %collective-permute-done.29.refs_0_, bf16[1024,128]{1,0:T(8,128)(2,1)S(1)} %collective-permute-done.30.refs_1_), custom_call_target="tpu_custom_call" | custom-call | flops 262144 | bytes 1572864 | tf_op jit(solution)/shard_map/pallas_call | solution.py:83
  180.5 2.2 %shard_map.83.refs_2_ = f32[128,64,128]{2,1,0:T(8,128)} custom-call(s32[2]{0:T(128)S(1)} %get-tuple-element.152.table, bf16[1024,128]{1,0:T(8,128)(2,1)S(1)} %collective-permute-done.27.refs_0_, bf16[1024,128]{1,0:T(8,128)(2,1)S(1)} %collective-permute-done.28.refs_1_, f32[128,64,128]{2,1,0:T(8,128)} %shard_map.82.refs_2_), custom_call_target="tpu_custom_call", output_to_operand_aliasing={{}: (3, {})} | custom-call | flops 262144 | bytes 1572864 | tf_op jit(solution)/shard_map/pallas_call | solution.py:83
  182.7 2.2 %shard_map.84.refs_2_ = f32[128,64,128]{2,1,0:T(8,128)} custom-call(s32[2]{0:T(128)S(1)} %get-tuple-element.151.table, bf16[1024,128]{1,0:T(8,128)(2,1)S(1)} %get-tuple-element.129.refs_0_, bf16[1024,128]{1,0:T(8,128)(2,1)S(1)} %collective-permute-done.26.refs_1_, f32[128,64,128]{2,1,0:T(8,128)} %shard_map.83.refs_2_), custom_call_target="tpu_custom_call", output_to_operand_aliasing={{}: (3, {})} | custom-call | flops 262144 | bytes 1572864 | tf_op jit(solution)/shard_map/pallas_call | solution.py:83
  184.8 8.0 %collective-permute-done.24.refs_0_ = bf16[1024,128]{1,0:T(8,128)(2,1)S(1)} collective-permute-done((bf16[1024,128]{1,0:T(8,128)(2,1)S(1)}, bf16[1024,128]{1,0:T(8,128)(2,1)S(1)}, u32[]{:S(2)}, u32[]{:S(2)}) %collective-permute-start.24) | collective-permute-done | bytes 262176 | tf_op jit(solution)/shard_map/ppermute | solution.py:291
  192.9 5.9 %collective-permute-done.25.refs_1_ = bf16[1024,128]{1,0:T(8,128)(2,1)S(1)} collective-permute-done((bf16[1024,128]{1,0:T(8,128)(2,1)S(1)}, bf16[1024,128]{1,0:T(8,128)(2,1)S(1)}, u32[]{:S(2)}, u32[]{:S(2)}) %collective-permute-start.25) | collective-permute-done | bytes 262176 | tf_op jit(solution)/shard_map/ppermute | solution.py:291
  198.7 2.2 %shard_map.85 = f32[128,64,128]{2,1,0:T(8,128)} custom-call(s32[2]{0:T(128)S(1)} %get-tuple-element.150.table, bf16[1024,128]{1,0:T(8,128)(2,1)S(1)} %collective-permute-done.24.refs_0_, bf16[1024,128]{1,0:T(8,128)(2,1)S(1)} %collective-permute-done.25.refs_1_, f32[128,64,128]{2,1,0:T(8,128)} %shard_map.84.refs_2_), custom_call_target="tpu_custom_call", output_to_operand_aliasing={{}: (3, {})} | custom-call | flops 262144 | bytes 1572864 | tf_op jit(solution)/shard_map/pallas_call | solution.py:83
  (83 shorter events, 7.2 us)
Async XLA Ops:
  1.0 17.3 %collective-permute-start = (bf16[64,2048]{1,0:T(8,128)(2,1)S(1)}, bf16[64,2048]{1,0:T(8,128)(2,1)S(1)}, u32[]{:S(2)}, u32[]{:S(2)}) collective-permute-start(bf16[64,2048]{1,0:T(8,128)(2,1)S(1)} %constant_dynamic-slice_fusion), channel_id=1, source_target_pairs={{0,16},{2,18},{4,20},{6,22},{8,24},{10,26},{12,28},{14,30},{16,0},... | collective-permute-start | bytes 786440 | tf_op jit(solution)/shard_map/ppermute | solution.py:291
  5.1 1.3 collective-permute-start.1
  15.2 8.6 %copy-start.10 = (bf16[128,2048]{1,0:T(8,128)(2,1)S(1)}, bf16[128,2048]{1,0:T(8,128)(2,1)}, u32[]{:S(2)}) copy-start(bf16[128,2048]{1,0:T(8,128)(2,1)} %refs_0_.1) | copy-start | bytes 1572868
  18.4 26.6 %collective-permute-start.2 = (bf16[128,2048]{1,0:T(8,128)(2,1)S(1)}, bf16[128,2048]{1,0:T(8,128)(2,1)S(1)}, u32[]{:S(2)}, u32[]{:S(2)}) collective-permute-start(bf16[128,2048]{1,0:T(8,128)(2,1)S(1)} %constant_dynamic-update-slice_fusion), channel_id=1, source_target_pairs={{0,8},{2,10},{4,12},{6,14},{8,0},{10,2},{12,4},{14,6},{16,24},{18,... | collective-permute-start | bytes 1572872 | tf_op jit(solution)/shard_map/ppermute | solution.py:291
  20.0 14.1 %collective-permute-start.3 = (bf16[1040,128]{1,0:T(8,128)(2,1)S(1)}, bf16[1040,128]{1,0:T(8,128)(2,1)S(1)}, u32[]{:S(2)}, u32[]{:S(2)}) collective-permute-start(bf16[1040,128]{1,0:T(8,128)(2,1)S(1)} %get-tuple-element.80), channel_id=1, source_target_pairs={{0,4},{2,6},{4,0},{6,2},{8,12},{10,14},{12,8},{14,10},{16,20},{18,... | collective-permute-start | bytes 798728 | tf_op jit(solution)/shard_map/ppermute | solution.py:291
  21.5 23.5 %collective-permute-start.4 = (bf16[1040,128]{1,0:T(8,128)(2,1)S(1)}, bf16[1040,128]{1,0:T(8,128)(2,1)S(1)}, u32[]{:S(2)}, u32[]{:S(2)}) collective-permute-start(bf16[1040,128]{1,0:T(8,128)(2,1)S(1)} %get-tuple-element.81), channel_id=1, source_target_pairs={{0,12},{2,14},{4,8},{6,10},{8,4},{10,6},{12,0},{14,2},{16,28},{18,... | collective-permute-start | bytes 798728 | tf_op jit(solution)/shard_map/ppermute | solution.py:291
  21.9 23.1 %collective-permute-start.5 = (bf16[1040,128]{1,0:T(8,128)(2,1)S(1)}, bf16[1040,128]{1,0:T(8,128)(2,1)S(1)}, u32[]{:S(2)}, u32[]{:S(2)}) collective-permute-start(bf16[1040,128]{1,0:T(8,128)(2,1)S(1)} %get-tuple-element.82), channel_id=1, source_target_pairs={{0,20},{2,22},{4,16},{6,18},{8,28},{10,30},{12,24},{14,26},{16,4},... | collective-permute-start | bytes 798728 | tf_op jit(solution)/shard_map/ppermute | solution.py:291
  45.1 24.7 %collective-permute-start.6 = (bf16[256,2048]{1,0:T(8,128)(2,1)S(1)}, bf16[256,2048]{1,0:T(8,128)(2,1)S(1)}, u32[]{:S(2)}, u32[]{:S(2)}) collective-permute-start(bf16[256,2048]{1,0:T(8,128)(2,1)S(1)} %constant_dynamic-update-slice_fusion.2), channel_id=1, source_target_pairs={{0,4},{2,6},{4,0},{6,2},{8,12},{10,14},{12,8},{14,10},{16,20},{18,... | collective-permute-start | bytes 3145736 | tf_op jit(solution)/shard_map/ppermute | solution.py:291
  45.7 22.2 %collective-permute-start.7 = (bf16[192,2048]{1,0:T(8,128)(2,1)S(1)}, bf16[192,2048]{1,0:T(8,128)(2,1)S(1)}, u32[]{:S(2)}, u32[]{:S(2)}) collective-permute-start(bf16[192,2048]{1,0:T(8,128)(2,1)S(1)} %slice.80), channel_id=1, source_target_pairs={{0,1},{1,0},{2,3},{3,2},{4,5},{5,4},{6,7},{7,6},{8,9},{9,8},{10,11... | collective-permute-start | bytes 2359304 | tf_op jit(solution)/shard_map/ppermute | solution.py:293
  47.3 20.6 %collective-permute-start.8 = (bf16[1040,128]{1,0:T(8,128)(2,1)S(1)}, bf16[1040,128]{1,0:T(8,128)(2,1)S(1)}, u32[]{:S(2)}, u32[]{:S(2)}) collective-permute-start(bf16[1040,128]{1,0:T(8,128)(2,1)S(1)} %get-tuple-element.89), channel_id=1, source_target_pairs={{0,16},{2,18},{4,20},{6,22},{8,24},{10,26},{12,28},{14,30},{16,0},... | collective-permute-start | bytes 798728 | tf_op jit(solution)/shard_map/ppermute | solution.py:291
  49.8 18.1 %collective-permute-start.9 = (bf16[1040,128]{1,0:T(8,128)(2,1)S(1)}, bf16[1040,128]{1,0:T(8,128)(2,1)S(1)}, u32[]{:S(2)}, u32[]{:S(2)}) collective-permute-start(bf16[1040,128]{1,0:T(8,128)(2,1)S(1)} %get-tuple-element.90), channel_id=1, source_target_pairs={{0,24},{2,26},{4,28},{6,30},{8,16},{10,18},{12,20},{14,22},{16,8},... | collective-permute-start | bytes 798728 | tf_op jit(solution)/shard_map/ppermute | solution.py:291
  51.4 2.0 %copy-start = (bf16[1024,2048]{1,0:T(8,128)(2,1)}, bf16[1024,2048]{1,0:T(8,128)(2,1)S(1)}, u32[]{:S(2)}) copy-start(bf16[1024,2048]{1,0:T(8,128)(2,1)S(1)} %get-tuple-element.106.refs_4_) | copy-start | bytes 12582916
  67.9 5.1 %copy-start.11 = (bf16[1040,128]{1,0:T(8,128)(2,1)}, bf16[1040,128]{1,0:T(8,128)(2,1)S(1)}, u32[]{:S(2)}) copy-start(bf16[1040,128]{1,0:T(8,128)(2,1)S(1)} %collective-permute-done.9.refs_3_) | copy-start | bytes 798724
  67.9 4.2 %copy-start.8 = (bf16[192,2048]{1,0:T(8,128)(2,1)}, bf16[192,2048]{1,0:T(8,128)(2,1)S(1)}, u32[]{:S(2)}) copy-start(bf16[192,2048]{1,0:T(8,128)(2,1)S(1)} %collective-permute-done.7.refs_1_) | copy-start | bytes 2359300
  70.6 17.5 %collective-permute-start.10 = (bf16[128,2048]{1,0:T(8,128)(2,1)}, bf16[128,2048]{1,0:T(8,128)(2,1)}, u32[]{:S(2)}, u32[]{:S(2)}) collective-permute-start(bf16[128,2048]{1,0:T(8,128)(2,1)} %slice.61), channel_id=1, source_target_pairs={{0,1},{1,0},{2,3},{3,2},{4,5},{5,4},{6,7},{7,6},{8,9},{9,8},{10,11... | collective-permute-start | bytes 1572872 | tf_op jit(solution)/shard_map/ppermute | solution.py:293
  73.0 18.2 %collective-permute-start.11 = (bf16[128,2048]{1,0:T(8,128)(2,1)}, bf16[128,2048]{1,0:T(8,128)(2,1)}, u32[]{:S(2)}, u32[]{:S(2)}) collective-permute-start(bf16[128,2048]{1,0:T(8,128)(2,1)} %slice.62), channel_id=1, source_target_pairs={{0,4},{2,6},{4,0},{6,2},{8,12},{10,14},{12,8},{14,10},{16,20},{18,... | collective-permute-start | bytes 1572872 | tf_op jit(solution)/shard_map/ppermute | solution.py:291
  73.5 12.3 %collective-permute-start.12 = (bf16[1040,128]{1,0:T(8,128)(2,1)}, bf16[1040,128]{1,0:T(8,128)(2,1)}, u32[]{:S(2)}, u32[]{:S(2)}) collective-permute-start(bf16[1040,128]{1,0:T(8,128)(2,1)} %get-tuple-element.102), channel_id=1, source_target_pairs={{0,28},{2,30},{4,24},{6,26},{8,20},{10,22},{12,16},{14,18},{16,12}... | collective-permute-start | bytes 798728 | tf_op jit(solution)/shard_map/ppermute | solution.py:291
  75.9 12.2 %collective-permute-start.13 = (bf16[1040,128]{1,0:T(8,128)(2,1)}, bf16[1040,128]{1,0:T(8,128)(2,1)}, u32[]{:S(2)}, u32[]{:S(2)}) collective-permute-start(bf16[1040,128]{1,0:T(8,128)(2,1)} %get-tuple-element.103), channel_id=1, source_target_pairs={{0,8},{2,10},{4,12},{6,14},{8,0},{10,2},{12,4},{14,6},{16,24},{18,... | collective-permute-start | bytes 798728 | tf_op jit(solution)/shard_map/ppermute | solution.py:291
  77.5 2.2 %copy-start.1 = (bf16[1024,2048]{1,0:T(8,128)(2,1)S(1)}, bf16[1024,2048]{1,0:T(8,128)(2,1)}, u32[]{:S(2)}) copy-start(bf16[1024,2048]{1,0:T(8,128)(2,1)} %copy-done) | copy-start | bytes 12582916
  79.7 1.1 copy-start.9
  80.9 1.0 copy-start.12
  92.8 2.0 %copy-start.2 = (bf16[1024,2048]{1,0:T(8,128)(2,1)}, bf16[1024,2048]{1,0:T(8,128)(2,1)S(1)}, u32[]{:S(2)}) copy-start(bf16[1024,2048]{1,0:T(8,128)(2,1)S(1)} %get-tuple-element.114.b_ref.refs_4_) | copy-start | bytes 12582916
  94.8 2.2 %copy-start.3 = (bf16[1024,2048]{1,0:T(8,128)(2,1)S(1)}, bf16[1024,2048]{1,0:T(8,128)(2,1)}, u32[]{:S(2)}) copy-start(bf16[1024,2048]{1,0:T(8,128)(2,1)} %copy-done.2) | copy-start | bytes 12582916
  99.6 4.5 %collective-permute-start.16 = (f32[1024,512]{1,0:T(8,128)}, f32[1024,512]{1,0:T(8,128)}, u32[]{:S(2)}, u32[]{:S(2)}) collective-permute-start(f32[1024,512]{1,0:T(8,128)} %shard_map.73), channel_id=1, source_target_pairs={{0,2},{2,0},{4,6},{6,4},{8,10},{10,8},{12,14},{14,12},{16,18},{18,... | collective-permute-start | bytes 6291464 | tf_op jit(solution)/shard_map/ppermute | solution.py:292
  99.7 2.2 %copy-start.4 = (bf16[1024,2048]{1,0:T(8,128)(2,1)S(1)}, bf16[1024,2048]{1,0:T(8,128)(2,1)}, u32[]{:S(2)}) copy-start(bf16[1024,2048]{1,0:T(8,128)(2,1)} %copy-done.2) | copy-start | bytes 12582916
  103.6 3.3 %copy-start.5 = (bf16[1024,2048]{1,0:T(8,128)(2,1)S(1)}, bf16[1024,2048]{1,0:T(8,128)(2,1)}, u32[]{:S(2)}) copy-start(bf16[1024,2048]{1,0:T(8,128)(2,1)} %copy-done.2) | copy-start | bytes 12582916
  107.0 3.4 %copy-start.13 = (s32[64,128]{1,0:T(8,128)S(1)}, s32[64,128]{1,0:T(8,128)}, u32[]{:S(2)}) copy-start(s32[64,128]{1,0:T(8,128)} %param.11) | copy-start | bytes 98308
  110.3 11.1 %collective-permute-start.19 = (f32[1024,512]{1,0:T(8,128)}, f32[1024,512]{1,0:T(8,128)}, u32[]{:S(2)}, u32[]{:S(2)}) collective-permute-start(f32[1024,512]{1,0:T(8,128)} %shard_map.76), channel_id=1, source_target_pairs={{0,2},{2,0},{4,6},{6,4},{8,10},{10,8},{12,14},{14,12},{16,18},{18,... | collective-permute-start | bytes 6291464 | tf_op jit(solution)/shard_map/ppermute | solution.py:292
  110.4 3.7 %collective-permute-start.14 = (f32[3,128]{1,0:T(4,128)S(1)}, f32[3,128]{1,0:T(4,128)S(1)}, u32[]{:S(2)}, u32[]{:S(2)}) collective-permute-start(f32[3,128]{1,0:T(4,128)S(1)} %get-tuple-element.140), channel_id=1, source_target_pairs={{0,1},{1,0},{2,3},{3,2},{4,5},{5,4},{6,7},{7,6},{8,9},{9,8},{10,11... | collective-permute-start | bytes 4616 | tf_op jit(solution)/shard_map/ppermute | solution.py:392
  111.0 3.6 %collective-permute-start.15 = (f32[3,128]{1,0:T(4,128)S(1)}, f32[3,128]{1,0:T(4,128)S(1)}, u32[]{:S(2)}, u32[]{:S(2)}) collective-permute-start(f32[3,128]{1,0:T(4,128)S(1)} %get-tuple-element.139), channel_id=1, source_target_pairs={{1,0},{0,1},{3,2},{2,3},{5,4},{4,5},{7,6},{6,7},{9,8},{8,9},{11,10... | collective-permute-start | bytes 4616 | tf_op jit(solution)/shard_map/ppermute | solution.py:394
  114.7 12.4 %collective-permute-start.17 = (bf16[3,128,512]{2,1,0:T(8,128)(2,1)S(1)}, bf16[3,128,512]{2,1,0:T(8,128)(2,1)S(1)}, u32[]{:S(2)}, u32[]{:S(2)}) collective-permute-start(bf16[3,128,512]{2,1,0:T(8,128)(2,1)S(1)} %bitcast.44), channel_id=1, source_target_pairs={{0,4},{2,6},{4,12},{6,14},{12,8},{14,10},{8,16},{10,18},{16,20},{1... | collective-permute-start | bytes 1179656 | tf_op jit(solution)/shard_map/ppermute | solution.py:419
  115.3 13.1 %collective-permute-start.18 = (bf16[3,128,512]{2,1,0:T(8,128)(2,1)S(1)}, bf16[3,128,512]{2,1,0:T(8,128)(2,1)S(1)}, u32[]{:S(2)}, u32[]{:S(2)}) collective-permute-start(bf16[3,128,512]{2,1,0:T(8,128)(2,1)S(1)} %bitcast.43), channel_id=1, source_target_pairs={{4,0},{6,2},{12,4},{14,6},{8,12},{10,14},{16,8},{18,10},{20,16},{2... | collective-permute-start | bytes 1179656 | tf_op jit(solution)/shard_map/ppermute | solution.py:420
  116.8 2.2 %copy-start.6 = (bf16[1024,2048]{1,0:T(8,128)(2,1)S(1)}, bf16[1024,2048]{1,0:T(8,128)(2,1)}, u32[]{:S(2)}) copy-start(bf16[1024,2048]{1,0:T(8,128)(2,1)} %copy-done.2) | copy-start | bytes 12582916
  123.4 10.8 %collective-permute-start.20 = (bf16[3,128,512]{2,1,0:T(8,128)(2,1)S(1)}, bf16[3,128,512]{2,1,0:T(8,128)(2,1)S(1)}, u32[]{:S(2)}, u32[]{:S(2)}) collective-permute-start(bf16[3,128,512]{2,1,0:T(8,128)(2,1)S(1)} %bitcast.46), channel_id=1, source_target_pairs={{0,4},{2,6},{4,12},{6,14},{12,8},{14,10},{8,16},{10,18},{16,20},{1... | collective-permute-start | bytes 1179656 | tf_op jit(solution)/shard_map/ppermute | solution.py:419
  126.9 9.7 %collective-permute-start.21 = (bf16[3,128,512]{2,1,0:T(8,128)(2,1)S(1)}, bf16[3,128,512]{2,1,0:T(8,128)(2,1)S(1)}, u32[]{:S(2)}, u32[]{:S(2)}) collective-permute-start(bf16[3,128,512]{2,1,0:T(8,128)(2,1)S(1)} %bitcast.45), channel_id=1, source_target_pairs={{4,0},{6,2},{12,4},{14,6},{8,12},{10,14},{16,8},{18,10},{20,16},{2... | collective-permute-start | bytes 1179656 | tf_op jit(solution)/shard_map/ppermute | solution.py:420
  128.7 16.1 %copy-start.7 = (bf16[1024,2048]{1,0:T(8,128)(2,1)S(1)}, bf16[1024,2048]{1,0:T(8,128)(2,1)}, u32[]{:S(2)}) copy-start(bf16[1024,2048]{1,0:T(8,128)(2,1)} %copy-done.2) | copy-start | bytes 12582916
  134.2 8.1 %collective-permute-start.22 = (bf16[1024,512]{1,0:T(8,128)(2,1)S(1)}, bf16[1024,512]{1,0:T(8,128)(2,1)S(1)}, u32[]{:S(2)}, u32[]{:S(2)}) collective-permute-start(bf16[1024,512]{1,0:T(8,128)(2,1)S(1)} %bitcast.31), channel_id=1, source_target_pairs={{0,2},{2,0},{4,6},{6,4},{8,10},{10,8},{12,14},{14,12},{16,18},{18,... | collective-permute-start | bytes 3145736 | tf_op jit(solution)/shard_map/ppermute | solution.py:292
  142.1 2.7 %collective-permute-start.23 = (bf16[1024,512]{1,0:T(8,128)(2,1)S(1)}, bf16[1024,512]{1,0:T(8,128)(2,1)S(1)}, u32[]{:S(2)}, u32[]{:S(2)}) collective-permute-start(bf16[1024,512]{1,0:T(8,128)(2,1)S(1)} %bitcast.36), channel_id=1, source_target_pairs={{0,2},{2,0},{4,6},{6,4},{8,10},{10,8},{12,14},{14,12},{16,18},{18,... | collective-permute-start | bytes 3145736 | tf_op jit(solution)/shard_map/ppermute | solution.py:292
  146.9 14.9 %collective-permute-start.29 = (bf16[1024,128]{1,0:T(8,128)(2,1)S(1)}, bf16[1024,128]{1,0:T(8,128)(2,1)S(1)}, u32[]{:S(2)}, u32[]{:S(2)}) collective-permute-start(bf16[1024,128]{1,0:T(8,128)(2,1)S(1)} %get-tuple-element.133), channel_id=1, source_target_pairs={{0,24},{2,26},{4,28},{6,30},{8,16},{10,18},{12,20},{14,22},{16,8},... | collective-permute-start | bytes 786440 | tf_op jit(solution)/shard_map/ppermute | solution.py:291
  147.0 20.8 %collective-permute-start.30 = (bf16[1024,128]{1,0:T(8,128)(2,1)S(1)}, bf16[1024,128]{1,0:T(8,128)(2,1)S(1)}, u32[]{:S(2)}, u32[]{:S(2)}) collective-permute-start(bf16[1024,128]{1,0:T(8,128)(2,1)S(1)} %get-tuple-element.134), channel_id=1, source_target_pairs={{0,28},{2,30},{4,24},{6,26},{8,20},{10,22},{12,16},{14,18},{16,12}... | collective-permute-start | bytes 786440 | tf_op jit(solution)/shard_map/ppermute | solution.py:291
  158.2 24.4 %collective-permute-start.26 = (bf16[1024,128]{1,0:T(8,128)(2,1)S(1)}, bf16[1024,128]{1,0:T(8,128)(2,1)S(1)}, u32[]{:S(2)}, u32[]{:S(2)}) collective-permute-start(bf16[1024,128]{1,0:T(8,128)(2,1)S(1)} %get-tuple-element.130), channel_id=1, source_target_pairs={{0,4},{2,6},{4,0},{6,2},{8,12},{10,14},{12,8},{14,10},{16,20},{18,... | collective-permute-start | bytes 786440 | tf_op jit(solution)/shard_map/ppermute | solution.py:291
  158.6 21.9 %collective-permute-start.27 = (bf16[1024,128]{1,0:T(8,128)(2,1)S(1)}, bf16[1024,128]{1,0:T(8,128)(2,1)S(1)}, u32[]{:S(2)}, u32[]{:S(2)}) collective-permute-start(bf16[1024,128]{1,0:T(8,128)(2,1)S(1)} %get-tuple-element.131), channel_id=1, source_target_pairs={{0,8},{2,10},{4,12},{6,14},{8,0},{10,2},{12,4},{14,6},{16,24},{18,... | collective-permute-start | bytes 786440 | tf_op jit(solution)/shard_map/ppermute | solution.py:291
  158.6 21.9 %collective-permute-start.28 = (bf16[1024,128]{1,0:T(8,128)(2,1)S(1)}, bf16[1024,128]{1,0:T(8,128)(2,1)S(1)}, u32[]{:S(2)}, u32[]{:S(2)}) collective-permute-start(bf16[1024,128]{1,0:T(8,128)(2,1)S(1)} %get-tuple-element.132), channel_id=1, source_target_pairs={{0,12},{2,14},{4,8},{6,10},{8,4},{10,6},{12,0},{14,2},{16,28},{18,... | collective-permute-start | bytes 786440 | tf_op jit(solution)/shard_map/ppermute | solution.py:291
  161.8 31.1 %collective-permute-start.24 = (bf16[1024,128]{1,0:T(8,128)(2,1)S(1)}, bf16[1024,128]{1,0:T(8,128)(2,1)S(1)}, u32[]{:S(2)}, u32[]{:S(2)}) collective-permute-start(bf16[1024,128]{1,0:T(8,128)(2,1)S(1)} %get-tuple-element.121), channel_id=1, source_target_pairs={{0,16},{2,18},{4,20},{6,22},{8,24},{10,26},{12,28},{14,30},{16,0},... | collective-permute-start | bytes 786440 | tf_op jit(solution)/shard_map/ppermute | solution.py:291
  167.8 30.9 %collective-permute-start.25 = (bf16[1024,128]{1,0:T(8,128)(2,1)S(1)}, bf16[1024,128]{1,0:T(8,128)(2,1)S(1)}, u32[]{:S(2)}, u32[]{:S(2)}) collective-permute-start(bf16[1024,128]{1,0:T(8,128)(2,1)S(1)} %get-tuple-element.122), channel_id=1, source_target_pairs={{0,20},{2,22},{4,16},{6,18},{8,28},{10,30},{12,24},{14,26},{16,4},... | collective-permute-start | bytes 786440 | tf_op jit(solution)/shard_map/ppermute | solution.py:291

commit v2 on v1

v2 whole, which is shorter than its diff:
```python
import functools
import math

import jax
import jax.numpy as jnp
from jax import lax
from jax.experimental import pallas as pl
from jax.experimental.pallas import tpu as pltpu
from jax.sharding import PartitionSpec as P

SWEEPS = 4
HALO = SWEEPS - 1
CHUNKS = 2
MIB = 1024 * 1024
F32, BF16 = jnp.float32, jnp.bfloat16


def params(mib):
    return pltpu.CompilerParams(vmem_limit_bytes=mib * MIB)


def cost(flops, nbytes):
    return pl.CostEstimate(flops=int(flops), bytes_accessed=int(nbytes), transcendentals=0)


LATE = pl.CostEstimate(flops=40_000_000_000, bytes_accessed=0, transcendentals=0)


def scale_body(table, w_ref, e_ref, x_ref, *o_refs):
    pairs = len(o_refs) // 2
    rows = x_ref.shape[1] // 2
    wide = x_ref.shape[2]
    w = w_ref[...]
    for i in range(pairs):

        @pl.when(pl.program_id(0) == i)
        def _(i=i):
            swap = table[pairs + i] != 0
            a_ref, b_ref = o_refs[2 * i], o_refs[2 * i + 1]
            for r in range(rows):
                low = (x_ref[:, r, :] * w).astype(BF16).T
                high = (x_ref[:, rows + r, :] * w).astype(BF16).T
                a_ref[r * wide : (r + 1) * wide, :] = jnp.where(swap, high, low)
                b_ref[r * wide : (r + 1) * wide, :] = jnp.where(swap, low, high)
            a_ref[rows * wide :, :] = e_ref[...]
            b_ref[rows * wide :, :] = e_ref[...]


def scale(table, weight, extra, divergence, chips):
    planes, width, wide = divergence.shape
    rows, pairs = width // chips, chips // 2
    tall = rows * wide + extra.shape[0]
    return pl.pallas_call(
        scale_body,
        grid_spec=pltpu.PrefetchScalarGridSpec(
            num_scalar_prefetch=1,
            grid=(pairs,),
            in_specs=[
                pl.BlockSpec((planes, 1), lambda i, t: (0, 0)),
                pl.BlockSpec(extra.shape, lambda i, t: (0, 0)),
                pl.BlockSpec((planes, 2 * rows, wide), lambda i, t: (0, t[i], 0)),
            ],
            out_specs=[pl.BlockSpec(memory_space=pltpu.VMEM)] * chips,
        ),
        out_shape=[jax.ShapeDtypeStruct((tall, planes), BF16)] * chips,
        compiler_params=params(12),
        cost_estimate=cost(planes * width * wide, planes * width * wide * 6),
    )(table, weight, extra, divergence)


def place_body(table, *refs):
    a_ref, b_ref, o_ref = refs[0], refs[1], refs[-1]
    rows = o_ref.shape[1] // 2
    wide = o_ref.shape[2]
    swap = table[1] != 0
    for r in range(rows):
        a = a_ref[r * wide : (r + 1) * wide, :]
        b = b_ref[r * wide : (r + 1) * wide, :]
        o_ref[:, r, :] = jnp.where(swap, b, a).T.astype(F32)
        o_ref[:, rows + r, :] = jnp.where(swap, a, b).T.astype(F32)


def place_pair(table, a, b, out, shape, rows):
    planes, _, wide = shape
    spec = pl.BlockSpec((rows * wide, planes), lambda i, t: (0, 0))
    ins, specs, alias = [a, b], [spec, spec], {}
    if out is not None:
        ins.append(out)
        specs.append(pl.BlockSpec(memory_space=pl.ANY))
        alias = {3: 0}
    return pl.pallas_call(
        place_body,
        grid_spec=pltpu.PrefetchScalarGridSpec(
            num_scalar_prefetch=1,
            grid=(1,),
            in_specs=specs,
            out_specs=pl.BlockSpec((planes, 2 * rows, wide), lambda i, t: (0, t[0], 0)),
        ),
        out_shape=jax.ShapeDtypeStruct(shape, F32),
        input_output_aliases=alias,
        compiler_params=params(12),
        cost_estimate=cost(planes * rows * wide * 2, planes * rows * wide * 12),
    )(table, *ins)


def run_copies(copies, sem):
    handles = [pltpu.make_async_copy(p, q, sem.at[k]) for k, (p, q) in enumerate(copies)]
    for h in handles:
        h.start()
    for h in handles:
        h.wait()


def gather_body(blocks, *refs):
    x_refs, (o_ref, e_ref, sem) = refs[: len(blocks)], refs[-3:]
    cells, planes = o_ref.shape[-2], x_refs[0].shape[1]
    copies = []
    for ref, s in zip(x_refs, blocks):
        tail = ref.shape[0] - cells
        copies.append((ref.at[pl.ds(cells, tail), :], e_ref.at[s]))
        place = o_ref.at[s] if len(o_ref.shape) == 3 else o_ref.at[:, pl.ds(s * planes, planes)]
        copies.append((ref.at[pl.ds(0, cells), :], place))
    run_copies(copies, sem)


def gather(xs, blocks, cells, chips, held, mark):
    tall, planes = xs[0].shape
    out = [
        pltpu.VMEM((chips, cells, planes) if planes % 128 else (cells, chips * planes), BF16),
        pltpu.VMEM((chips, tall - cells, planes), BF16),
    ]
    count = len(xs) + (len(held) if held else 0)
    return pl.pallas_call(
        functools.partial(gather_body, tuple(blocks)),
        in_specs=[pl.BlockSpec(memory_space=pltpu.VMEM)] * count,
        out_specs=[pl.BlockSpec(memory_space=pltpu.VMEM)] * 2,
        out_shape=out,
        input_output_aliases={len(xs): 0, len(xs) + 1: 1} if held else {},
        scratch_shapes=[pltpu.SemaphoreType.DMA((2 * len(xs),))],
        compiler_params=params(12),
        cost_estimate=mark,
    )(*xs, *(held or []))


def join_body(layout, planes, half_ref, *refs):
    b_refs, (out, sem) = refs[: len(layout)], refs[-2:]
    part = planes // 2
    half = half_ref[0]
    copies = []
    for ref, (kind, ids) in zip(b_refs, layout):
        for j, s in enumerate(ids):
            if kind == "whole":
                src, dst = ref, out.at[pl.ds(s * planes, planes), :]
            else:
                side = half if kind == "mine" else 1 - half
                start = pl.multiple_of(s * planes + side * part, part)
                src, dst = ref.at[pl.ds(j * part, part), :], out.at[pl.ds(start, part), :]
            copies.append((src, dst))
    run_copies(copies, sem)


def join(half, pieces, layout, planes, chips, held, mark):
    modes = pieces[0].shape[1]
    home = pl.BlockSpec(memory_space=pltpu.HBM)
    specs = [pl.BlockSpec(memory_space=pltpu.SMEM)] + [pl.BlockSpec(memory_space=pltpu.VMEM)] * len(pieces)
    ins, alias = list(pieces), {}
    if held is not None:
        alias = {1 + len(ins): 0}
        specs.append(home)
        ins.append(held)
    return pl.pallas_call(
        functools.partial(join_body, layout, planes),
        in_specs=specs,
        out_specs=home,
        out_shape=pltpu.HBM((chips * planes, modes), BF16),
        input_output_aliases=alias,
        scratch_shapes=[pltpu.SemaphoreType.DMA((sum(len(ids) for _, ids in layout),))],
        compiler_params=params(12),
        cost_estimate=mark,
    )(half, *ins)


def forward_body(table, x_ref, b_ref, *refs):
    x = x_ref[...]
    if len(x.shape) == 3:
        x = jnp.concatenate([x[k] for k in range(x.shape[0])], axis=1)
    total = jnp.dot(x, b_ref[...], preferred_element_type=F32)
    if len(refs) == 2:
        total = total + refs[0][...]
    refs[-1][...] = total.astype(refs[-1].dtype)


def forward(table, x, basis, modes, tile, theirs=None):
    cells, depth = x.shape[-2], basis.shape[0]
    extra = [] if theirs is None else [theirs]
    return pl.pallas_call(
        forward_body,
        grid_spec=pltpu.PrefetchScalarGridSpec(
            num_scalar_prefetch=1,
            grid=(modes // tile,),
            in_specs=[
                pl.BlockSpec(memory_space=pltpu.VMEM),
                pl.BlockSpec((depth, tile), lambda j, t: (0, t[0] + j)),
            ]
            + [pl.BlockSpec((cells, tile), lambda j, t: (0, j))] * len(extra),
            out_specs=pl.BlockSpec((cells, tile), lambda j, t: (0, j)),
        ),
        out_shape=jax.ShapeDtypeStruct((cells, modes), BF16 if extra else F32),
        compiler_params=params(16),
        cost_estimate=cost(2 * cells * depth * modes, 2 * cells * depth + 2 * depth * modes + 4 * cells * modes),
    )(table, x, basis, *extra)


def sweep_body(eigen_ref, fluid_ref, up_ref, own_ref, down_ref, o_ref, rhs, ua, ub):
    rows = own_ref.shape[0]
    ext = rows + 2 * HALO
    diag = eigen_ref[...] + 4.0
    spread = 4.0 / diag
    keep, gain = [], []
    for step in range(SWEEPS):
        omega = 1.0 / (1.0 + spread * math.cos(math.pi * (2 * step + 1) / (2 * SWEEPS)))
        keep.append(1.0 - omega)
        gain.append(omega / diag)

    def load(ref, first):
        def body(r, _):
            s = ref[r].astype(F32)
            rhs[first + r] = s
            ua[first + r] = fluid_ref[first + r] * (gain[0] * s)
            return 0

        lax.fori_loop(0, ref.shape[0], body, 0)

    load(up_ref, 0)
    load(own_ref, HALO)
    load(down_ref, HALO + rows)
    src, dst = ua, ub
    for step in range(1, SWEEPS):
        last = step == SWEEPS - 1

        def body(r, _, src=src, dst=dst, step=step, last=last):
            c = src[r]
            wide = c.shape[0]
            beside = src[r - 1] + src[r + 1] + (pltpu.roll(c, 1, 0) + pltpu.roll(c, wide - 1, 0))
            new = fluid_ref[r] * (keep[step] * c + gain[step] * (rhs[r] + beside))
            if last:
                o_ref[r - HALO] = new.astype(BF16)
            else:
                dst[r] = new
            return 0

        lax.fori_loop(step, ext - step, body, 0)
        src, dst = dst, src


def sweep(eigen, fluid, up, own, down):
    rows, wide, modes = own.shape
    ext, lanes = rows + 2 * HALO, 128
    block = lambda n: pl.BlockSpec((n, wide, lanes), lambda j: (0, 0, j))
    return pl.pallas_call(
        sweep_body,
        grid=(modes // lanes,),
        in_specs=[
            pl.BlockSpec((1, lanes), lambda j: (0, j)),
            pl.BlockSpec((ext, wide, lanes), lambda j: (0, 0, 0)),
            block(HALO),
            block(rows),
            block(HALO),
        ],
        out_specs=block(rows),
        out_shape=jax.ShapeDtypeStruct((rows, wide, modes), BF16),
        scratch_shapes=[pltpu.VMEM((ext, wide, lanes), F32)] * 3,
        compiler_params=params(16),
        cost_estimate=cost(modes * wide * ext * 400, 4 * modes * wide * ext),
    )(eigen, fluid, up, own, down)


def inverse_body(tile, table, *refs):
    parts, b_ref, o_refs = refs[:-3], refs[-3], refs[-2:]
    cells, wide = parts[0].shape
    planes = o_refs[0].shape[1]

    def body(i, _):
        rows = pl.ds(pl.multiple_of(i * tile, tile), tile)
        total = None
        for k, part in enumerate(parts):
            cols = pl.ds(pl.multiple_of(table[k] * wide, wide), wide)
            term = lax.dot_general(
                part[rows, :], b_ref[:, cols], (((1,), (1,)), ((), ())), preferred_element_type=F32
            )
            total = term if total is None else total + term
        o_refs[0][rows, :] = total[:, :planes].astype(BF16)
        o_refs[1][rows, :] = total[:, planes:].astype(BF16)
        return 0

    lax.fori_loop(0, cells // tile, body, 0)


def inverse(table, parts, basis, pair, planes):
    cells, wide = parts[0].shape
    modes = basis.shape[1]
    out = jax.ShapeDtypeStruct((cells, planes), BF16)
    whole = pl.BlockSpec(memory_space=pltpu.VMEM)
    return pl.pallas_call(
        functools.partial(inverse_body, min(cells, 256)),
        grid=(1,),
        in_specs=[pl.BlockSpec(memory_space=pltpu.SMEM)]
        + [whole] * len(parts)
        + [pl.BlockSpec((2 * planes, modes), lambda i: (pair, 0))],
        out_specs=[whole] * 2,
        out_shape=[out, out],
        compiler_params=params(16),
        cost_estimate=cost(4 * cells * modes * planes, 2 * cells * modes + 4 * planes * modes),
    )(table, *parts, basis)


def local(divergence, basis, eigen, plane_level, spacing, solid):
    planes, width, wide = divergence.shape
    wn, tiles = lax.axis_size("wn"), lax.axis_size("tile")
    chips = wn // 2
    rows = width // chips
    cells = rows * wide
    modes = basis.shape[1]
    mine = modes // 2
    me, t = lax.axis_index("wn"), lax.axis_index("tile")
    core, chip = me % 2, me // 2
    z, y, odd = chip // 2, chip % 2, t % 2
    i32 = lambda *v: jnp.stack([jnp.asarray(x, jnp.int32) for x in v])

    flip = lambda s: [(i, i ^ (2 * s)) for i in range(wn)]
    chip_swap = lambda v, s: lax.ppermute(v, "wn", flip(s))
    core_swap = lambda v: lax.ppermute(v, "wn", [(i, i ^ 1) for i in range(wn)])
    tile_swap = lambda v: lax.ppermute(v, "tile", [(i, i ^ 1) for i in range(tiles)])

    def pair_table(i):
        pz = z ^ i
        block = jnp.where(odd == 0, pz, chips // 2 - 1 - pz)
        return i32(block, y ^ (pz % 2) ^ odd)

    tables = [pair_table(i) for i in range(chips // 2)]
    order = lambda g: (g // 2) * 2 + ((g % 2) ^ ((g // 2) % 2))

    def device(tt, g):
        return order(g if tt % 2 == 0 else chips - 1 - g)

    snake = [(tt, device(tt, g)) for tt in range(tiles) for g in range(chips)]
    onward = [
        ((qa * 2 + c) * tiles + ta, (qb * 2 + c) * tiles + tb)
        for (ta, qa), (tb, qb) in zip(snake, snake[1:] + snake[:1])
        for c in range(2)
    ]
    backward = [(b, a) for a, b in onward]

    onehot = (plane_level[:, None] == jnp.arange(spacing.shape[0], dtype=jnp.int32)[None, :]).astype(F32)
    weight = jnp.sum(onehot * spacing[None, :], axis=1)[:, None]

    sibling = core_swap(eigen)
    both = jnp.stack([jnp.where(core == 0, eigen, sibling), jnp.where(core == 0, sibling, eigen)])
    high = lax.reduce_precision(both, 8, 7)
    middle = lax.reduce_precision(both - high, 8, 7)
    low = both - high - middle
    extra = jnp.concatenate([high, middle, low, jnp.zeros((10, planes), F32)]).astype(BF16)

    inside = (1 - solid).astype(F32)
    edges = [
        lax.ppermute(inside[width - HALO :], "tile", [(i, (i + 1) % tiles) for i in range(tiles)]),
        lax.ppermute(inside[:HALO], "tile", [((i + 1) % tiles, i) for i in range(tiles)]),
    ]

    divergence = pltpu.with_memory_space_constraint(divergence, pltpu.HBM)
    extra, edges = lax.optimization_barrier((extra, edges))
    blocks = [table[0] for table in tables] + [table[1] for table in tables]
    send = scale(i32(*blocks), weight, extra, divergence, chips)

    half = planes // 2
    far = chips // 2
    ids = tuple(range(2, chips, 2))
    odds = tuple(range(1, chips, 2))
    small = cost(0, 1 << 20)

    own = lax.dynamic_slice_in_dim(basis, odd * half, half, 0)
    column = [chip_swap(own, s) for s in ids]
    beside = chip_swap(own, 1)
    layout = (("whole", (0,)), *[("mine", (s,)) for s in ids], ("mine", (1,)))
    full = join(i32(odd), [basis, *column, beside], layout, planes, chips, None, LATE)
    column, beside, full, send = lax.optimization_barrier((column, beside, full, send))

    held = jnp.concatenate(column)
    over_y, over_x = chip_swap(held, 1), tile_swap(jnp.concatenate([held, beside]))
    evens = list(range(far, chips, 2))
    x = gather([send[0], *[chip_swap(send[s], s) for s in evens]], [0, *evens], cells, chips, None, LATE)
    over_y, over_x, x, send = lax.optimization_barrier((over_y, over_x, x, send))

    corner = tile_swap(over_y)
    full = join(i32(odd), [over_y, over_x], (("mine", odds[1:]), ("other", (*ids, 1))), planes, chips, full, small)
    last = list(range(far + 1, chips, 2))
    x = gather([chip_swap(send[s], s) for s in last], last, cells, chips, x, LATE)
    nearby = list(range(1, far))
    x = gather([chip_swap(send[s], s) for s in nearby], nearby, cells, chips, x, small)
    full, x, corner = lax.optimization_barrier((full, x, corner))
    full = join(i32(odd), [corner], (("other", odds[1:]),), planes, chips, full, small)
    x, tails = x

    ring = jnp.concatenate([edges[0], inside, edges[1]])
    e = 2 * z + (y ^ (z % 2))
    g = jnp.where(odd == 0, e, chips - 1 - e)
    fluid = lax.dynamic_slice_in_dim(ring, g * rows, rows + 2 * HALO, 0)
    fluid = jnp.broadcast_to(fluid[:, :, None], fluid.shape + (128,))

    tails = tails.astype(F32)
    values = tails[:, 0:2] + tails[:, 2:4] + tails[:, 4:6]
    want = (core * (chips // 2) + jnp.arange(chips // 2, dtype=jnp.int32)) ^ chip
    pick = want[:, None] == jnp.arange(chips, dtype=jnp.int32)[None, :]
    eigens = jnp.sum(jnp.where(pick[:, :, None, None], values[None], 0.0), axis=1).reshape(1, mine)

    size = mine // CHUNKS
    tile = min(256, size)
    per = size // tile
    stored = pltpu.with_memory_space_constraint(full, pltpu.HBM)
    halos, solved, theirs = [], [], []
    mark = None
    for j in range(CHUNKS):
        start = i32(((1 - core) * CHUNKS + j) * per)
        if mark is not None:
            start, mark = lax.optimization_barrier((start, mark))
        mark = forward(start, x, stored, size, tile)
        theirs.append(core_swap(mark))
    for j in range(CHUNKS):
        start = i32((core * CHUNKS + j) * per)
        start, mark = lax.optimization_barrier((start, mark))
        mark = forward(start, x, stored, size, tile, theirs[j])
        spectral = mark.reshape(rows, wide, size)
        up = lax.ppermute(spectral[rows - HALO :], ("wn", "tile"), onward)
        down = lax.ppermute(spectral[:HALO], ("wn", "tile"), backward)
        halos.append((up, spectral, down))
    others = []
    for j in range(CHUNKS):
        up, spectral, down = halos[j]
        u = sweep(eigens[:, j * size : (j + 1) * size], fluid, up, spectral, down).reshape(cells, size)
        solved.append(u)
        others.append(core_swap(u))

    columns = i32(
        *[core * CHUNKS + j for j in range(CHUNKS)], *[(1 - core) * CHUNKS + j for j in range(CHUNKS)]
    )
    home = [None] * chips
    pairs = list(range(chips // 2))
    for i in [0, *reversed(pairs[1:])]:
        home[2 * i], home[2 * i + 1] = inverse(columns, solved + others, full, i, planes)
    first = [1, *[s for i in reversed(pairs[chips // 4 + 1 :]) for s in (2 * i + 1, 2 * i)]]
    second = [s for i in reversed(pairs[1 : chips // 4 + 1]) for s in (2 * i + 1, 2 * i)]
    held = [home[s] for s in second]
    for s in first:
        home[s] = chip_swap(home[s], s)
    home[1], held = lax.optimization_barrier((home[1], held))
    for s, v in zip(second, held):
        home[s] = chip_swap(v, s)

    out = None
    for i in [0, *pairs[chips // 4 + 1 :], *pairs[1 : chips // 4 + 1]]:
        out = place_pair(tables[i], home[2 * i], home[2 * i + 1], out, divergence.shape, rows)
    return out


def solution(mesh):
    return jax.shard_map(
        local,
        mesh=mesh,
        in_specs=(P("wn", "tile", None), P("wn", None), P("wn"), P("wn"), P(), P("tile", None)),
        out_specs=P("wn", "tile", None),
        check_vma=False,
    )
```

time: 202 us -> 185 us (0.916)
  local copies, waits for them, and re-layouts: 19 us -> 2.85 us
  starting transfers between devices: 54.6 us -> 61.4 us
  waiting for transfers between devices: 69.4 us -> 64.3 us
  other arithmetic: 6.15 us -> 2.91 us
    ppermute x18 -> x19, waiting for transfers between devices: 60.5 us -> 42.8 us  [local(): chip_swap = lambda v, s: lax.ppermute(v, 'wn', flip(s))]
    unnamed x30 -> x12, local copies, waits for them, and re-layouts: 14.9 us -> 1.19 us
    ppermute x2, waiting for transfers between devices: 0.01 us -> 6.99 us  [local(): lax.ppermute(v, 'tile', [(i, i ^ 1) for i in range(tiles)])]
    ppermute x18 -> x19, starting transfers between devices: 43.7 us -> 50.5 us  [local(): chip_swap = lambda v, s: lax.ppermute(v, 'wn', flip(s))]
    ppermute x2, waiting for transfers between devices: 0.01 us -> 4.86 us  [local(): up = lax.ppermute(spectral[rows - HALO:], ('wn', 'tile'), onward)]
    convert_element_type x2 -> x0, other arithmetic: 4.12 us -> none  [local(): spectral = (part + theirs).astype(BF16).reshape(rows, wide, size)]
    pallas_call x4, Pallas kernels: 10.2 us -> 13 us  [forward(): pl.pallas_call(forward_body, grid_spec=pltpu.PrefetchScalarGridSpec(num_s...]
    slice x4 -> x0, local copies, waits for them, and re-layouts: 2.43 us -> none  [the longest x1 0.85 us: local(): corner_y = chip_swap(over_x[(cut - 1) * half:], 1)]
  transfers between devices with their start and end apart: 31 -> 32, of which waited for: 16 -> 18; matrix products, arithmetic and copies ran while one was open for 3% -> 2% of each run, Pallas kernels for 20% -> 23%
where the time goes in v2:
time: 185 us
  waiting for transfers between devices  64.3 us (35%)
  starting transfers between devices  61.4 us (33%)
  Pallas kernels  53.3 us (29%)
  other arithmetic  2.91 us (2%)
  local copies, waits for them, and re-layouts  2.85 us (2%)
    ppermute x19, starting transfers between devices, local(): chip_swap = lambda v, s: lax.ppermute(v, 'wn', flip(s))  50.5 us
    ppermute x19, waiting for transfers between devices, local(): chip_swap = lambda v, s: lax.ppermute(v, 'wn', flip(s))  42.8 us
    pallas_call x4, Pallas kernels, forward(): pl.pallas_call(forward_body, grid_spec=pltpu.PrefetchScalarGridSpec(num_s...  13 us
    pallas_call x2, Pallas kernels, sweep(): pl.pallas_call(sweep_body, grid=(modes // lanes,), in_specs=[pl.BlockSpec...  10.9 us
    pallas_call x4, Pallas kernels, inverse(): pl.pallas_call(functools.partial(inverse_body, min(cells, 256)), grid=(1,...  9.73 us
    pallas_call x4, Pallas kernels, place_pair(): pl.pallas_call(place_body, grid_spec=pltpu.PrefetchScalarGridSpec(num_sca...  8.65 us
    ppermute x2, waiting for transfers between devices, local(): lax.ppermute(v, 'tile', [(i, i ^ 1) for i in range(tiles)])  6.99 us
    pallas_call x1, Pallas kernels, scale(): pl.pallas_call(scale_body, grid_spec=pltpu.PrefetchScalarGridSpec(num_sca...  5.91 us
  transfers between devices with their start and end apart: 32, of which 18 were waited for; matrix products, arithmetic and copies ran while one was open for 2% of the time, Pallas kernels for 23%

profile of v2, /device:TPU:0, one launch (start us, length us, event | category | flops | bytes accessed | tf_op | source)
XLA Modules:
  0.0 185.0 jit_solution(8486163665475138972)
XLA Ops:
  0.0 1.0 constant_dynamic-slice_fusion
  1.0 3.1 %collective-permute-start = (bf16[64,2048]{1,0:T(8,128)(2,1)S(1)}, bf16[64,2048]{1,0:T(8,128)(2,1)S(1)}, u32[]{:S(2)}, u32[]{:S(2)}) collective-permute-start(bf16[64,2048]{1,0:T(8,128)(2,1)S(1)} %constant_dynamic-slice_fusion), channel_id=1, source_target_pairs={{0,8},{2,10},{4,12},{6,14},{8,0},{10,2},{12,4},{14,6},{16,24},{18,... | collective-permute-start | bytes 786440 | tf_op jit(solution)/shard_map/ppermute | solution.py:331
  4.1 2.6 %collective-permute-start.1 = (bf16[64,2048]{1,0:T(8,128)(2,1)S(1)}, bf16[64,2048]{1,0:T(8,128)(2,1)S(1)}, u32[]{:S(2)}, u32[]{:S(2)}) collective-permute-start(bf16[64,2048]{1,0:T(8,128)(2,1)S(1)} %constant_dynamic-slice_fusion), channel_id=1, source_target_pairs={{0,16},{2,18},{4,20},{6,22},{8,24},{10,26},{12,28},{14,30},{16,0},... | collective-permute-start | bytes 786440 | tf_op jit(solution)/shard_map/ppermute | solution.py:331
  6.7 1.7 collective-permute-start.3
  8.4 0.8 select_reduce_fusion.1
  9.3 0.8 subtract_convert_fusion
  10.2 1.6 collective-permute-start.5
  11.8 0.7 fusion.3
  12.4 1.4 collective-permute-done.5
  13.9 1.5 collective-permute-start.6
  15.4 2.0 %collective-permute-done.6 = f32[3,128]{1,0:T(4,128)S(1)} collective-permute-done((f32[3,128]{1,0:T(4,128)S(1)}, f32[3,128]{1,0:T(4,128)S(1)}, u32[]{:S(2)}, u32[]{:S(2)}) %collective-permute-start.6) | collective-permute-done | bytes 1568 | tf_op jit(solution)/shard_map/ppermute | solution.py:367
  17.4 5.9 %shard_map.65 = (bf16[1040,128]{1,0:T(8,128)(2,1)S(1)}, bf16[1040,128]{1,0:T(8,128)(2,1)S(1)}, bf16[1040,128]{1,0:T(8,128)(2,1)S(1)}, bf16[1040,128]{1,0:T(8,128...) custom-call(s32[8]{0:T(128)S(1)} %stack.95.table, ...), custom_call_target="tpu_custom_call" | custom-call | flops 1048576 | bytes 6291456 | tf_op jit(solution)/shard_map/pallas_call | solution.py:53
  23.4 2.1 %collective-permute-done.1.refs_2_ = bf16[64,2048]{1,0:T(8,128)(2,1)S(1)} collective-permute-done((bf16[64,2048]{1,0:T(8,128)(2,1)S(1)}, bf16[64,2048]{1,0:T(8,128)(2,1)S(1)}, u32[]{:S(2)}, u32[]{:S(2)}) %collective-permute-start.1) | collective-permute-done | bytes 262176 | tf_op jit(solution)/shard_map/ppermute | solution.py:331
  25.4 1.2 shard_map.64.refs_2_
  26.7 5.8 %collective-permute-start.9 = (bf16[1040,128]{1,0:T(8,128)(2,1)S(1)}, bf16[1040,128]{1,0:T(8,128)(2,1)S(1)}, u32[]{:S(2)}, u32[]{:S(2)}) collective-permute-start(bf16[1040,128]{1,0:T(8,128)(2,1)S(1)} %get-tuple-element.78), channel_id=1, source_target_pairs={{0,16},{2,18},{4,20},{6,22},{8,24},{10,26},{12,28},{14,30},{16,0},... | collective-permute-start | bytes 798728 | tf_op jit(solution)/shard_map/ppermute | solution.py:331
  32.5 1.4 collective-permute-start.10
  33.9 1.6 collective-permute-start.7
  35.5 1.6 collective-permute-start.8
  37.1 13.3 %collective-permute-done.9.refs_1_ = bf16[1040,128]{1,0:T(8,128)(2,1)S(1)} collective-permute-done((bf16[1040,128]{1,0:T(8,128)(2,1)S(1)}, bf16[1040,128]{1,0:T(8,128)(2,1)S(1)}, u32[]{:S(2)}, u32[]{:S(2)}) %collective-permute-start.9) | collective-permute-done | bytes 266272 | tf_op jit(solution)/shard_map/ppermute | solution.py:331
  50.7 0.9 collective-permute-done.7.refs_0_
  51.5 7.0 %collective-permute-done.8.refs_1_ = bf16[256,2048]{1,0:T(8,128)(2,1)S(1)} collective-permute-done((bf16[256,2048]{1,0:T(8,128)(2,1)S(1)}, bf16[256,2048]{1,0:T(8,128)(2,1)S(1)}, u32[]{:S(2)}, u32[]{:S(2)}) %collective-permute-start.8) | collective-permute-done | bytes 1048608 | tf_op jit(solution)/shard_map/ppermute | solution.py:333
  58.5 2.8 %collective-permute-start.15 = (bf16[1040,128]{1,0:T(8,128)(2,1)}, bf16[1040,128]{1,0:T(8,128)(2,1)}, u32[]{:S(2)}, u32[]{:S(2)}) collective-permute-start(bf16[1040,128]{1,0:T(8,128)(2,1)} %get-tuple-element.94), channel_id=1, source_target_pairs={{0,28},{2,30},{4,24},{6,26},{8,20},{10,22},{12,16},{14,18},{16,12}... | collective-permute-start | bytes 798728 | tf_op jit(solution)/shard_map/ppermute | solution.py:331
  61.4 1.1 collective-permute-start.11
  62.5 1.0 collective-permute-start.12
  63.4 1.5 collective-permute-start.16
  64.9 1.2 copy-done.2
  66.1 1.3 shard_map.67.refs_1_
  67.4 9.5 %collective-permute-done.14.refs_0_ = bf16[1040,128]{1,0:T(8,128)(2,1)} collective-permute-done((bf16[1040,128]{1,0:T(8,128)(2,1)}, bf16[1040,128]{1,0:T(8,128)(2,1)}, u32[]{:S(2)}, u32[]{:S(2)}) %collective-permute-start.14) | collective-permute-done | bytes 266272 | tf_op jit(solution)/shard_map/ppermute | solution.py:331
  76.9 1.2 shard_map.68
  78.1 0.6 collective-permute-done.12.refs_1_
  78.7 7.2 %collective-permute-done.13.refs_2_ = bf16[1040,128]{1,0:T(8,128)(2,1)S(1)} collective-permute-done((bf16[1040,128]{1,0:T(8,128)(2,1)S(1)}, bf16[1040,128]{1,0:T(8,128)(2,1)S(1)}, u32[]{:S(2)}, u32[]{:S(2)}) %collective-permute-start.13) | collective-permute-done | bytes 266272 | tf_op jit(solution)/shard_map/ppermute | solution.py:331
  86.0 0.3 shard_map.69
  86.3 0.9 shard_map.70.b_ref.refs_4_
  87.2 3.6 %shard_map.71 = f32[1024,512]{1,0:T(8,128)} custom-call(s32[1]{0:T(128)} %bitcast.19.table, bf16[1024,1024]{1,0:T(8,128)(2,1)S(1)} %get-tuple-element.104.x_ref, bf16[1024,2048]{1,0:T(8,128)(2,1)} %shard_map.70.b_ref.refs_4_), custom_call_target="tpu_custom_call" | custom-call | flops 1073741824 | bytes 5242880 | tf_op jit(solution)/shard_map/pallas_call | solution.py:196
  90.8 3.6 %shard_map.72 = f32[1024,512]{1,0:T(8,128)} custom-call(s32[1]{0:T(128)} %bitcast.18.table, bf16[1024,1024]{1,0:T(8,128)(2,1)S(1)} %get-tuple-element.104.x_ref, bf16[1024,2048]{1,0:T(8,128)(2,1)} %shard_map.70.b_ref.refs_4_), custom_call_target="tpu_custom_call" | custom-call | flops 1073741824 | bytes 5242880 | tf_op jit(solution)/shard_map/pallas_call | solution.py:196
  94.3 0.5 collective-permute-start.20
  95.0 0.3 collective-permute-done.17.refs_0_
  95.3 2.9 %shard_map.73 = bf16[1024,512]{1,0:T(8,128)(2,1)S(1)} custom-call(s32[1]{0:T(128)} %bitcast.17.table, bf16[1024,1024]{1,0:T(8,128)(2,1)S(1)} %get-tuple-element.104.x_ref, bf16[1024,2048]{1,0:T(8,128)(2,1)} %shard_map.70.b_ref.refs_4_, f32[1024,512]{1,0:T(8,128)} %collective-permute-done.17.refs_0_), custom_call_target="tpu_custom_call" | custom-call | flops 1073741824 | bytes 5242880 | tf_op jit(solution)/shard_map/pallas_call | solution.py:196
  98.3 0.7 collective-permute-start.18
  99.0 1.3 collective-permute-start.19
  100.3 2.9 %shard_map.75 = bf16[1024,512]{1,0:T(8,128)(2,1)S(1)} custom-call(s32[1]{0:T(128)} %bitcast.24.table, bf16[1024,1024]{1,0:T(8,128)(2,1)S(1)} %get-tuple-element.104.x_ref, bf16[1024,2048]{1,0:T(8,128)(2,1)} %shard_map.70.b_ref.refs_4_, f32[1024,512]{1,0:T(8,128)} %collective-permute-done.20.refs_0_), custom_call_target="tpu_custom_call" | custom-call | flops 1073741824 | bytes 5242880 | tf_op jit(solution)/shard_map/pallas_call | solution.py:196
  103.3 1.7 collective-permute-start.21
  105.0 0.4 collective-permute-start.22
  105.5 4.7 %collective-permute-done.18.up_ref = bf16[3,128,512]{2,1,0:T(8,128)(2,1)S(1)} collective-permute-done((bf16[3,128,512]{2,1,0:T(8,128)(2,1)S(1)}, bf16[3,128,512]{2,1,0:T(8,128)(2,1)S(1)}, u32[]{:S(2)}, u32[]{:S(2)}) %collective-permute-start.18) | collective-permute-done | bytes 393248 | tf_op jit(solution)/shard_map/ppermute | solution.py:433
  110.3 1.7 collective-permute-done.19.down_ref
  112.2 5.4 %shard_map.74 = bf16[8,128,512]{2,1,0:T(8,128)(2,1)S(1)} custom-call(f32[1,512]{1,0:T(1,128)S(1)} %get-tuple-element.130.eigen_ref, f32[14,128,128]{2,1,0:T(8,128)S(1)} %broadcast_in_dim.44.fluid_ref, bf16[3,128,512]{2,1,0:T(8,128)(2,1)S(1)} %collective-permute-done.18.up_ref, bf16[8,128,512]{2,1,0:T(8,128)(2,1)S(1)} %bitcast.41, ...), custom_call_target="tpu_custom_call" | custom-call | flops 367001600 | bytes 3670016 | tf_op jit(solution)/shard_map/pallas_call | solution.py:260
  117.9 1.6 collective-permute-done.22.down_ref
  119.5 5.4 %shard_map.76 = bf16[8,128,512]{2,1,0:T(8,128)(2,1)S(1)} custom-call(f32[1,512]{1,0:T(1,128)S(1)} %get-tuple-element.129.eigen_ref, f32[14,128,128]{2,1,0:T(8,128)S(1)} %broadcast_in_dim.44.fluid_ref, bf16[3,128,512]{2,1,0:T(8,128)(2,1)S(1)} %collective-permute-done.21.up_ref, bf16[8,128,512]{2,1,0:T(8,128)(2,1)S(1)} %bitcast.42, ...), custom_call_target="tpu_custom_call" | custom-call | flops 367001600 | bytes 3670016 | tf_op jit(solution)/shard_map/pallas_call | solution.py:260
  125.1 2.6 %collective-permute-done.24.refs_3_ = bf16[1024,512]{1,0:T(8,128)(2,1)S(1)} collective-permute-done((bf16[1024,512]{1,0:T(8,128)(2,1)S(1)}, bf16[1024,512]{1,0:T(8,128)(2,1)S(1)}, u32[]{:S(2)}, u32[]{:S(2)}) %collective-permute-start.24) | collective-permute-done | bytes 1048608 | tf_op jit(solution)/shard_map/ppermute | solution.py:332
  127.7 2.4 %shard_map.77 = (bf16[1024,128]{1,0:T(8,128)(2,1)S(1)}, bf16[1024,128]{1,0:T(8,128)(2,1)S(1)}) custom-call(s32[4]{0:T(128)S(1)} %pad_add_fusion.1.table, bf16[1024,512]{1,0:T(8,128)(2,1)S(1)} %bitcast.32, bf16[1024,512]{1,0:T(8,128)(2,1)S(1)} %bitcast.37, bf16[1024,512]{1,0:T(8,128)(2,1)S(1)} %collective-permute-done.23.refs_2_, ...), custom_call_target="tpu_custom_call" | custom-call | flops 1073741824 | bytes 5242880 | tf_op jit(solution)/shard_map/pallas_call | solution.py:304
  130.1 1.8 collective-permute-start.25
  132.0 2.4 %shard_map.80 = (bf16[1024,128]{1,0:T(8,128)(2,1)S(1)}, bf16[1024,128]{1,0:T(8,128)(2,1)S(1)}) custom-call(s32[4]{0:T(128)S(1)} %pad_add_fusion.1.table, bf16[1024,512]{1,0:T(8,128)(2,1)S(1)} %bitcast.33, bf16[1024,512]{1,0:T(8,128)(2,1)S(1)} %bitcast.38, bf16[1024,512]{1,0:T(8,128)(2,1)S(1)} %collective-permute-done.23.refs_2_, ...), custom_call_target="tpu_custom_call" | custom-call | flops 1073741824 | bytes 5242880 | tf_op jit(solution)/shard_map/pallas_call | solution.py:304
  134.5 3.5 %collective-permute-start.31 = (bf16[1024,128]{1,0:T(8,128)(2,1)S(1)}, bf16[1024,128]{1,0:T(8,128)(2,1)S(1)}, u32[]{:S(2)}, u32[]{:S(2)}) collective-permute-start(bf16[1024,128]{1,0:T(8,128)(2,1)S(1)} %get-tuple-element.120), channel_id=1, source_target_pairs={{0,28},{2,30},{4,24},{6,26},{8,20},{10,22},{12,16},{14,18},{16,12}... | collective-permute-start | bytes 786440 | tf_op jit(solution)/shard_map/ppermute | solution.py:331
  138.0 2.4 %shard_map.78 = (bf16[1024,128]{1,0:T(8,128)(2,1)S(1)}, bf16[1024,128]{1,0:T(8,128)(2,1)S(1)}) custom-call(s32[4]{0:T(128)S(1)} %pad_add_fusion.1.table, bf16[1024,512]{1,0:T(8,128)(2,1)S(1)} %bitcast.34, bf16[1024,512]{1,0:T(8,128)(2,1)S(1)} %bitcast.39, bf16[1024,512]{1,0:T(8,128)(2,1)S(1)} %collective-permute-done.23.refs_2_, ...), custom_call_target="tpu_custom_call" | custom-call | flops 1073741824 | bytes 5242880 | tf_op jit(solution)/shard_map/pallas_call | solution.py:304
  140.4 2.4 %shard_map.79 = (bf16[1024,128]{1,0:T(8,128)(2,1)S(1)}, bf16[1024,128]{1,0:T(8,128)(2,1)S(1)}) custom-call(s32[4]{0:T(128)S(1)} %pad_add_fusion.1.table, bf16[1024,512]{1,0:T(8,128)(2,1)S(1)} %bitcast.35, bf16[1024,512]{1,0:T(8,128)(2,1)S(1)} %bitcast.40, bf16[1024,512]{1,0:T(8,128)(2,1)S(1)} %collective-permute-done.23.refs_2_, ...), custom_call_target="tpu_custom_call" | custom-call | flops 1073741824 | bytes 5242880 | tf_op jit(solution)/shard_map/pallas_call | solution.py:304
  143.0 4.1 %collective-permute-start.27 = (bf16[1024,128]{1,0:T(8,128)(2,1)S(1)}, bf16[1024,128]{1,0:T(8,128)(2,1)S(1)}, u32[]{:S(2)}, u32[]{:S(2)}) collective-permute-start(bf16[1024,128]{1,0:T(8,128)(2,1)S(1)} %get-tuple-element.116), channel_id=1, source_target_pairs={{0,20},{2,22},{4,16},{6,18},{8,28},{10,30},{12,24},{14,26},{16,4},... | collective-permute-start | bytes 786440 | tf_op jit(solution)/shard_map/ppermute | solution.py:331
  147.1 19.8 %collective-permute-start.29 = (bf16[1024,128]{1,0:T(8,128)(2,1)S(1)}, bf16[1024,128]{1,0:T(8,128)(2,1)S(1)}, u32[]{:S(2)}, u32[]{:S(2)}) collective-permute-start(bf16[1024,128]{1,0:T(8,128)(2,1)S(1)} %get-tuple-element.118), channel_id=1, source_target_pairs={{0,12},{2,14},{4,8},{6,10},{8,4},{10,6},{12,0},{14,2},{16,28},{18,... | collective-permute-start | bytes 786440 | tf_op jit(solution)/shard_map/ppermute | solution.py:331
  167.1 2.2 %shard_map.81.refs_2_ = f32[128,64,128]{2,1,0:T(8,128)} custom-call(s32[2]{0:T(128)S(1)} %pad_add_fusion.4.table, bf16[1024,128]{1,0:T(8,128)(2,1)S(1)} %get-tuple-element.121.refs_0_, bf16[1024,128]{1,0:T(8,128)(2,1)S(1)} %collective-permute-done.25.refs_1_), custom_call_target="tpu_custom_call" | custom-call | flops 262144 | bytes 1572864 | tf_op jit(solution)/shard_map/pallas_call | solution.py:91
  169.3 2.2 %shard_map.82.refs_2_ = f32[128,64,128]{2,1,0:T(8,128)} custom-call(s32[2]{0:T(128)S(1)} %pad_add_fusion.3.table, bf16[1024,128]{1,0:T(8,128)(2,1)S(1)} %collective-permute-done.30.refs_0_, bf16[1024,128]{1,0:T(8,128)(2,1)S(1)} %collective-permute-done.31.refs_1_, f32[128,64,128]{2,1,0:T(8,128)} %shard_map.81.refs_2_), custom_call_target="tpu_custom_call", output_to_operand_aliasing={{}: (3, {})} | custom-call | flops 262144 | bytes 1572864 | tf_op jit(solution)/shard_map/pallas_call | solution.py:91
  171.5 3.2 %collective-permute-done.29.refs_1_ = bf16[1024,128]{1,0:T(8,128)(2,1)S(1)} collective-permute-done((bf16[1024,128]{1,0:T(8,128)(2,1)S(1)}, bf16[1024,128]{1,0:T(8,128)(2,1)S(1)}, u32[]{:S(2)}, u32[]{:S(2)}) %collective-permute-start.29) | collective-permute-done | bytes 262176 | tf_op jit(solution)/shard_map/ppermute | solution.py:331
  174.7 2.2 %shard_map.83.refs_2_ = f32[128,64,128]{2,1,0:T(8,128)} custom-call(s32[2]{0:T(128)S(1)} %get-tuple-element.137.table, bf16[1024,128]{1,0:T(8,128)(2,1)S(1)} %collective-permute-done.28.refs_0_, bf16[1024,128]{1,0:T(8,128)(2,1)S(1)} %collective-permute-done.29.refs_1_, f32[128,64,128]{2,1,0:T(8,128)} %shard_map.82.refs_2_), custom_call_target="tpu_custom_call", output_to_operand_aliasing={{}: (3, {})} | custom-call | flops 262144 | bytes 1572864 | tf_op jit(solution)/shard_map/pallas_call | solution.py:91
  176.9 3.0 %collective-permute-done.26.refs_0_ = bf16[1024,128]{1,0:T(8,128)(2,1)S(1)} collective-permute-done((bf16[1024,128]{1,0:T(8,128)(2,1)S(1)}, bf16[1024,128]{1,0:T(8,128)(2,1)S(1)}, u32[]{:S(2)}, u32[]{:S(2)}) %collective-permute-start.26) | collective-permute-done | bytes 262176 | tf_op jit(solution)/shard_map/ppermute | solution.py:331
  179.9 2.9 %collective-permute-done.27.refs_1_ = bf16[1024,128]{1,0:T(8,128)(2,1)S(1)} collective-permute-done((bf16[1024,128]{1,0:T(8,128)(2,1)S(1)}, bf16[1024,128]{1,0:T(8,128)(2,1)S(1)}, u32[]{:S(2)}, u32[]{:S(2)}) %collective-permute-start.27) | collective-permute-done | bytes 262176 | tf_op jit(solution)/shard_map/ppermute | solution.py:331
  182.9 2.2 %shard_map.84 = f32[128,64,128]{2,1,0:T(8,128)} custom-call(s32[2]{0:T(128)S(1)} %get-tuple-element.136.table, bf16[1024,128]{1,0:T(8,128)(2,1)S(1)} %collective-permute-done.26.refs_0_, bf16[1024,128]{1,0:T(8,128)(2,1)S(1)} %collective-permute-done.27.refs_1_, f32[128,64,128]{2,1,0:T(8,128)} %shard_map.83.refs_2_), custom_call_target="tpu_custom_call", output_to_operand_aliasing={{}: (3, {})} | custom-call | flops 262144 | bytes 1572864 | tf_op jit(solution)/shard_map/pallas_call | solution.py:91
  (61 shorter events, 2.2 us)
Async XLA Ops:
  1.0 22.4 %collective-permute-start = (bf16[64,2048]{1,0:T(8,128)(2,1)S(1)}, bf16[64,2048]{1,0:T(8,128)(2,1)S(1)}, u32[]{:S(2)}, u32[]{:S(2)}) collective-permute-start(bf16[64,2048]{1,0:T(8,128)(2,1)S(1)} %constant_dynamic-slice_fusion), channel_id=1, source_target_pairs={{0,8},{2,10},{4,12},{6,14},{8,0},{10,2},{12,4},{14,6},{16,24},{18,... | collective-permute-start | bytes 786440 | tf_op jit(solution)/shard_map/ppermute | solution.py:331
  4.1 21.4 %collective-permute-start.1 = (bf16[64,2048]{1,0:T(8,128)(2,1)S(1)}, bf16[64,2048]{1,0:T(8,128)(2,1)S(1)}, u32[]{:S(2)}, u32[]{:S(2)}) collective-permute-start(bf16[64,2048]{1,0:T(8,128)(2,1)S(1)} %constant_dynamic-slice_fusion), channel_id=1, source_target_pairs={{0,16},{2,18},{4,20},{6,22},{8,24},{10,26},{12,28},{14,30},{16,0},... | collective-permute-start | bytes 786440 | tf_op jit(solution)/shard_map/ppermute | solution.py:331
  6.6 18.8 %collective-permute-start.2 = (bf16[64,2048]{1,0:T(8,128)(2,1)S(1)}, bf16[64,2048]{1,0:T(8,128)(2,1)S(1)}, u32[]{:S(2)}, u32[]{:S(2)}) collective-permute-start(bf16[64,2048]{1,0:T(8,128)(2,1)S(1)} %constant_dynamic-slice_fusion), channel_id=1, source_target_pairs={{0,24},{2,26},{4,28},{6,30},{8,16},{10,18},{12,20},{14,22},{16,8},... | collective-permute-start | bytes 786440 | tf_op jit(solution)/shard_map/ppermute | solution.py:331
  6.7 18.8 %collective-permute-start.3 = (bf16[64,2048]{1,0:T(8,128)(2,1)S(1)}, bf16[64,2048]{1,0:T(8,128)(2,1)S(1)}, u32[]{:S(2)}, u32[]{:S(2)}) collective-permute-start(bf16[64,2048]{1,0:T(8,128)(2,1)S(1)} %constant_dynamic-slice_fusion), channel_id=1, source_target_pairs={{0,4},{2,6},{4,0},{6,2},{8,12},{10,14},{12,8},{14,10},{16,20},{18,... | collective-permute-start | bytes 786440 | tf_op jit(solution)/shard_map/ppermute | solution.py:331
  8.4 1.8 collective-permute-start.4
  10.2 3.6 %collective-permute-start.5 = (f32[3,128]{1,0:T(4,128)S(1)}, f32[3,128]{1,0:T(4,128)S(1)}, u32[]{:S(2)}, u32[]{:S(2)}) collective-permute-start(f32[3,128]{1,0:T(4,128)S(1)} %get-tuple-element.128), channel_id=1, source_target_pairs={{0,1},{1,0},{2,3},{3,2},{4,5},{5,4},{6,7},{7,6},{8,9},{9,8},{10,11... | collective-permute-start | bytes 4616 | tf_op jit(solution)/shard_map/ppermute | solution.py:366
  13.9 3.6 %collective-permute-start.6 = (f32[3,128]{1,0:T(4,128)S(1)}, f32[3,128]{1,0:T(4,128)S(1)}, u32[]{:S(2)}, u32[]{:S(2)}) collective-permute-start(f32[3,128]{1,0:T(4,128)S(1)} %get-tuple-element.127), channel_id=1, source_target_pairs={{1,0},{0,1},{3,2},{2,3},{5,4},{4,5},{7,6},{6,7},{9,8},{8,9},{11,10... | collective-permute-start | bytes 4616 | tf_op jit(solution)/shard_map/ppermute | solution.py:367
  15.4 10.0 %copy-start.3 = (bf16[128,2048]{1,0:T(8,128)(2,1)S(1)}, bf16[128,2048]{1,0:T(8,128)(2,1)}, u32[]{:S(2)}) copy-start(bf16[128,2048]{1,0:T(8,128)(2,1)} %refs_0_.1) | copy-start | bytes 1572868
  23.4 3.3 %copy-start.4 = (bf16[1040,128]{1,0:T(8,128)(2,1)}, bf16[1040,128]{1,0:T(8,128)(2,1)S(1)}, u32[]{:S(2)}) copy-start(bf16[1040,128]{1,0:T(8,128)(2,1)S(1)} %get-tuple-element.91) | copy-start | bytes 798724
  23.4 3.3 %copy-start.5 = (bf16[1040,128]{1,0:T(8,128)(2,1)}, bf16[1040,128]{1,0:T(8,128)(2,1)S(1)}, u32[]{:S(2)}) copy-start(bf16[1040,128]{1,0:T(8,128)(2,1)S(1)} %get-tuple-element.90) | copy-start | bytes 798724
  26.7 23.7 %collective-permute-start.9 = (bf16[1040,128]{1,0:T(8,128)(2,1)S(1)}, bf16[1040,128]{1,0:T(8,128)(2,1)S(1)}, u32[]{:S(2)}, u32[]{:S(2)}) collective-permute-start(bf16[1040,128]{1,0:T(8,128)(2,1)S(1)} %get-tuple-element.78), channel_id=1, source_target_pairs={{0,16},{2,18},{4,20},{6,22},{8,24},{10,26},{12,28},{14,30},{16,0},... | collective-permute-start | bytes 798728 | tf_op jit(solution)/shard_map/ppermute | solution.py:331
  32.5 17.9 %collective-permute-start.10 = (bf16[1040,128]{1,0:T(8,128)(2,1)S(1)}, bf16[1040,128]{1,0:T(8,128)(2,1)S(1)}, u32[]{:S(2)}, u32[]{:S(2)}) collective-permute-start(bf16[1040,128]{1,0:T(8,128)(2,1)S(1)} %get-tuple-element.79), channel_id=1, source_target_pairs={{0,24},{2,26},{4,28},{6,30},{8,16},{10,18},{12,20},{14,22},{16,8},... | collective-permute-start | bytes 798728 | tf_op jit(solution)/shard_map/ppermute | solution.py:331
  33.9 17.6 %collective-permute-start.7 = (bf16[192,2048]{1,0:T(8,128)(2,1)S(1)}, bf16[192,2048]{1,0:T(8,128)(2,1)S(1)}, u32[]{:S(2)}, u32[]{:S(2)}) collective-permute-start(bf16[192,2048]{1,0:T(8,128)(2,1)S(1)} %pad_maximum_fusion.1), channel_id=1, source_target_pairs={{0,4},{2,6},{4,0},{6,2},{8,12},{10,14},{12,8},{14,10},{16,20},{18,... | collective-permute-start | bytes 2359304 | tf_op jit(solution)/shard_map/ppermute | solution.py:331
  35.5 23.0 %collective-permute-start.8 = (bf16[256,2048]{1,0:T(8,128)(2,1)S(1)}, bf16[256,2048]{1,0:T(8,128)(2,1)S(1)}, u32[]{:S(2)}, u32[]{:S(2)}) collective-permute-start(bf16[256,2048]{1,0:T(8,128)(2,1)S(1)} %pad_maximum_fusion), channel_id=1, source_target_pairs={{0,1},{1,0},{2,3},{3,2},{4,5},{5,4},{6,7},{7,6},{8,9},{9,8},{10,11... | collective-permute-start | bytes 3145736 | tf_op jit(solution)/shard_map/ppermute | solution.py:333
  51.5 7.0 %copy-start.1 = (bf16[192,2048]{1,0:T(8,128)(2,1)}, bf16[192,2048]{1,0:T(8,128)(2,1)S(1)}, u32[]{:S(2)}) copy-start(bf16[192,2048]{1,0:T(8,128)(2,1)S(1)} %collective-permute-done.7.refs_0_) | copy-start | bytes 2359300
  58.5 18.4 %collective-permute-start.14 = (bf16[1040,128]{1,0:T(8,128)(2,1)}, bf16[1040,128]{1,0:T(8,128)(2,1)}, u32[]{:S(2)}, u32[]{:S(2)}) collective-permute-start(bf16[1040,128]{1,0:T(8,128)(2,1)} %get-tuple-element.93), channel_id=1, source_target_pairs={{0,20},{2,22},{4,16},{6,18},{8,28},{10,30},{12,24},{14,26},{16,4},... | collective-permute-start | bytes 798728 | tf_op jit(solution)/shard_map/ppermute | solution.py:331
  58.5 18.4 %collective-permute-start.15 = (bf16[1040,128]{1,0:T(8,128)(2,1)}, bf16[1040,128]{1,0:T(8,128)(2,1)}, u32[]{:S(2)}, u32[]{:S(2)}) collective-permute-start(bf16[1040,128]{1,0:T(8,128)(2,1)} %get-tuple-element.94), channel_id=1, source_target_pairs={{0,28},{2,30},{4,24},{6,26},{8,20},{10,22},{12,16},{14,18},{16,12}... | collective-permute-start | bytes 798728 | tf_op jit(solution)/shard_map/ppermute | solution.py:331
  61.4 16.8 %collective-permute-start.11 = (bf16[1040,128]{1,0:T(8,128)(2,1)}, bf16[1040,128]{1,0:T(8,128)(2,1)S(1)}, u32[]{:S(2)}, u32[]{:S(2)}) collective-permute-start(bf16[1040,128]{1,0:T(8,128)(2,1)} %copy-done.5), channel_id=1, source_target_pairs={{0,4},{2,6},{4,0},{6,2},{8,12},{10,14},{12,8},{14,10},{16,20},{18,... | collective-permute-start | bytes 798728 | tf_op jit(solution)/shard_map/ppermute | solution.py:331
  62.5 16.3 %collective-permute-start.12 = (bf16[1040,128]{1,0:T(8,128)(2,1)}, bf16[1040,128]{1,0:T(8,128)(2,1)S(1)}, u32[]{:S(2)}, u32[]{:S(2)}) collective-permute-start(bf16[1040,128]{1,0:T(8,128)(2,1)} %copy-done.4), channel_id=1, source_target_pairs={{0,8},{2,10},{4,12},{6,14},{8,0},{10,2},{12,4},{14,6},{16,24},{18,... | collective-permute-start | bytes 798728 | tf_op jit(solution)/shard_map/ppermute | solution.py:331
  63.4 22.9 %collective-permute-start.16 = (bf16[192,2048]{1,0:T(8,128)(2,1)}, bf16[192,2048]{1,0:T(8,128)(2,1)S(1)}, u32[]{:S(2)}, u32[]{:S(2)}) collective-permute-start(bf16[192,2048]{1,0:T(8,128)(2,1)} %copy-done.1), channel_id=1, source_target_pairs={{0,1},{1,0},{2,3},{3,2},{4,5},{5,4},{6,7},{7,6},{8,9},{9,8},{10,11... | collective-permute-start | bytes 2359304 | tf_op jit(solution)/shard_map/ppermute | solution.py:333
  64.9 1.2 copy-start.2
  76.9 9.1 %collective-permute-start.13 = (bf16[1040,128]{1,0:T(8,128)(2,1)S(1)}, bf16[1040,128]{1,0:T(8,128)(2,1)S(1)}, u32[]{:S(2)}, u32[]{:S(2)}) collective-permute-start(bf16[1040,128]{1,0:T(8,128)(2,1)S(1)} %get-tuple-element.92), channel_id=1, source_target_pairs={{0,12},{2,14},{4,8},{6,10},{8,4},{10,6},{12,0},{14,2},{16,28},{18,... | collective-permute-start | bytes 798728 | tf_op jit(solution)/shard_map/ppermute | solution.py:331
  90.8 4.5 %collective-permute-start.17 = (f32[1024,512]{1,0:T(8,128)}, f32[1024,512]{1,0:T(8,128)}, u32[]{:S(2)}, u32[]{:S(2)}) collective-permute-start(f32[1024,512]{1,0:T(8,128)} %shard_map.71), channel_id=1, source_target_pairs={{0,2},{2,0},{4,6},{6,4},{8,10},{10,8},{12,14},{14,12},{16,18},{18,... | collective-permute-start | bytes 6291464 | tf_op jit(solution)/shard_map/ppermute | solution.py:332
  94.3 6.0 %collective-permute-start.20 = (f32[1024,512]{1,0:T(8,128)}, f32[1024,512]{1,0:T(8,128)}, u32[]{:S(2)}, u32[]{:S(2)}) collective-permute-start(f32[1024,512]{1,0:T(8,128)} %shard_map.72), channel_id=1, source_target_pairs={{0,2},{2,0},{4,6},{6,4},{8,10},{10,8},{12,14},{14,12},{16,18},{18,... | collective-permute-start | bytes 6291464 | tf_op jit(solution)/shard_map/ppermute | solution.py:332
  98.3 12.0 %collective-permute-start.18 = (bf16[3,128,512]{2,1,0:T(8,128)(2,1)S(1)}, bf16[3,128,512]{2,1,0:T(8,128)(2,1)S(1)}, u32[]{:S(2)}, u32[]{:S(2)}) collective-permute-start(bf16[3,128,512]{2,1,0:T(8,128)(2,1)S(1)} %bitcast.45), channel_id=1, source_target_pairs={{0,4},{2,6},{4,12},{6,14},{12,8},{14,10},{8,16},{10,18},{16,20},{1... | collective-permute-start | bytes 1179656 | tf_op jit(solution)/shard_map/ppermute | solution.py:433
  99.0 12.9 %collective-permute-start.19 = (bf16[3,128,512]{2,1,0:T(8,128)(2,1)S(1)}, bf16[3,128,512]{2,1,0:T(8,128)(2,1)S(1)}, u32[]{:S(2)}, u32[]{:S(2)}) collective-permute-start(bf16[3,128,512]{2,1,0:T(8,128)(2,1)S(1)} %bitcast.43), channel_id=1, source_target_pairs={{4,0},{6,2},{12,4},{14,6},{8,12},{10,14},{16,8},{18,10},{20,16},{2... | collective-permute-start | bytes 1179656 | tf_op jit(solution)/shard_map/ppermute | solution.py:434
  103.3 14.6 %collective-permute-start.21 = (bf16[3,128,512]{2,1,0:T(8,128)(2,1)S(1)}, bf16[3,128,512]{2,1,0:T(8,128)(2,1)S(1)}, u32[]{:S(2)}, u32[]{:S(2)}) collective-permute-start(bf16[3,128,512]{2,1,0:T(8,128)(2,1)S(1)} %bitcast.46), channel_id=1, source_target_pairs={{0,4},{2,6},{4,12},{6,14},{12,8},{14,10},{8,16},{10,18},{16,20},{1... | collective-permute-start | bytes 1179656 | tf_op jit(solution)/shard_map/ppermute | solution.py:433
  105.0 14.5 %collective-permute-start.22 = (bf16[3,128,512]{2,1,0:T(8,128)(2,1)S(1)}, bf16[3,128,512]{2,1,0:T(8,128)(2,1)S(1)}, u32[]{:S(2)}, u32[]{:S(2)}) collective-permute-start(bf16[3,128,512]{2,1,0:T(8,128)(2,1)S(1)} %bitcast.44), channel_id=1, source_target_pairs={{4,0},{6,2},{12,4},{14,6},{8,12},{10,14},{16,8},{18,10},{20,16},{2... | collective-permute-start | bytes 1179656 | tf_op jit(solution)/shard_map/ppermute | solution.py:434
  112.2 15.5 %copy-start = (bf16[1024,2048]{1,0:T(8,128)(2,1)S(1)}, bf16[1024,2048]{1,0:T(8,128)(2,1)}, u32[]{:S(2)}) copy-start(bf16[1024,2048]{1,0:T(8,128)(2,1)} %shard_map.70.b_ref.refs_4_) | copy-start | bytes 12582916
  117.7 7.5 %collective-permute-start.23 = (bf16[1024,512]{1,0:T(8,128)(2,1)S(1)}, bf16[1024,512]{1,0:T(8,128)(2,1)S(1)}, u32[]{:S(2)}, u32[]{:S(2)}) collective-permute-start(bf16[1024,512]{1,0:T(8,128)(2,1)S(1)} %bitcast.31), channel_id=1, source_target_pairs={{0,2},{2,0},{4,6},{6,4},{8,10},{10,8},{12,14},{14,12},{16,18},{18,... | collective-permute-start | bytes 3145736 | tf_op jit(solution)/shard_map/ppermute | solution.py:332
  125.0 2.7 %collective-permute-start.24 = (bf16[1024,512]{1,0:T(8,128)(2,1)S(1)}, bf16[1024,512]{1,0:T(8,128)(2,1)S(1)}, u32[]{:S(2)}, u32[]{:S(2)}) collective-permute-start(bf16[1024,512]{1,0:T(8,128)(2,1)S(1)} %bitcast.36), channel_id=1, source_target_pairs={{0,2},{2,0},{4,6},{6,4},{8,10},{10,8},{12,14},{14,12},{16,18},{18,... | collective-permute-start | bytes 3145736 | tf_op jit(solution)/shard_map/ppermute | solution.py:332
  130.1 12.7 %collective-permute-start.25 = (bf16[1024,128]{1,0:T(8,128)(2,1)S(1)}, bf16[1024,128]{1,0:T(8,128)(2,1)S(1)}, u32[]{:S(2)}, u32[]{:S(2)}) collective-permute-start(bf16[1024,128]{1,0:T(8,128)(2,1)S(1)} %get-tuple-element.110), channel_id=1, source_target_pairs={{0,4},{2,6},{4,0},{6,2},{8,12},{10,14},{12,8},{14,10},{16,20},{18,... | collective-permute-start | bytes 786440 | tf_op jit(solution)/shard_map/ppermute | solution.py:331
  134.4 12.7 %collective-permute-start.30 = (bf16[1024,128]{1,0:T(8,128)(2,1)S(1)}, bf16[1024,128]{1,0:T(8,128)(2,1)S(1)}, u32[]{:S(2)}, u32[]{:S(2)}) collective-permute-start(bf16[1024,128]{1,0:T(8,128)(2,1)S(1)} %get-tuple-element.119), channel_id=1, source_target_pairs={{0,24},{2,26},{4,28},{6,30},{8,16},{10,18},{12,20},{14,22},{16,8},... | collective-permute-start | bytes 786440 | tf_op jit(solution)/shard_map/ppermute | solution.py:331
  134.5 34.8 %collective-permute-start.31 = (bf16[1024,128]{1,0:T(8,128)(2,1)S(1)}, bf16[1024,128]{1,0:T(8,128)(2,1)S(1)}, u32[]{:S(2)}, u32[]{:S(2)}) collective-permute-start(bf16[1024,128]{1,0:T(8,128)(2,1)S(1)} %get-tuple-element.120), channel_id=1, source_target_pairs={{0,28},{2,30},{4,24},{6,26},{8,20},{10,22},{12,16},{14,18},{16,12}... | collective-permute-start | bytes 786440 | tf_op jit(solution)/shard_map/ppermute | solution.py:331
  142.9 37.0 %collective-permute-start.26 = (bf16[1024,128]{1,0:T(8,128)(2,1)S(1)}, bf16[1024,128]{1,0:T(8,128)(2,1)S(1)}, u32[]{:S(2)}, u32[]{:S(2)}) collective-permute-start(bf16[1024,128]{1,0:T(8,128)(2,1)S(1)} %get-tuple-element.115), channel_id=1, source_target_pairs={{0,16},{2,18},{4,20},{6,22},{8,24},{10,26},{12,28},{14,30},{16,0},... | collective-permute-start | bytes 786440 | tf_op jit(solution)/shard_map/ppermute | solution.py:331
  143.0 39.9 %collective-permute-start.27 = (bf16[1024,128]{1,0:T(8,128)(2,1)S(1)}, bf16[1024,128]{1,0:T(8,128)(2,1)S(1)}, u32[]{:S(2)}, u32[]{:S(2)}) collective-permute-start(bf16[1024,128]{1,0:T(8,128)(2,1)S(1)} %get-tuple-element.116), channel_id=1, source_target_pairs={{0,20},{2,22},{4,16},{6,18},{8,28},{10,30},{12,24},{14,26},{16,4},... | collective-permute-start | bytes 786440 | tf_op jit(solution)/shard_map/ppermute | solution.py:331
  147.1 24.4 %collective-permute-start.28 = (bf16[1024,128]{1,0:T(8,128)(2,1)S(1)}, bf16[1024,128]{1,0:T(8,128)(2,1)S(1)}, u32[]{:S(2)}, u32[]{:S(2)}) collective-permute-start(bf16[1024,128]{1,0:T(8,128)(2,1)S(1)} %get-tuple-element.117), channel_id=1, source_target_pairs={{0,8},{2,10},{4,12},{6,14},{8,0},{10,2},{12,4},{14,6},{16,24},{18,... | collective-permute-start | bytes 786440 | tf_op jit(solution)/shard_map/ppermute | solution.py:331
  147.1 27.6 %collective-permute-start.29 = (bf16[1024,128]{1,0:T(8,128)(2,1)S(1)}, bf16[1024,128]{1,0:T(8,128)(2,1)S(1)}, u32[]{:S(2)}, u32[]{:S(2)}) collective-permute-start(bf16[1024,128]{1,0:T(8,128)(2,1)S(1)} %get-tuple-element.118), channel_id=1, source_target_pairs={{0,12},{2,14},{4,8},{6,10},{8,4},{10,6},{12,0},{14,2},{16,28},{18,... | collective-permute-start | bytes 786440 | tf_op jit(solution)/shard_map/ppermute | solution.py:331

commit v3 on v2

--- a/solution.py
+++ b/solution.py
@@ -222,34 +222,22 @@
         keep.append(1.0 - omega)
         gain.append(omega / diag)
 
-    def load(ref, first):
-        def body(r, _):
+    for ref, first in ((up_ref, 0), (own_ref, HALO), (down_ref, HALO + rows)):
+        for r in range(ref.shape[0]):
             s = ref[r].astype(F32)
             rhs[first + r] = s
             ua[first + r] = fluid_ref[first + r] * (gain[0] * s)
-            return 0
-
-        lax.fori_loop(0, ref.shape[0], body, 0)
-
-    load(up_ref, 0)
-    load(own_ref, HALO)
-    load(down_ref, HALO + rows)
     src, dst = ua, ub
     for step in range(1, SWEEPS):
-        last = step == SWEEPS - 1
-
-        def body(r, _, src=src, dst=dst, step=step, last=last):
+        for r in range(step, ext - step):
             c = src[r]
             wide = c.shape[0]
             beside = src[r - 1] + src[r + 1] + (pltpu.roll(c, 1, 0) + pltpu.roll(c, wide - 1, 0))
             new = fluid_ref[r] * (keep[step] * c + gain[step] * (rhs[r] + beside))
-            if last:
+            if step == SWEEPS - 1:
                 o_ref[r - HALO] = new.astype(BF16)
             else:
                 dst[r] = new
-            return 0
-
-        lax.fori_loop(step, ext - step, body, 0)
         src, dst = dst, src
 
 
@@ -380,25 +368,27 @@
 
     own = lax.dynamic_slice_in_dim(basis, odd * half, half, 0)
     column = [chip_swap(own, s) for s in ids]
-    beside = chip_swap(own, 1)
-    layout = (("whole", (0,)), *[("mine", (s,)) for s in ids], ("mine", (1,)))
+    beside = chip_swap(basis, 1)
+    layout = (("whole", (0,)), *[("mine", (s,)) for s in ids], ("whole", (1,)))
     full = join(i32(odd), [basis, *column, beside], layout, planes, chips, None, LATE)
     column, beside, full, send = lax.optimization_barrier((column, beside, full, send))
 
     held = jnp.concatenate(column)
-    over_y, over_x = chip_swap(held, 1), tile_swap(jnp.concatenate([held, beside]))
-    evens = list(range(far, chips, 2))
+    over_y, over_x = chip_swap(held, 1), tile_swap(held)
+    evens = list(range(far, far + far // 2))
     x = gather([send[0], *[chip_swap(send[s], s) for s in evens]], [0, *evens], cells, chips, None, LATE)
     over_y, over_x, x, send = lax.optimization_barrier((over_y, over_x, x, send))
 
-    corner = tile_swap(over_y)
-    full = join(i32(odd), [over_y, over_x], (("mine", odds[1:]), ("other", (*ids, 1))), planes, chips, full, small)
-    last = list(range(far + 1, chips, 2))
-    x = gather([chip_swap(send[s], s) for s in last], last, cells, chips, x, LATE)
-    nearby = list(range(1, far))
+    cut = (2 * len(ids) + 2) // 3
+    corner_x, corner_y = tile_swap(over_y[: cut * half]), chip_swap(over_x[cut * half :], 1)
+    full = join(i32(odd), [over_y, over_x], (("mine", odds[1:]), ("other", ids)), planes, chips, full, small)
+    last, nearby = list(range(far + far // 2, chips)), list(range(1, far))
+    final = [chip_swap(send[s], s) for s in last]
     x = gather([chip_swap(send[s], s) for s in nearby], nearby, cells, chips, x, small)
-    full, x, corner = lax.optimization_barrier((full, x, corner))
-    full = join(i32(odd), [corner], (("other", odds[1:]),), planes, chips, full, small)
+    corner_x, corner_y, x = lax.optimization_barrier((corner_x, corner_y, x))
+    x = gather(final, last, cells, chips, x, LATE)
+    layout = (("other", odds[1 : cut + 1]), ("other", odds[cut + 1 :]))
+    full = join(i32(odd), [corner_x, corner_y], layout, planes, chips, full, small)
     x, tails = x
 
     ring = jnp.concatenate([edges[0], inside, edges[1]])
@@ -445,19 +435,20 @@
     )
     home = [None] * chips
     pairs = list(range(chips // 2))
-    for i in [0, *reversed(pairs[1:])]:
+    for i in reversed(pairs):
         home[2 * i], home[2 * i + 1] = inverse(columns, solved + others, full, i, planes)
-    first = [1, *[s for i in reversed(pairs[chips // 4 + 1 :]) for s in (2 * i + 1, 2 * i)]]
-    second = [s for i in reversed(pairs[1 : chips // 4 + 1]) for s in (2 * i + 1, 2 * i)]
+    first = [s for i in reversed(pairs[chips // 4 + 1 :]) for s in (2 * i + 1, 2 * i)]
+    second = [s for i in reversed(pairs[: chips // 4 + 1]) for s in (2 * i + 1, 2 * i) if s]
     held = [home[s] for s in second]
+    sign = core_swap(home[first[0]][:16])
     for s in first:
         home[s] = chip_swap(home[s], s)
-    home[1], held = lax.optimization_barrier((home[1], held))
+    sign, held = lax.optimization_barrier((sign, held))
     for s, v in zip(second, held):
         home[s] = chip_swap(v, s)
 
     out = None
-    for i in [0, *pairs[chips // 4 + 1 :], *pairs[1 : chips // 4 + 1]]:
+    for i in [*pairs[chips // 4 + 1 :], *pairs[: chips // 4 + 1]]:
         out = place_pair(tables[i], home[2 * i], home[2 * i + 1], out, divergence.shape, rows)
     return out
 

time: 185 us -> 184 us (level); the launches traced: 185 us -> 180 us
  waiting for transfers between devices: 64.3 us -> 56.1 us
  local copies, waits for them, and re-layouts: 2.85 us -> 5.2 us
    ppermute x2, waiting for transfers between devices: 6.99 us -> 0.01 us  [local(): lax.ppermute(v, 'tile', [(i, i ^ 1) for i in range(tiles)])]
    ppermute x19 -> x20, waiting for transfers between devices: 42.8 us -> 40.3 us  [local(): chip_swap = lambda v, s: lax.ppermute(v, 'wn', flip(s))]
    ppermute x2, waiting for transfers between devices: 3.3 us -> 5.56 us  [local(): down = lax.ppermute(spectral[:HALO], ('wn', 'tile'), backward)]
    pallas_call x2, Pallas kernels: 10.9 us -> 9.01 us  [sweep(): pl.pallas_call(sweep_body, grid=(modes // lanes,), in_specs=[pl.BlockSpec...]
    ppermute x19 -> x20, starting transfers between devices: 50.5 us -> 50.8 us  [local(): chip_swap = lambda v, s: lax.ppermute(v, 'wn', flip(s))]
  transfers between devices with their start and end apart: 32 -> 33, of which waited for: 18 -> 18; matrix products, arithmetic and copies ran while one was open for 2% -> 3% of each run, Pallas kernels for 23% -> 24%
where the time goes in v3:
time: 184 us; the launch traced here: 180 us
  starting transfers between devices  62.5 us (34%)
  waiting for transfers between devices  56.1 us (30%)
  Pallas kernels  53.4 us (29%)
  local copies, waits for them, and re-layouts  5.2 us (3%)
  other arithmetic  2.79 us (2%)
    ppermute x20, starting transfers between devices, local(): chip_swap = lambda v, s: lax.ppermute(v, 'wn', flip(s))  50.8 us
    ppermute x20, waiting for transfers between devices, local(): chip_swap = lambda v, s: lax.ppermute(v, 'wn', flip(s))  40.3 us
    pallas_call x4, Pallas kernels, forward(): pl.pallas_call(forward_body, grid_spec=pltpu.PrefetchScalarGridSpec(num_s...  13 us
    pallas_call x4, Pallas kernels, inverse(): pl.pallas_call(functools.partial(inverse_body, min(cells, 256)), grid=(1,...  9.73 us
    pallas_call x2, Pallas kernels, sweep(): pl.pallas_call(sweep_body, grid=(modes // lanes,), in_specs=[pl.BlockSpec...  9.01 us
    pallas_call x4, Pallas kernels, place_pair(): pl.pallas_call(place_body, grid_spec=pltpu.PrefetchScalarGridSpec(num_sca...  8.64 us
    pallas_call x1, Pallas kernels, scale(): pl.pallas_call(scale_body, grid_spec=pltpu.PrefetchScalarGridSpec(num_sca...  6.01 us
    ppermute x2, waiting for transfers between devices, local(): down = lax.ppermute(spectral[:HALO], ('wn', 'tile'), backward)  5.56 us
  transfers between devices with their start and end apart: 33, of which 18 were waited for; matrix products, arithmetic and copies ran while one was open for 3% of the time, Pallas kernels for 24%

profile of v3, /device:TPU:0, one launch (start us, length us, event | category | flops | bytes accessed | tf_op | source)
XLA Modules:
  0.0 180.3 jit_solution(690904173809796965)
XLA Ops:
  0.0 1.0 constant_dynamic-slice_fusion
  1.0 3.1 %collective-permute-start = (bf16[64,2048]{1,0:T(8,128)(2,1)S(1)}, bf16[64,2048]{1,0:T(8,128)(2,1)S(1)}, u32[]{:S(2)}, u32[]{:S(2)}) collective-permute-start(bf16[64,2048]{1,0:T(8,128)(2,1)S(1)} %constant_dynamic-slice_fusion), channel_id=1, source_target_pairs={{0,8},{2,10},{4,12},{6,14},{8,0},{10,2},{12,4},{14,6},{16,24},{18,... | collective-permute-start | bytes 786440 | tf_op jit(solution)/shard_map/ppermute | solution.py:319
  4.1 2.6 %collective-permute-start.1 = (bf16[64,2048]{1,0:T(8,128)(2,1)S(1)}, bf16[64,2048]{1,0:T(8,128)(2,1)S(1)}, u32[]{:S(2)}, u32[]{:S(2)}) collective-permute-start(bf16[64,2048]{1,0:T(8,128)(2,1)S(1)} %constant_dynamic-slice_fusion), channel_id=1, source_target_pairs={{0,16},{2,18},{4,20},{6,22},{8,24},{10,26},{12,28},{14,30},{16,0},... | collective-permute-start | bytes 786440 | tf_op jit(solution)/shard_map/ppermute | solution.py:319
  6.7 1.7 collective-permute-start.3
  8.5 0.8 select_reduce_fusion.1
  9.3 0.8 subtract_convert_fusion
  10.3 1.6 collective-permute-start.5
  11.8 0.7 fusion.3
  12.5 1.4 collective-permute-done.5
  13.9 1.5 collective-permute-start.6
  15.5 2.0 %collective-permute-done.6 = f32[3,128]{1,0:T(4,128)S(1)} collective-permute-done((f32[3,128]{1,0:T(4,128)S(1)}, f32[3,128]{1,0:T(4,128)S(1)}, u32[]{:S(2)}, u32[]{:S(2)}) %collective-permute-start.6) | collective-permute-done | bytes 1568 | tf_op jit(solution)/shard_map/ppermute | solution.py:355
  17.5 6.0 %shard_map.65 = (bf16[1040,128]{1,0:T(8,128)(2,1)S(1)}, bf16[1040,128]{1,0:T(8,128)(2,1)S(1)}, bf16[1040,128]{1,0:T(8,128)(2,1)S(1)}, bf16[1040,128]{1,0:T(8,128...) custom-call(s32[8]{0:T(128)S(1)} %stack.95.table, ...), custom_call_target="tpu_custom_call" | custom-call | flops 1048576 | bytes 6291456 | tf_op jit(solution)/shard_map/pallas_call | solution.py:53
  23.5 2.0 %collective-permute-done.1.refs_2_ = bf16[64,2048]{1,0:T(8,128)(2,1)S(1)} collective-permute-done((bf16[64,2048]{1,0:T(8,128)(2,1)S(1)}, bf16[64,2048]{1,0:T(8,128)(2,1)S(1)}, u32[]{:S(2)}, u32[]{:S(2)}) %collective-permute-start.1) | collective-permute-done | bytes 262176 | tf_op jit(solution)/shard_map/ppermute | solution.py:319
  25.5 1.3 shard_map.64.refs_2_
  26.8 5.8 %collective-permute-start.9 = (bf16[1040,128]{1,0:T(8,128)(2,1)S(1)}, bf16[1040,128]{1,0:T(8,128)(2,1)S(1)}, u32[]{:S(2)}, u32[]{:S(2)}) collective-permute-start(bf16[1040,128]{1,0:T(8,128)(2,1)S(1)} %get-tuple-element.76), channel_id=1, source_target_pairs={{0,16},{2,18},{4,20},{6,22},{8,24},{10,26},{12,28},{14,30},{16,0},... | collective-permute-start | bytes 798728 | tf_op jit(solution)/shard_map/ppermute | solution.py:319
  32.6 1.0 collective-permute-start.10
  34.3 1.5 collective-permute-start.8
  35.8 14.7 %collective-permute-done.9.refs_1_ = bf16[1040,128]{1,0:T(8,128)(2,1)S(1)} collective-permute-done((bf16[1040,128]{1,0:T(8,128)(2,1)S(1)}, bf16[1040,128]{1,0:T(8,128)(2,1)S(1)}, u32[]{:S(2)}, u32[]{:S(2)}) %collective-permute-start.9) | collective-permute-done | bytes 266272 | tf_op jit(solution)/shard_map/ppermute | solution.py:319
  50.5 5.5 %collective-permute-done.10.refs_2_ = bf16[1040,128]{1,0:T(8,128)(2,1)S(1)} collective-permute-done((bf16[1040,128]{1,0:T(8,128)(2,1)S(1)}, bf16[1040,128]{1,0:T(8,128)(2,1)S(1)}, u32[]{:S(2)}, u32[]{:S(2)}) %collective-permute-start.10) | collective-permute-done | bytes 266272 | tf_op jit(solution)/shard_map/ppermute | solution.py:319
  56.4 1.0 collective-permute-done.7.refs_0_
  57.9 1.6 collective-permute-start.16
  59.4 0.8 slice.54
  60.3 1.5 collective-permute-start.13
  61.8 1.4 collective-permute-start.17
  63.2 2.0 %collective-permute-start.11 = (bf16[1040,128]{1,0:T(8,128)(2,1)}, bf16[1040,128]{1,0:T(8,128)(2,1)}, u32[]{:S(2)}, u32[]{:S(2)}) collective-permute-start(bf16[1040,128]{1,0:T(8,128)(2,1)} %get-tuple-element.85), channel_id=1, source_target_pairs={{0,24},{2,26},{4,28},{6,30},{8,16},{10,18},{12,20},{14,22},{16,8},... | collective-permute-start | bytes 798728 | tf_op jit(solution)/shard_map/ppermute | solution.py:319
  65.4 1.6 collective-permute-start.12
  67.0 0.7 slice.55
  67.7 0.7 copy-done.5
  68.4 1.5 collective-permute-start.14
  69.9 1.1 copy-done.2
  71.0 1.2 shard_map.69.refs_2_
  72.2 1.0 collective-permute-done.17.refs_2_
  73.2 1.2 shard_map.67
  74.5 3.5 %collective-permute-done.14.refs_1_ = bf16[64,2048]{1,0:T(8,128)(2,1)} collective-permute-done((bf16[64,2048]{1,0:T(8,128)(2,1)}, bf16[64,2048]{1,0:T(8,128)(2,1)}, u32[]{:S(2)}, u32[]{:S(2)}) %collective-permute-start.14) | collective-permute-done | bytes 262176 | tf_op jit(solution)/shard_map/ppermute | solution.py:319
  78.0 1.9 %shard_map.70.b_ref.refs_4_ = bf16[1024,2048]{1,0:T(8,128)(2,1)} custom-call(s32[1]{0:T(128)} %bitcast.6.half_ref, bf16[128,2048]{1,0:T(8,128)(2,1)S(1)} %collective-permute-done.13.refs_0_, bf16[64,2048]{1,0:T(8,128)(2,1)} %collective-permute-done.14.refs_1_, bf16[1024,2048]{1,0:T(8,128)(2,1)} %shard_map.69.refs_2_), custom_call_target="tpu_custom_call", output_to_operand_aliasing={{}: (3, {})} | custom-call | bytes 1048576 | tf_op jit(solution)/shard_map/pallas_call | solution.py:171
  80.4 3.4 %collective-permute-done.12.refs_1_ = bf16[1040,128]{1,0:T(8,128)(2,1)} collective-permute-done((bf16[1040,128]{1,0:T(8,128)(2,1)}, bf16[1040,128]{1,0:T(8,128)(2,1)}, u32[]{:S(2)}, u32[]{:S(2)}) %collective-permute-start.12) | collective-permute-done | bytes 266272 | tf_op jit(solution)/shard_map/ppermute | solution.py:319
  83.8 1.2 shard_map.68
  85.1 3.6 %shard_map.71 = f32[1024,512]{1,0:T(8,128)} custom-call(s32[1]{0:T(128)} %bitcast.19.table, bf16[1024,1024]{1,0:T(8,128)(2,1)S(1)} %get-tuple-element.101.x_ref, bf16[1024,2048]{1,0:T(8,128)(2,1)} %shard_map.70.b_ref.refs_4_), custom_call_target="tpu_custom_call" | custom-call | flops 1073741824 | bytes 5242880 | tf_op jit(solution)/shard_map/pallas_call | solution.py:196
  88.6 3.6 %shard_map.72 = f32[1024,512]{1,0:T(8,128)} custom-call(s32[1]{0:T(128)} %bitcast.18.table, bf16[1024,1024]{1,0:T(8,128)(2,1)S(1)} %get-tuple-element.101.x_ref, bf16[1024,2048]{1,0:T(8,128)(2,1)} %shard_map.70.b_ref.refs_4_), custom_call_target="tpu_custom_call" | custom-call | flops 1073741824 | bytes 5242880 | tf_op jit(solution)/shard_map/pallas_call | solution.py:196
  93.1 2.9 %shard_map.73 = bf16[1024,512]{1,0:T(8,128)(2,1)S(1)} custom-call(s32[1]{0:T(128)} %bitcast.17.table, bf16[1024,1024]{1,0:T(8,128)(2,1)S(1)} %get-tuple-element.101.x_ref, bf16[1024,2048]{1,0:T(8,128)(2,1)} %shard_map.70.b_ref.refs_4_, f32[1024,512]{1,0:T(8,128)} %collective-permute-done.18.refs_0_), custom_call_target="tpu_custom_call" | custom-call | flops 1073741824 | bytes 5242880 | tf_op jit(solution)/shard_map/pallas_call | solution.py:196
  96.1 0.9 collective-permute-start.19
  97.1 1.1 collective-permute-start.20
  98.2 2.9 %shard_map.75 = bf16[1024,512]{1,0:T(8,128)(2,1)S(1)} custom-call(s32[1]{0:T(128)} %bitcast.24.table, bf16[1024,1024]{1,0:T(8,128)(2,1)S(1)} %get-tuple-element.101.x_ref, bf16[1024,2048]{1,0:T(8,128)(2,1)} %shard_map.70.b_ref.refs_4_, f32[1024,512]{1,0:T(8,128)} %collective-permute-done.21.refs_0_), custom_call_target="tpu_custom_call" | custom-call | flops 1073741824 | bytes 5242880 | tf_op jit(solution)/shard_map/pallas_call | solution.py:196
  101.2 2.9 %collective-permute-start.22 = (bf16[3,128,512]{2,1,0:T(8,128)(2,1)S(1)}, bf16[3,128,512]{2,1,0:T(8,128)(2,1)S(1)}, u32[]{:S(2)}, u32[]{:S(2)}) collective-permute-start(bf16[3,128,512]{2,1,0:T(8,128)(2,1)S(1)} %bitcast.46), channel_id=1, source_target_pairs={{0,4},{2,6},{4,12},{6,14},{12,8},{14,10},{8,16},{10,18},{16,20},{1... | collective-permute-start | bytes 1179656 | tf_op jit(solution)/shard_map/ppermute | solution.py:423
  104.2 3.9 %collective-permute-done.19.up_ref = bf16[3,128,512]{2,1,0:T(8,128)(2,1)S(1)} collective-permute-done((bf16[3,128,512]{2,1,0:T(8,128)(2,1)S(1)}, bf16[3,128,512]{2,1,0:T(8,128)(2,1)S(1)}, u32[]{:S(2)}, u32[]{:S(2)}) %collective-permute-start.19) | collective-permute-done | bytes 393248 | tf_op jit(solution)/shard_map/ppermute | solution.py:423
  108.1 2.8 %collective-permute-done.20.down_ref = bf16[3,128,512]{2,1,0:T(8,128)(2,1)S(1)} collective-permute-done((bf16[3,128,512]{2,1,0:T(8,128)(2,1)S(1)}, bf16[3,128,512]{2,1,0:T(8,128)(2,1)S(1)}, u32[]{:S(2)}, u32[]{:S(2)}) %collective-permute-start.20) | collective-permute-done | bytes 393248 | tf_op jit(solution)/shard_map/ppermute | solution.py:424
  111.3 4.5 %shard_map.74 = bf16[8,128,512]{2,1,0:T(8,128)(2,1)S(1)} custom-call(f32[1,512]{1,0:T(1,128)S(1)} %get-tuple-element.128.eigen_ref, f32[14,128,128]{2,1,0:T(8,128)S(1)} %broadcast_in_dim.44.fluid_ref, bf16[3,128,512]{2,1,0:T(8,128)(2,1)S(1)} %collective-permute-done.19.up_ref, bf16[8,128,512]{2,1,0:T(8,128)(2,1)S(1)} %bitcast.41, ...), custom_call_target="tpu_custom_call" | custom-call | flops 367001600 | bytes 3670016 | tf_op jit(solution)/shard_map/pallas_call | solution.py:248
  115.9 2.7 %collective-permute-done.23.down_ref = bf16[3,128,512]{2,1,0:T(8,128)(2,1)S(1)} collective-permute-done((bf16[3,128,512]{2,1,0:T(8,128)(2,1)S(1)}, bf16[3,128,512]{2,1,0:T(8,128)(2,1)S(1)}, u32[]{:S(2)}, u32[]{:S(2)}) %collective-permute-start.23) | collective-permute-done | bytes 393248 | tf_op jit(solution)/shard_map/ppermute | solution.py:424
  118.6 4.5 %shard_map.76 = bf16[8,128,512]{2,1,0:T(8,128)(2,1)S(1)} custom-call(f32[1,512]{1,0:T(1,128)S(1)} %get-tuple-element.127.eigen_ref, f32[14,128,128]{2,1,0:T(8,128)S(1)} %broadcast_in_dim.44.fluid_ref, bf16[3,128,512]{2,1,0:T(8,128)(2,1)S(1)} %collective-permute-done.22.up_ref, bf16[8,128,512]{2,1,0:T(8,128)(2,1)S(1)} %bitcast.42, ...), custom_call_target="tpu_custom_call" | custom-call | flops 367001600 | bytes 3670016 | tf_op jit(solution)/shard_map/pallas_call | solution.py:248
  123.3 2.6 %collective-permute-done.25.refs_3_ = bf16[1024,512]{1,0:T(8,128)(2,1)S(1)} collective-permute-done((bf16[1024,512]{1,0:T(8,128)(2,1)S(1)}, bf16[1024,512]{1,0:T(8,128)(2,1)S(1)}, u32[]{:S(2)}, u32[]{:S(2)}) %collective-permute-start.25) | collective-permute-done | bytes 1048608 | tf_op jit(solution)/shard_map/ppermute | solution.py:320
  125.8 2.4 %shard_map.80 = (bf16[1024,128]{1,0:T(8,128)(2,1)S(1)}, bf16[1024,128]{1,0:T(8,128)(2,1)S(1)}) custom-call(s32[4]{0:T(128)S(1)} %pad_add_fusion.1.table, bf16[1024,512]{1,0:T(8,128)(2,1)S(1)} %bitcast.32, bf16[1024,512]{1,0:T(8,128)(2,1)S(1)} %bitcast.37, bf16[1024,512]{1,0:T(8,128)(2,1)S(1)} %collective-permute-done.24.refs_2_, ...), custom_call_target="tpu_custom_call" | custom-call | flops 1073741824 | bytes 5242880 | tf_op jit(solution)/shard_map/pallas_call | solution.py:292
  128.4 5.0 %collective-permute-start.32 = (bf16[1024,128]{1,0:T(8,128)(2,1)S(1)}, bf16[1024,128]{1,0:T(8,128)(2,1)S(1)}, u32[]{:S(2)}, u32[]{:S(2)}) collective-permute-start(bf16[1024,128]{1,0:T(8,128)(2,1)S(1)} %get-tuple-element.120), channel_id=1, source_target_pairs={{0,28},{2,30},{4,24},{6,26},{8,20},{10,22},{12,16},{14,18},{16,12}... | collective-permute-start | bytes 786440 | tf_op jit(solution)/shard_map/ppermute | solution.py:319
  133.3 2.4 %shard_map.77 = (bf16[1024,128]{1,0:T(8,128)(2,1)S(1)}, bf16[1024,128]{1,0:T(8,128)(2,1)S(1)}) custom-call(s32[4]{0:T(128)S(1)} %pad_add_fusion.1.table, bf16[1024,512]{1,0:T(8,128)(2,1)S(1)} %bitcast.33, bf16[1024,512]{1,0:T(8,128)(2,1)S(1)} %bitcast.38, bf16[1024,512]{1,0:T(8,128)(2,1)S(1)} %collective-permute-done.24.refs_2_, ...), custom_call_target="tpu_custom_call" | custom-call | flops 1073741824 | bytes 5242880 | tf_op jit(solution)/shard_map/pallas_call | solution.py:292
  135.8 2.4 %shard_map.78 = (bf16[1024,128]{1,0:T(8,128)(2,1)S(1)}, bf16[1024,128]{1,0:T(8,128)(2,1)S(1)}) custom-call(s32[4]{0:T(128)S(1)} %pad_add_fusion.1.table, bf16[1024,512]{1,0:T(8,128)(2,1)S(1)} %bitcast.34, bf16[1024,512]{1,0:T(8,128)(2,1)S(1)} %bitcast.39, bf16[1024,512]{1,0:T(8,128)(2,1)S(1)} %collective-permute-done.24.refs_2_, ...), custom_call_target="tpu_custom_call" | custom-call | flops 1073741824 | bytes 5242880 | tf_op jit(solution)/shard_map/pallas_call | solution.py:292
  138.2 2.4 %shard_map.79 = (bf16[1024,128]{1,0:T(8,128)(2,1)S(1)}, bf16[1024,128]{1,0:T(8,128)(2,1)S(1)}) custom-call(s32[4]{0:T(128)S(1)} %pad_add_fusion.1.table, bf16[1024,512]{1,0:T(8,128)(2,1)S(1)} %bitcast.35, bf16[1024,512]{1,0:T(8,128)(2,1)S(1)} %bitcast.40, bf16[1024,512]{1,0:T(8,128)(2,1)S(1)} %collective-permute-done.24.refs_2_, ...), custom_call_target="tpu_custom_call" | custom-call | flops 1073741824 | bytes 5242880 | tf_op jit(solution)/shard_map/pallas_call | solution.py:292
  140.7 2.6 %collective-permute-start.27 = (bf16[1024,128]{1,0:T(8,128)(2,1)S(1)}, bf16[1024,128]{1,0:T(8,128)(2,1)S(1)}, u32[]{:S(2)}, u32[]{:S(2)}) collective-permute-start(bf16[1024,128]{1,0:T(8,128)(2,1)S(1)} %get-tuple-element.114), channel_id=1, source_target_pairs={{0,20},{2,22},{4,16},{6,18},{8,28},{10,30},{12,24},{14,26},{16,4},... | collective-permute-start | bytes 786440 | tf_op jit(solution)/shard_map/ppermute | solution.py:319
  143.4 18.2 %collective-permute-start.29 = (bf16[1024,128]{1,0:T(8,128)(2,1)S(1)}, bf16[1024,128]{1,0:T(8,128)(2,1)S(1)}, u32[]{:S(2)}, u32[]{:S(2)}) collective-permute-start(bf16[1024,128]{1,0:T(8,128)(2,1)S(1)} %get-tuple-element.116), channel_id=1, source_target_pairs={{0,12},{2,14},{4,8},{6,10},{8,4},{10,6},{12,0},{14,2},{16,28},{18,... | collective-permute-start | bytes 786440 | tf_op jit(solution)/shard_map/ppermute | solution.py:319
  161.6 1.4 collective-permute-start.30
  163.2 2.2 %shard_map.81.refs_2_ = f32[128,64,128]{2,1,0:T(8,128)} custom-call(s32[2]{0:T(128)S(1)} %pad_add_fusion.4.table, bf16[1024,128]{1,0:T(8,128)(2,1)S(1)} %collective-permute-done.31.refs_0_, bf16[1024,128]{1,0:T(8,128)(2,1)S(1)} %collective-permute-done.32.refs_1_), custom_call_target="tpu_custom_call" | custom-call | flops 262144 | bytes 1572864 | tf_op jit(solution)/shard_map/pallas_call | solution.py:91
  165.4 7.3 %collective-permute-done.30.refs_1_ = bf16[1024,128]{1,0:T(8,128)(2,1)S(1)} collective-permute-done((bf16[1024,128]{1,0:T(8,128)(2,1)S(1)}, bf16[1024,128]{1,0:T(8,128)(2,1)S(1)}, u32[]{:S(2)}, u32[]{:S(2)}) %collective-permute-start.30) | collective-permute-done | bytes 262176 | tf_op jit(solution)/shard_map/ppermute | solution.py:319
  172.7 2.2 %shard_map.82.refs_2_ = f32[128,64,128]{2,1,0:T(8,128)} custom-call(s32[2]{0:T(128)S(1)} %pad_add_fusion.3.table, bf16[1024,128]{1,0:T(8,128)(2,1)S(1)} %get-tuple-element.117.refs_0_, bf16[1024,128]{1,0:T(8,128)(2,1)S(1)} %collective-permute-done.30.refs_1_, f32[128,64,128]{2,1,0:T(8,128)} %shard_map.81.refs_2_), custom_call_target="tpu_custom_call", output_to_operand_aliasing={{}: (3, {})} | custom-call | flops 262144 | bytes 1572864 | tf_op jit(solution)/shard_map/pallas_call | solution.py:91
  174.9 2.2 %shard_map.83.refs_2_ = f32[128,64,128]{2,1,0:T(8,128)} custom-call(s32[2]{0:T(128)S(1)} %get-tuple-element.135.table, bf16[1024,128]{1,0:T(8,128)(2,1)S(1)} %collective-permute-done.28.refs_0_, bf16[1024,128]{1,0:T(8,128)(2,1)S(1)} %collective-permute-done.29.refs_1_, f32[128,64,128]{2,1,0:T(8,128)} %shard_map.82.refs_2_), custom_call_target="tpu_custom_call", output_to_operand_aliasing={{}: (3, {})} | custom-call | flops 262144 | bytes 1572864 | tf_op jit(solution)/shard_map/pallas_call | solution.py:91
  177.0 1.1 collective-permute-done.27.refs_1_
  178.2 2.2 %shard_map.84 = f32[128,64,128]{2,1,0:T(8,128)} custom-call(s32[2]{0:T(128)S(1)} %get-tuple-element.134.table, bf16[1024,128]{1,0:T(8,128)(2,1)S(1)} %collective-permute-done.26.refs_0_, bf16[1024,128]{1,0:T(8,128)(2,1)S(1)} %collective-permute-done.27.refs_1_, f32[128,64,128]{2,1,0:T(8,128)} %shard_map.83.refs_2_), custom_call_target="tpu_custom_call", output_to_operand_aliasing={{}: (3, {})} | custom-call | flops 262144 | bytes 1572864 | tf_op jit(solution)/shard_map/pallas_call | solution.py:91
  (70 shorter events, 4.6 us)
Async XLA Ops:
  0.0 25.5 %copy-start.7 = (bf16[128,2048]{1,0:T(8,128)(2,1)S(1)}, bf16[128,2048]{1,0:T(8,128)(2,1)}, u32[]{:S(2)}) copy-start(bf16[128,2048]{1,0:T(8,128)(2,1)} %refs_0_.1) | copy-start | bytes 1572868
  1.0 22.5 %collective-permute-start = (bf16[64,2048]{1,0:T(8,128)(2,1)S(1)}, bf16[64,2048]{1,0:T(8,128)(2,1)S(1)}, u32[]{:S(2)}, u32[]{:S(2)}) collective-permute-start(bf16[64,2048]{1,0:T(8,128)(2,1)S(1)} %constant_dynamic-slice_fusion), channel_id=1, source_target_pairs={{0,8},{2,10},{4,12},{6,14},{8,0},{10,2},{12,4},{14,6},{16,24},{18,... | collective-permute-start | bytes 786440 | tf_op jit(solution)/shard_map/ppermute | solution.py:319
  4.1 21.4 %collective-permute-start.1 = (bf16[64,2048]{1,0:T(8,128)(2,1)S(1)}, bf16[64,2048]{1,0:T(8,128)(2,1)S(1)}, u32[]{:S(2)}, u32[]{:S(2)}) collective-permute-start(bf16[64,2048]{1,0:T(8,128)(2,1)S(1)} %constant_dynamic-slice_fusion), channel_id=1, source_target_pairs={{0,16},{2,18},{4,20},{6,22},{8,24},{10,26},{12,28},{14,30},{16,0},... | collective-permute-start | bytes 786440 | tf_op jit(solution)/shard_map/ppermute | solution.py:319
  6.7 18.8 %collective-permute-start.2 = (bf16[64,2048]{1,0:T(8,128)(2,1)S(1)}, bf16[64,2048]{1,0:T(8,128)(2,1)S(1)}, u32[]{:S(2)}, u32[]{:S(2)}) collective-permute-start(bf16[64,2048]{1,0:T(8,128)(2,1)S(1)} %constant_dynamic-slice_fusion), channel_id=1, source_target_pairs={{0,24},{2,26},{4,28},{6,30},{8,16},{10,18},{12,20},{14,22},{16,8},... | collective-permute-start | bytes 786440 | tf_op jit(solution)/shard_map/ppermute | solution.py:319
  6.7 18.8 %collective-permute-start.3 = (bf16[128,2048]{1,0:T(8,128)(2,1)}, bf16[128,2048]{1,0:T(8,128)(2,1)S(1)}, u32[]{:S(2)}, u32[]{:S(2)}) collective-permute-start(bf16[128,2048]{1,0:T(8,128)(2,1)} %refs_0_.1), channel_id=1, source_target_pairs={{0,4},{2,6},{4,0},{6,2},{8,12},{10,14},{12,8},{14,10},{16,20},{18,... | collective-permute-start | bytes 1572872 | tf_op jit(solution)/shard_map/ppermute | solution.py:319
  8.5 1.8 %collective-permute-start.4 = (f32[128]{0:T(128)}, f32[128]{0:T(128)S(1)}, u32[]{:S(2)}, u32[]{:S(2)}) collective-permute-start(f32[128]{0:T(128)} %param.8), channel_id=1, source_target_pairs={{0,2},{2,0},{4,6},{6,4},{8,10},{10,8},{12,14},{14,12},{16,18},{18,... | collective-permute-start | bytes 1544 | tf_op jit(solution)/shard_map/ppermute | solution.py:320
  10.3 3.6 %collective-permute-start.5 = (f32[3,128]{1,0:T(4,128)S(1)}, f32[3,128]{1,0:T(4,128)S(1)}, u32[]{:S(2)}, u32[]{:S(2)}) collective-permute-start(f32[3,128]{1,0:T(4,128)S(1)} %get-tuple-element.126), channel_id=1, source_target_pairs={{0,1},{1,0},{2,3},{3,2},{4,5},{5,4},{6,7},{7,6},{8,9},{9,8},{10,11... | collective-permute-start | bytes 4616 | tf_op jit(solution)/shard_map/ppermute | solution.py:354
  13.9 3.6 %collective-permute-start.6 = (f32[3,128]{1,0:T(4,128)S(1)}, f32[3,128]{1,0:T(4,128)S(1)}, u32[]{:S(2)}, u32[]{:S(2)}) collective-permute-start(f32[3,128]{1,0:T(4,128)S(1)} %get-tuple-element.125), channel_id=1, source_target_pairs={{1,0},{0,1},{3,2},{2,3},{5,4},{4,5},{7,6},{6,7},{9,8},{8,9},{11,10... | collective-permute-start | bytes 4616 | tf_op jit(solution)/shard_map/ppermute | solution.py:355
  26.8 23.7 %collective-permute-start.9 = (bf16[1040,128]{1,0:T(8,128)(2,1)S(1)}, bf16[1040,128]{1,0:T(8,128)(2,1)S(1)}, u32[]{:S(2)}, u32[]{:S(2)}) collective-permute-start(bf16[1040,128]{1,0:T(8,128)(2,1)S(1)} %get-tuple-element.76), channel_id=1, source_target_pairs={{0,16},{2,18},{4,20},{6,22},{8,24},{10,26},{12,28},{14,30},{16,0},... | collective-permute-start | bytes 798728 | tf_op jit(solution)/shard_map/ppermute | solution.py:319
  32.6 23.4 %collective-permute-start.10 = (bf16[1040,128]{1,0:T(8,128)(2,1)S(1)}, bf16[1040,128]{1,0:T(8,128)(2,1)S(1)}, u32[]{:S(2)}, u32[]{:S(2)}) collective-permute-start(bf16[1040,128]{1,0:T(8,128)(2,1)S(1)} %get-tuple-element.77), channel_id=1, source_target_pairs={{0,20},{2,22},{4,16},{6,18},{8,28},{10,30},{12,24},{14,26},{16,4},... | collective-permute-start | bytes 798728 | tf_op jit(solution)/shard_map/ppermute | solution.py:319
  33.7 23.6 %collective-permute-start.7 = (bf16[192,2048]{1,0:T(8,128)(2,1)S(1)}, bf16[192,2048]{1,0:T(8,128)(2,1)S(1)}, u32[]{:S(2)}, u32[]{:S(2)}) collective-permute-start(bf16[192,2048]{1,0:T(8,128)(2,1)S(1)} %constant_dynamic-update-slice_fusion), channel_id=1, source_target_pairs={{0,4},{2,6},{4,0},{6,2},{8,12},{10,14},{12,8},{14,10},{16,20},{18,... | collective-permute-start | bytes 2359304 | tf_op jit(solution)/shard_map/ppermute | solution.py:319
  34.3 23.1 %collective-permute-start.8 = (bf16[192,2048]{1,0:T(8,128)(2,1)S(1)}, bf16[192,2048]{1,0:T(8,128)(2,1)S(1)}, u32[]{:S(2)}, u32[]{:S(2)}) collective-permute-start(bf16[192,2048]{1,0:T(8,128)(2,1)S(1)} %constant_dynamic-update-slice_fusion), channel_id=1, source_target_pairs={{0,1},{1,0},{2,3},{3,2},{4,5},{5,4},{6,7},{7,6},{8,9},{9,8},{10,11... | collective-permute-start | bytes 2359304 | tf_op jit(solution)/shard_map/ppermute | solution.py:321
  57.4 9.6 %copy-start.1 = (bf16[192,2048]{1,0:T(8,128)(2,1)}, bf16[192,2048]{1,0:T(8,128)(2,1)S(1)}, u32[]{:S(2)}) copy-start(bf16[192,2048]{1,0:T(8,128)(2,1)S(1)} %collective-permute-done.8.refs_1_) | copy-start | bytes 2359300
  57.4 8.0 %collective-permute-start.15 = (bf16[1040,128]{1,0:T(8,128)(2,1)S(1)}, bf16[1040,128]{1,0:T(8,128)(2,1)S(1)}, u32[]{:S(2)}, u32[]{:S(2)}) collective-permute-start(bf16[1040,128]{1,0:T(8,128)(2,1)S(1)} %get-tuple-element.89), channel_id=1, source_target_pairs={{0,4},{2,6},{4,0},{6,2},{8,12},{10,14},{12,8},{14,10},{16,20},{18,... | collective-permute-start | bytes 798728 | tf_op jit(solution)/shard_map/ppermute | solution.py:319
  57.9 9.8 %collective-permute-start.16 = (bf16[1040,128]{1,0:T(8,128)(2,1)S(1)}, bf16[1040,128]{1,0:T(8,128)(2,1)S(1)}, u32[]{:S(2)}, u32[]{:S(2)}) collective-permute-start(bf16[1040,128]{1,0:T(8,128)(2,1)S(1)} %get-tuple-element.90), channel_id=1, source_target_pairs={{0,8},{2,10},{4,12},{6,14},{8,0},{10,2},{12,4},{14,6},{16,24},{18,... | collective-permute-start | bytes 798728 | tf_op jit(solution)/shard_map/ppermute | solution.py:319
  60.3 17.7 %collective-permute-start.13 = (bf16[128,2048]{1,0:T(8,128)(2,1)}, bf16[128,2048]{1,0:T(8,128)(2,1)S(1)}, u32[]{:S(2)}, u32[]{:S(2)}) collective-permute-start(bf16[128,2048]{1,0:T(8,128)(2,1)} %slice.54), channel_id=1, source_target_pairs={{0,1},{1,0},{2,3},{3,2},{4,5},{5,4},{6,7},{7,6},{8,9},{9,8},{10,11... | collective-permute-start | bytes 1572872 | tf_op jit(solution)/shard_map/ppermute | solution.py:321
  61.8 11.5 %collective-permute-start.17 = (bf16[1040,128]{1,0:T(8,128)(2,1)}, bf16[1040,128]{1,0:T(8,128)(2,1)}, u32[]{:S(2)}, u32[]{:S(2)}) collective-permute-start(bf16[1040,128]{1,0:T(8,128)(2,1)} %get-tuple-element.91), channel_id=1, source_target_pairs={{0,12},{2,14},{4,8},{6,10},{8,4},{10,6},{12,0},{14,2},{16,28},{18,... | collective-permute-start | bytes 798728 | tf_op jit(solution)/shard_map/ppermute | solution.py:319
  63.2 17.2 %collective-permute-start.11 = (bf16[1040,128]{1,0:T(8,128)(2,1)}, bf16[1040,128]{1,0:T(8,128)(2,1)}, u32[]{:S(2)}, u32[]{:S(2)}) collective-permute-start(bf16[1040,128]{1,0:T(8,128)(2,1)} %get-tuple-element.85), channel_id=1, source_target_pairs={{0,24},{2,26},{4,28},{6,30},{8,16},{10,18},{12,20},{14,22},{16,8},... | collective-permute-start | bytes 798728 | tf_op jit(solution)/shard_map/ppermute | solution.py:319
  65.4 2.3 %copy-start.3 = (bf16[1040,128]{1,0:T(8,128)(2,1)}, bf16[1040,128]{1,0:T(8,128)(2,1)S(1)}, u32[]{:S(2)}) copy-start(bf16[1040,128]{1,0:T(8,128)(2,1)S(1)} %collective-permute-done.15.refs_0_) | copy-start | bytes 798724
  65.4 18.4 %collective-permute-start.12 = (bf16[1040,128]{1,0:T(8,128)(2,1)}, bf16[1040,128]{1,0:T(8,128)(2,1)}, u32[]{:S(2)}, u32[]{:S(2)}) collective-permute-start(bf16[1040,128]{1,0:T(8,128)(2,1)} %get-tuple-element.86), channel_id=1, source_target_pairs={{0,28},{2,30},{4,24},{6,26},{8,20},{10,22},{12,16},{14,18},{16,12}... | collective-permute-start | bytes 798728 | tf_op jit(solution)/shard_map/ppermute | solution.py:319
  67.7 0.7 copy-start.5
  68.4 9.6 %collective-permute-start.14 = (bf16[64,2048]{1,0:T(8,128)(2,1)}, bf16[64,2048]{1,0:T(8,128)(2,1)}, u32[]{:S(2)}, u32[]{:S(2)}) collective-permute-start(bf16[64,2048]{1,0:T(8,128)(2,1)} %slice.55), channel_id=1, source_target_pairs={{0,4},{2,6},{4,0},{6,2},{8,12},{10,14},{12,8},{14,10},{16,20},{18,... | collective-permute-start | bytes 786440 | tf_op jit(solution)/shard_map/ppermute | solution.py:319
  69.9 1.1 copy-start.2
  71.0 2.2 %copy-start.4 = (bf16[1040,128]{1,0:T(8,128)(2,1)S(1)}, bf16[1040,128]{1,0:T(8,128)(2,1)}, u32[]{:S(2)}) copy-start(bf16[1040,128]{1,0:T(8,128)(2,1)} %copy-done.3) | copy-start | bytes 798724
  71.0 2.2 %copy-start.6 = (bf16[1040,128]{1,0:T(8,128)(2,1)S(1)}, bf16[1040,128]{1,0:T(8,128)(2,1)}, u32[]{:S(2)}) copy-start(bf16[1040,128]{1,0:T(8,128)(2,1)} %copy-done.5) | copy-start | bytes 798724
  88.6 4.5 %collective-permute-start.18 = (f32[1024,512]{1,0:T(8,128)}, f32[1024,512]{1,0:T(8,128)}, u32[]{:S(2)}, u32[]{:S(2)}) collective-permute-start(f32[1024,512]{1,0:T(8,128)} %shard_map.71), channel_id=1, source_target_pairs={{0,2},{2,0},{4,6},{6,4},{8,10},{10,8},{12,14},{14,12},{16,18},{18,... | collective-permute-start | bytes 6291464 | tf_op jit(solution)/shard_map/ppermute | solution.py:320
  92.2 6.0 %collective-permute-start.21 = (f32[1024,512]{1,0:T(8,128)}, f32[1024,512]{1,0:T(8,128)}, u32[]{:S(2)}, u32[]{:S(2)}) collective-permute-start(f32[1024,512]{1,0:T(8,128)} %shard_map.72), channel_id=1, source_target_pairs={{0,2},{2,0},{4,6},{6,4},{8,10},{10,8},{12,14},{14,12},{16,18},{18,... | collective-permute-start | bytes 6291464 | tf_op jit(solution)/shard_map/ppermute | solution.py:320
  96.1 12.0 %collective-permute-start.19 = (bf16[3,128,512]{2,1,0:T(8,128)(2,1)S(1)}, bf16[3,128,512]{2,1,0:T(8,128)(2,1)S(1)}, u32[]{:S(2)}, u32[]{:S(2)}) collective-permute-start(bf16[3,128,512]{2,1,0:T(8,128)(2,1)S(1)} %bitcast.45), channel_id=1, source_target_pairs={{0,4},{2,6},{4,12},{6,14},{12,8},{14,10},{8,16},{10,18},{16,20},{1... | collective-permute-start | bytes 1179656 | tf_op jit(solution)/shard_map/ppermute | solution.py:423
  97.1 13.9 %collective-permute-start.20 = (bf16[3,128,512]{2,1,0:T(8,128)(2,1)S(1)}, bf16[3,128,512]{2,1,0:T(8,128)(2,1)S(1)}, u32[]{:S(2)}, u32[]{:S(2)}) collective-permute-start(bf16[3,128,512]{2,1,0:T(8,128)(2,1)S(1)} %bitcast.43), channel_id=1, source_target_pairs={{4,0},{6,2},{12,4},{14,6},{8,12},{10,14},{16,8},{18,10},{20,16},{2... | collective-permute-start | bytes 1179656 | tf_op jit(solution)/shard_map/ppermute | solution.py:424
  101.2 14.7 %collective-permute-start.22 = (bf16[3,128,512]{2,1,0:T(8,128)(2,1)S(1)}, bf16[3,128,512]{2,1,0:T(8,128)(2,1)S(1)}, u32[]{:S(2)}, u32[]{:S(2)}) collective-permute-start(bf16[3,128,512]{2,1,0:T(8,128)(2,1)S(1)} %bitcast.46), channel_id=1, source_target_pairs={{0,4},{2,6},{4,12},{6,14},{12,8},{14,10},{8,16},{10,18},{16,20},{1... | collective-permute-start | bytes 1179656 | tf_op jit(solution)/shard_map/ppermute | solution.py:423
  104.1 14.5 %collective-permute-start.23 = (bf16[3,128,512]{2,1,0:T(8,128)(2,1)S(1)}, bf16[3,128,512]{2,1,0:T(8,128)(2,1)S(1)}, u32[]{:S(2)}, u32[]{:S(2)}) collective-permute-start(bf16[3,128,512]{2,1,0:T(8,128)(2,1)S(1)} %bitcast.44), channel_id=1, source_target_pairs={{4,0},{6,2},{12,4},{14,6},{8,12},{10,14},{16,8},{18,10},{20,16},{2... | collective-permute-start | bytes 1179656 | tf_op jit(solution)/shard_map/ppermute | solution.py:424
  111.0 14.9 %copy-start = (bf16[1024,2048]{1,0:T(8,128)(2,1)S(1)}, bf16[1024,2048]{1,0:T(8,128)(2,1)}, u32[]{:S(2)}) copy-start(bf16[1024,2048]{1,0:T(8,128)(2,1)} %shard_map.70.b_ref.refs_4_) | copy-start | bytes 12582916
  115.8 7.5 %collective-permute-start.24 = (bf16[1024,512]{1,0:T(8,128)(2,1)S(1)}, bf16[1024,512]{1,0:T(8,128)(2,1)S(1)}, u32[]{:S(2)}, u32[]{:S(2)}) collective-permute-start(bf16[1024,512]{1,0:T(8,128)(2,1)S(1)} %bitcast.31), channel_id=1, source_target_pairs={{0,2},{2,0},{4,6},{6,4},{8,10},{10,8},{12,14},{14,12},{16,18},{18,... | collective-permute-start | bytes 3145736 | tf_op jit(solution)/shard_map/ppermute | solution.py:320
  123.1 2.7 %collective-permute-start.25 = (bf16[1024,512]{1,0:T(8,128)(2,1)S(1)}, bf16[1024,512]{1,0:T(8,128)(2,1)S(1)}, u32[]{:S(2)}, u32[]{:S(2)}) collective-permute-start(bf16[1024,512]{1,0:T(8,128)(2,1)S(1)} %bitcast.36), channel_id=1, source_target_pairs={{0,2},{2,0},{4,6},{6,4},{8,10},{10,8},{12,14},{14,12},{16,18},{18,... | collective-permute-start | bytes 3145736 | tf_op jit(solution)/shard_map/ppermute | solution.py:320
  128.3 15.1 %collective-permute-start.31 = (bf16[1024,128]{1,0:T(8,128)(2,1)S(1)}, bf16[1024,128]{1,0:T(8,128)(2,1)S(1)}, u32[]{:S(2)}, u32[]{:S(2)}) collective-permute-start(bf16[1024,128]{1,0:T(8,128)(2,1)S(1)} %get-tuple-element.119), channel_id=1, source_target_pairs={{0,24},{2,26},{4,28},{6,30},{8,16},{10,18},{12,20},{14,22},{16,8},... | collective-permute-start | bytes 786440 | tf_op jit(solution)/shard_map/ppermute | solution.py:319
  128.4 33.3 %collective-permute-start.32 = (bf16[1024,128]{1,0:T(8,128)(2,1)S(1)}, bf16[1024,128]{1,0:T(8,128)(2,1)S(1)}, u32[]{:S(2)}, u32[]{:S(2)}) collective-permute-start(bf16[1024,128]{1,0:T(8,128)(2,1)S(1)} %get-tuple-element.120), channel_id=1, source_target_pairs={{0,28},{2,30},{4,24},{6,26},{8,20},{10,22},{12,16},{14,18},{16,12}... | collective-permute-start | bytes 786440 | tf_op jit(solution)/shard_map/ppermute | solution.py:319
  140.7 36.3 %collective-permute-start.26 = (bf16[1024,128]{1,0:T(8,128)(2,1)S(1)}, bf16[1024,128]{1,0:T(8,128)(2,1)S(1)}, u32[]{:S(2)}, u32[]{:S(2)}) collective-permute-start(bf16[1024,128]{1,0:T(8,128)(2,1)S(1)} %get-tuple-element.113), channel_id=1, source_target_pairs={{0,16},{2,18},{4,20},{6,22},{8,24},{10,26},{12,28},{14,30},{16,0},... | collective-permute-start | bytes 786440 | tf_op jit(solution)/shard_map/ppermute | solution.py:319
  140.7 37.4 %collective-permute-start.27 = (bf16[1024,128]{1,0:T(8,128)(2,1)S(1)}, bf16[1024,128]{1,0:T(8,128)(2,1)S(1)}, u32[]{:S(2)}, u32[]{:S(2)}) collective-permute-start(bf16[1024,128]{1,0:T(8,128)(2,1)S(1)} %get-tuple-element.114), channel_id=1, source_target_pairs={{0,20},{2,22},{4,16},{6,18},{8,28},{10,30},{12,24},{14,26},{16,4},... | collective-permute-start | bytes 786440 | tf_op jit(solution)/shard_map/ppermute | solution.py:319
  143.4 31.5 %collective-permute-start.28 = (bf16[1024,128]{1,0:T(8,128)(2,1)S(1)}, bf16[1024,128]{1,0:T(8,128)(2,1)S(1)}, u32[]{:S(2)}, u32[]{:S(2)}) collective-permute-start(bf16[1024,128]{1,0:T(8,128)(2,1)S(1)} %get-tuple-element.115), channel_id=1, source_target_pairs={{0,8},{2,10},{4,12},{6,14},{8,0},{10,2},{12,4},{14,6},{16,24},{18,... | collective-permute-start | bytes 786440 | tf_op jit(solution)/shard_map/ppermute | solution.py:319
  143.4 31.5 %collective-permute-start.29 = (bf16[1024,128]{1,0:T(8,128)(2,1)S(1)}, bf16[1024,128]{1,0:T(8,128)(2,1)S(1)}, u32[]{:S(2)}, u32[]{:S(2)}) collective-permute-start(bf16[1024,128]{1,0:T(8,128)(2,1)S(1)} %get-tuple-element.116), channel_id=1, source_target_pairs={{0,12},{2,14},{4,8},{6,10},{8,4},{10,6},{12,0},{14,2},{16,28},{18,... | collective-permute-start | bytes 786440 | tf_op jit(solution)/shard_map/ppermute | solution.py:319
  161.6 11.1 %collective-permute-start.30 = (bf16[1024,128]{1,0:T(8,128)(2,1)S(1)}, bf16[1024,128]{1,0:T(8,128)(2,1)S(1)}, u32[]{:S(2)}, u32[]{:S(2)}) collective-permute-start(bf16[1024,128]{1,0:T(8,128)(2,1)S(1)} %get-tuple-element.118), channel_id=1, source_target_pairs={{0,4},{2,6},{4,0},{6,2},{8,12},{10,14},{12,8},{14,10},{16,20},{18,... | collective-permute-start | bytes 786440 | tf_op jit(solution)/shard_map/ppermute | solution.py:319

commit v4 on v3

--- a/solution.py
+++ b/solution.py
@@ -10,6 +10,7 @@
 
 SWEEPS = 4
 HALO = SWEEPS - 1
+TAIL = 16
 CHUNKS = 2
 MIB = 1024 * 1024
 F32, BF16 = jnp.float32, jnp.bfloat16
@@ -42,11 +43,13 @@
                 high = (x_ref[:, rows + r, :] * w).astype(BF16).T
                 a_ref[r * wide : (r + 1) * wide, :] = jnp.where(swap, high, low)
                 b_ref[r * wide : (r + 1) * wide, :] = jnp.where(swap, low, high)
-            a_ref[rows * wide :, :] = e_ref[...]
-            b_ref[rows * wide :, :] = e_ref[...]
-
-
-def scale(table, weight, extra, divergence, chips):
+            for ref in (a_ref, b_ref):
+                ref[rows * wide : rows * wide + TAIL, :] = e_ref[...]
+                if ref.shape[0] > rows * wide + TAIL:
+                    ref[rows * wide + TAIL :, :] = e_ref[...]
+
+
+def scale(table, weight, extra, divergence, chips, longer):
     planes, width, wide = divergence.shape
     rows, pairs = width // chips, chips // 2
     tall = rows * wide + extra.shape[0]
@@ -62,7 +65,7 @@
             ],
             out_specs=[pl.BlockSpec(memory_space=pltpu.VMEM)] * chips,
         ),
-        out_shape=[jax.ShapeDtypeStruct((tall, planes), BF16)] * chips,
+        out_shape=[jax.ShapeDtypeStruct((tall + TAIL * (s in longer), planes), BF16) for s in range(chips)],
         compiler_params=params(12),
         cost_estimate=cost(planes * width * wide, planes * width * wide * 6),
     )(table, weight, extra, divergence)
@@ -116,18 +119,17 @@
     cells, planes = o_ref.shape[-2], x_refs[0].shape[1]
     copies = []
     for ref, s in zip(x_refs, blocks):
-        tail = ref.shape[0] - cells
-        copies.append((ref.at[pl.ds(cells, tail), :], e_ref.at[s]))
+        copies.append((ref.at[pl.ds(cells, TAIL), :], e_ref.at[s]))
         place = o_ref.at[s] if len(o_ref.shape) == 3 else o_ref.at[:, pl.ds(s * planes, planes)]
         copies.append((ref.at[pl.ds(0, cells), :], place))
     run_copies(copies, sem)
 
 
 def gather(xs, blocks, cells, chips, held, mark):
-    tall, planes = xs[0].shape
+    planes = xs[0].shape[1]
     out = [
         pltpu.VMEM((chips, cells, planes) if planes % 128 else (cells, chips * planes), BF16),
-        pltpu.VMEM((chips, tall - cells, planes), BF16),
+        pltpu.VMEM((chips, TAIL, planes), BF16),
     ]
     count = len(xs) + (len(held) if held else 0)
     return pl.pallas_call(
@@ -263,43 +265,56 @@
     )(eigen, fluid, up, own, down)
 
 
-def inverse_body(tile, table, *refs):
-    parts, b_ref, o_refs = refs[:-3], refs[-3], refs[-2:]
+def inverse_body(tile, skip, based, table, *refs):
+    outs = 2 if len(refs) and refs[-1].dtype == BF16 else 1
+    o_refs, ins = refs[-outs:], refs[:-outs]
+    base_ref = ins[-1] if based else None
+    parts, b_ref = (ins[:-2], ins[-2]) if based else (ins[:-1], ins[-1])
     cells, wide = parts[0].shape
-    planes = o_refs[0].shape[1]
 
     def body(i, _):
         rows = pl.ds(pl.multiple_of(i * tile, tile), tile)
         total = None
         for k, part in enumerate(parts):
-            cols = pl.ds(pl.multiple_of(table[k] * wide, wide), wide)
+            cols = pl.ds(pl.multiple_of(table[skip + k] * wide, wide), wide)
             term = lax.dot_general(
                 part[rows, :], b_ref[:, cols], (((1,), (1,)), ((), ())), preferred_element_type=F32
             )
             total = term if total is None else total + term
-        o_refs[0][rows, :] = total[:, :planes].astype(BF16)
-        o_refs[1][rows, :] = total[:, planes:].astype(BF16)
+        if based:
+            total = total + base_ref[rows, :]
+        if outs == 1:
+            o_refs[0][rows, :] = total
+        else:
+            planes = o_refs[0].shape[1]
+            o_refs[0][rows, :] = total[:, :planes].astype(BF16)
+            o_refs[1][rows, :] = total[:, planes:].astype(BF16)
         return 0
 
     lax.fori_loop(0, cells // tile, body, 0)
 
 
-def inverse(table, parts, basis, pair, planes):
+def inverse(table, parts, basis, pair, planes, skip=0, base=None, part_only=False):
     cells, wide = parts[0].shape
     modes = basis.shape[1]
-    out = jax.ShapeDtypeStruct((cells, planes), BF16)
     whole = pl.BlockSpec(memory_space=pltpu.VMEM)
-    return pl.pallas_call(
-        functools.partial(inverse_body, min(cells, 256)),
+    if part_only:
+        out, out_specs = jax.ShapeDtypeStruct((cells, 2 * planes), F32), whole
+    else:
+        out, out_specs = [jax.ShapeDtypeStruct((cells, planes), BF16)] * 2, [whole] * 2
+    extra = [] if base is None else [base]
+    return pl.pallas_call(
+        functools.partial(inverse_body, min(cells, 256), skip, base is not None),
         grid=(1,),
         in_specs=[pl.BlockSpec(memory_space=pltpu.SMEM)]
         + [whole] * len(parts)
-        + [pl.BlockSpec((2 * planes, modes), lambda i: (pair, 0))],
-        out_specs=[whole] * 2,
-        out_shape=[out, out],
+        + [pl.BlockSpec((2 * planes, modes), lambda i: (pair, 0))]
+        + [whole] * len(extra),
+        out_specs=out_specs,
+        out_shape=out,
         compiler_params=params(16),
         cost_estimate=cost(4 * cells * modes * planes, 2 * cells * modes + 4 * planes * modes),
-    )(table, *parts, basis)
+    )(table, *parts, basis, *extra)
 
 
 def local(divergence, basis, eigen, plane_level, spacing, solid):
@@ -356,9 +371,8 @@
     ]
 
     divergence = pltpu.with_memory_space_constraint(divergence, pltpu.HBM)
-    extra, edges = lax.optimization_barrier((extra, edges))
     blocks = [table[0] for table in tables] + [table[1] for table in tables]
-    send = scale(i32(*blocks), weight, extra, divergence, chips)
+    send = scale(i32(*blocks), weight, extra, divergence, chips, range(3 * chips // 4, chips))
 
     half = planes // 2
     far = chips // 2
@@ -371,7 +385,7 @@
     beside = chip_swap(basis, 1)
     layout = (("whole", (0,)), *[("mine", (s,)) for s in ids], ("whole", (1,)))
     full = join(i32(odd), [basis, *column, beside], layout, planes, chips, None, LATE)
-    column, beside, full, send = lax.optimization_barrier((column, beside, full, send))
+    column, beside, full, send, edges = lax.optimization_barrier((column, beside, full, send, edges))
 
     held = jnp.concatenate(column)
     over_y, over_x = chip_swap(held, 1), tile_swap(held)
@@ -379,16 +393,14 @@
     x = gather([send[0], *[chip_swap(send[s], s) for s in evens]], [0, *evens], cells, chips, None, LATE)
     over_y, over_x, x, send = lax.optimization_barrier((over_y, over_x, x, send))
 
-    cut = (2 * len(ids) + 2) // 3
-    corner_x, corner_y = tile_swap(over_y[: cut * half]), chip_swap(over_x[cut * half :], 1)
+    corner = tile_swap(over_y)
     full = join(i32(odd), [over_y, over_x], (("mine", odds[1:]), ("other", ids)), planes, chips, full, small)
     last, nearby = list(range(far + far // 2, chips)), list(range(1, far))
     final = [chip_swap(send[s], s) for s in last]
-    x = gather([chip_swap(send[s], s) for s in nearby], nearby, cells, chips, x, small)
-    corner_x, corner_y, x = lax.optimization_barrier((corner_x, corner_y, x))
-    x = gather(final, last, cells, chips, x, LATE)
-    layout = (("other", odds[1 : cut + 1]), ("other", odds[cut + 1 :]))
-    full = join(i32(odd), [corner_x, corner_y], layout, planes, chips, full, small)
+    close = [chip_swap(send[s], s) for s in nearby]
+    x = gather([*final, *close], [*last, *nearby], cells, chips, x, LATE)
+    corner, x = lax.optimization_barrier((corner, x))
+    full = join(i32(odd), [corner], (("other", odds[1:]),), planes, chips, full, small)
     x, tails = x
 
     ring = jnp.concatenate([edges[0], inside, edges[1]])
@@ -435,7 +447,11 @@
     )
     home = [None] * chips
     pairs = list(range(chips // 2))
-    for i in reversed(pairs):
+    ready = [*solved, *others[:-1]]
+    begun = inverse(columns, ready, full, pairs[-1], planes, 0, None, True)
+    ended = inverse(columns, others[-1:], full, pairs[-1], planes, len(ready), begun)
+    home[2 * pairs[-1]], home[2 * pairs[-1] + 1] = ended
+    for i in reversed(pairs[:-1]):
         home[2 * i], home[2 * i + 1] = inverse(columns, solved + others, full, i, planes)
     first = [s for i in reversed(pairs[chips // 4 + 1 :]) for s in (2 * i + 1, 2 * i)]
     second = [s for i in reversed(pairs[: chips // 4 + 1]) for s in (2 * i + 1, 2 * i) if s]

time: 184 us -> 182 us (0.989); the launches traced: 180 us -> 181 us
  waiting for transfers between devices: 56.1 us -> 61.9 us
  starting transfers between devices: 62.5 us -> 59.2 us
    ppermute x20 -> x19, waiting for transfers between devices: 40.3 us -> 50.9 us  [local(): chip_swap = lambda v, s: lax.ppermute(v, 'wn', flip(s))]
    ppermute x2, waiting for transfers between devices: 5.56 us -> 2.79 us  [local(): down = lax.ppermute(spectral[:HALO], ('wn', 'tile'), backward)]
    ppermute x5, waiting for transfers between devices: 2.89 us -> 0.67 us  [local(): core_swap = lambda v: lax.ppermute(v, 'wn', [(i, i ^ 1) for i in range(wn)])]
    ppermute x2, waiting for transfers between devices: 3.9 us -> 5.93 us  [local(): up = lax.ppermute(spectral[rows - HALO:], ('wn', 'tile'), onward)]
    ppermute x1, waiting for transfers between devices: 2.02 us -> 0.01 us  [local(): lax.ppermute(inside[:HALO], 'tile', [((i + 1) % tiles, i) for i in range(...]
    ppermute x20 -> x19, starting transfers between devices: 50.8 us -> 49.3 us  [local(): chip_swap = lambda v, s: lax.ppermute(v, 'wn', flip(s))]
    pallas_call x4 -> x5, Pallas kernels: 9.73 us -> 11.1 us  [inverse(): pl.pallas_call(functools.partial(inverse_body, min(cells, 256), skip, bas...]
  transfers between devices with their start and end apart: 33 -> 32, of which waited for: 18 -> 16; matrix products, arithmetic and copies ran while one was open for 3% -> 2% of each run, Pallas kernels for 24% -> 25%
where the time goes in v4:
time: 182 us; the launch traced here: 181 us
  waiting for transfers between devices  61.9 us (34%)
  starting transfers between devices  59.2 us (33%)
  Pallas kernels  53.2 us (29%)
  local copies, waits for them, and re-layouts  3.83 us (2%)
  other arithmetic  2.79 us (2%)
    ppermute x19, waiting for transfers between devices, local(): chip_swap = lambda v, s: lax.ppermute(v, 'wn', flip(s))  50.9 us
    ppermute x19, starting transfers between devices, local(): chip_swap = lambda v, s: lax.ppermute(v, 'wn', flip(s))  49.3 us
    pallas_call x4, Pallas kernels, forward(): pl.pallas_call(forward_body, grid_spec=pltpu.PrefetchScalarGridSpec(num_s...  13 us
    pallas_call x5, Pallas kernels, inverse(): pl.pallas_call(functools.partial(inverse_body, min(cells, 256), skip, bas...  11.1 us
    pallas_call x2, Pallas kernels, sweep(): pl.pallas_call(sweep_body, grid=(modes // lanes,), in_specs=[pl.BlockSpec...  9.01 us
    pallas_call x4, Pallas kernels, place_pair(): pl.pallas_call(place_body, grid_spec=pltpu.PrefetchScalarGridSpec(num_sca...  8.65 us
    pallas_call x1, Pallas kernels, scale(): pl.pallas_call(scale_body, grid_spec=pltpu.PrefetchScalarGridSpec(num_sca...  6.04 us
    ppermute x2, waiting for transfers between devices, local(): up = lax.ppermute(spectral[rows - HALO:], ('wn', 'tile'), onward)  5.93 us
  transfers between devices with their start and end apart: 32, of which 16 were waited for; matrix products, arithmetic and copies ran while one was open for 2% of the time, Pallas kernels for 25%

profile of v4, /device:TPU:0, one launch (start us, length us, event | category | flops | bytes accessed | tf_op | source)
XLA Modules:
  0.0 181.2 jit_solution(10449222283932006086)
XLA Ops:
  0.0 1.0 constant_dynamic-slice_fusion
  1.0 3.1 %collective-permute-start = (bf16[64,2048]{1,0:T(8,128)(2,1)S(1)}, bf16[64,2048]{1,0:T(8,128)(2,1)S(1)}, u32[]{:S(2)}, u32[]{:S(2)}) collective-permute-start(bf16[64,2048]{1,0:T(8,128)(2,1)S(1)} %constant_dynamic-slice_fusion), channel_id=1, source_target_pairs={{0,8},{2,10},{4,12},{6,14},{8,0},{10,2},{12,4},{14,6},{16,24},{18,... | collective-permute-start | bytes 786440 | tf_op jit(solution)/shard_map/ppermute | solution.py:334
  4.1 2.6 %collective-permute-start.1 = (bf16[64,2048]{1,0:T(8,128)(2,1)S(1)}, bf16[64,2048]{1,0:T(8,128)(2,1)S(1)}, u32[]{:S(2)}, u32[]{:S(2)}) collective-permute-start(bf16[64,2048]{1,0:T(8,128)(2,1)S(1)} %constant_dynamic-slice_fusion), channel_id=1, source_target_pairs={{0,16},{2,18},{4,20},{6,22},{8,24},{10,26},{12,28},{14,30},{16,0},... | collective-permute-start | bytes 786440 | tf_op jit(solution)/shard_map/ppermute | solution.py:334
  6.7 1.7 collective-permute-start.3
  8.5 0.8 select_reduce_fusion.1
  9.3 0.8 subtract_convert_fusion
  10.3 1.6 collective-permute-start.5
  11.8 0.7 fusion.3
  12.6 6.0 %shard_map.65 = (bf16[1040,128]{1,0:T(8,128)(2,1)S(1)}, bf16[1040,128]{1,0:T(8,128)(2,1)}, bf16[1040,128]{1,0:T(8,128)(2,1)}, bf16[1040,128]{1,0:T(8,128)(2,1)},...) custom-call(s32[8]{0:T(128)S(1)} %stack.95.table, ...), custom_call_target="tpu_custom_call" | custom-call | flops 1048576 | bytes 6291456 | tf_op jit(solution)/shard_map/pallas_call | solution.py:56
  18.6 0.5 collective-permute-start.6
  19.2 6.3 %collective-permute-done.1.refs_2_ = bf16[64,2048]{1,0:T(8,128)(2,1)S(1)} collective-permute-done((bf16[64,2048]{1,0:T(8,128)(2,1)S(1)}, bf16[64,2048]{1,0:T(8,128)(2,1)S(1)}, u32[]{:S(2)}, u32[]{:S(2)}) %collective-permute-start.1) | collective-permute-done | bytes 262176 | tf_op jit(solution)/shard_map/ppermute | solution.py:334
  25.5 1.3 shard_map.64.refs_2_
  26.8 5.8 %collective-permute-start.9 = (bf16[1040,128]{1,0:T(8,128)(2,1)S(1)}, bf16[1040,128]{1,0:T(8,128)(2,1)S(1)}, u32[]{:S(2)}, u32[]{:S(2)}) collective-permute-start(bf16[1040,128]{1,0:T(8,128)(2,1)S(1)} %get-tuple-element.71), channel_id=1, source_target_pairs={{0,16},{2,18},{4,20},{6,22},{8,24},{10,26},{12,28},{14,30},{16,0},... | collective-permute-start | bytes 798728 | tf_op jit(solution)/shard_map/ppermute | solution.py:334
  32.7 1.0 collective-permute-start.10
  33.8 0.6 collective-permute-start.7
  34.3 1.5 collective-permute-start.8
  35.8 14.7 %collective-permute-done.9.refs_1_ = bf16[1040,128]{1,0:T(8,128)(2,1)S(1)} collective-permute-done((bf16[1040,128]{1,0:T(8,128)(2,1)S(1)}, bf16[1040,128]{1,0:T(8,128)(2,1)S(1)}, u32[]{:S(2)}, u32[]{:S(2)}) %collective-permute-start.9) | collective-permute-done | bytes 266272 | tf_op jit(solution)/shard_map/ppermute | solution.py:334
  50.6 5.5 %collective-permute-done.10.refs_2_ = bf16[1040,128]{1,0:T(8,128)(2,1)S(1)} collective-permute-done((bf16[1040,128]{1,0:T(8,128)(2,1)S(1)}, bf16[1040,128]{1,0:T(8,128)(2,1)S(1)}, u32[]{:S(2)}, u32[]{:S(2)}) %collective-permute-start.10) | collective-permute-done | bytes 266272 | tf_op jit(solution)/shard_map/ppermute | solution.py:334
  56.4 1.0 collective-permute-done.7.refs_0_
  57.4 0.9 copy-done.1
  58.3 1.4 collective-permute-start.12
  59.6 2.4 %collective-permute-start.13 = (bf16[1056,128]{1,0:T(8,128)(2,1)S(1)}, bf16[1056,128]{1,0:T(8,128)(2,1)}, u32[]{:S(2)}, u32[]{:S(2)}) collective-permute-start(bf16[1056,128]{1,0:T(8,128)(2,1)S(1)} %get-tuple-element.82), channel_id=1, source_target_pairs={{0,28},{2,30},{4,24},{6,26},{8,20},{10,22},{12,16},{14,18},{16,12}... | collective-permute-start | bytes 811016 | tf_op jit(solution)/shard_map/ppermute | solution.py:334
  62.1 1.5 collective-permute-start.14
  63.6 2.0 %collective-permute-start.16 = (bf16[1040,128]{1,0:T(8,128)(2,1)}, bf16[1040,128]{1,0:T(8,128)(2,1)}, u32[]{:S(2)}, u32[]{:S(2)}) collective-permute-start(bf16[1040,128]{1,0:T(8,128)(2,1)} %get-tuple-element.85), channel_id=1, source_target_pairs={{0,12},{2,14},{4,8},{6,10},{8,4},{10,6},{12,0},{14,2},{16,28},{18,... | collective-permute-start | bytes 798728 | tf_op jit(solution)/shard_map/ppermute | solution.py:334
  65.5 1.1 copy-done.2
  66.7 1.2 shard_map.68.refs_1_
  67.9 4.2 %collective-permute-done.14.refs_2_ = bf16[1040,128]{1,0:T(8,128)(2,1)} collective-permute-done((bf16[1040,128]{1,0:T(8,128)(2,1)}, bf16[1040,128]{1,0:T(8,128)(2,1)}, u32[]{:S(2)}, u32[]{:S(2)}) %collective-permute-start.14) | collective-permute-done | bytes 266272 | tf_op jit(solution)/shard_map/ppermute | solution.py:334
  72.0 1.5 collective-permute-start.11
  73.5 4.6 %collective-permute-done.15.refs_3_ = bf16[1040,128]{1,0:T(8,128)(2,1)} collective-permute-done((bf16[1040,128]{1,0:T(8,128)(2,1)}, bf16[1040,128]{1,0:T(8,128)(2,1)}, u32[]{:S(2)}, u32[]{:S(2)}) %collective-permute-start.15) | collective-permute-done | bytes 266272 | tf_op jit(solution)/shard_map/ppermute | solution.py:334
  78.1 5.6 %collective-permute-done.16.refs_4_ = bf16[1040,128]{1,0:T(8,128)(2,1)} collective-permute-done((bf16[1040,128]{1,0:T(8,128)(2,1)}, bf16[1040,128]{1,0:T(8,128)(2,1)}, u32[]{:S(2)}, u32[]{:S(2)}) %collective-permute-start.16) | collective-permute-done | bytes 266272 | tf_op jit(solution)/shard_map/ppermute | solution.py:334
  83.6 1.8 shard_map.67
  85.4 1.6 collective-permute-done.11.refs_0_
  87.1 0.9 shard_map.69.b_ref.refs_4_.refs_3_.refs_1_
  88.0 3.6 %shard_map.70 = f32[1024,512]{1,0:T(8,128)} custom-call(s32[1]{0:T(128)} %bitcast.19.table, bf16[1024,1024]{1,0:T(8,128)(2,1)S(1)} %get-tuple-element.93.x_ref, bf16[1024,2048]{1,0:T(8,128)(2,1)} %shard_map.69.b_ref.refs_4_.refs_3_.refs_1_), custom_call_target="tpu_custom_call" | custom-call | flops 1073741824 | bytes 5242880 | tf_op jit(solution)/shard_map/pallas_call | solution.py:198
  91.5 3.6 %shard_map.71 = f32[1024,512]{1,0:T(8,128)} custom-call(s32[1]{0:T(128)} %bitcast.18.table, bf16[1024,1024]{1,0:T(8,128)(2,1)S(1)} %get-tuple-element.93.x_ref, bf16[1024,2048]{1,0:T(8,128)(2,1)} %shard_map.69.b_ref.refs_4_.refs_3_.refs_1_), custom_call_target="tpu_custom_call" | custom-call | flops 1073741824 | bytes 5242880 | tf_op jit(solution)/shard_map/pallas_call | solution.py:198
  95.1 0.5 collective-permute-start.20
  96.0 2.9 %shard_map.72 = bf16[1024,512]{1,0:T(8,128)(2,1)S(1)} custom-call(s32[1]{0:T(128)} %bitcast.17.table, bf16[1024,1024]{1,0:T(8,128)(2,1)S(1)} %get-tuple-element.93.x_ref, bf16[1024,2048]{1,0:T(8,128)(2,1)} %shard_map.69.b_ref.refs_4_.refs_3_.refs_1_, f32[1024,512]{1,0:T(8,128)} %collective-permute-done.17.refs_0_), custom_call_target="tpu_custom_call" | custom-call | flops 1073741824 | bytes 5242880 | tf_op jit(solution)/shard_map/pallas_call | solution.py:198
  99.0 1.6 collective-permute-start.18
  100.6 0.5 collective-permute-start.19
  101.1 2.9 %shard_map.74 = bf16[1024,512]{1,0:T(8,128)(2,1)S(1)} custom-call(s32[1]{0:T(128)} %bitcast.24.table, bf16[1024,1024]{1,0:T(8,128)(2,1)S(1)} %get-tuple-element.93.x_ref, bf16[1024,2048]{1,0:T(8,128)(2,1)} %shard_map.69.b_ref.refs_4_.refs_3_.refs_1_, f32[1024,512]{1,0:T(8,128)} %collective-permute-done.20.refs_0_), custom_call_target="tpu_custom_call" | custom-call | flops 1073741824 | bytes 5242880 | tf_op jit(solution)/shard_map/pallas_call | solution.py:198
  104.1 1.6 collective-permute-start.21
  105.7 0.5 collective-permute-start.22
  106.3 4.8 %collective-permute-done.18.up_ref = bf16[3,128,512]{2,1,0:T(8,128)(2,1)S(1)} collective-permute-done((bf16[3,128,512]{2,1,0:T(8,128)(2,1)S(1)}, bf16[3,128,512]{2,1,0:T(8,128)(2,1)S(1)}, u32[]{:S(2)}, u32[]{:S(2)}) %collective-permute-start.18) | collective-permute-done | bytes 393248 | tf_op jit(solution)/shard_map/ppermute | solution.py:435
  111.0 1.6 collective-permute-done.19.down_ref
  112.9 4.5 %shard_map.73 = bf16[8,128,512]{2,1,0:T(8,128)(2,1)S(1)} custom-call(f32[1,512]{1,0:T(1,128)S(1)} %get-tuple-element.120.eigen_ref, f32[14,128,128]{2,1,0:T(8,128)S(1)} %broadcast_in_dim.44.fluid_ref, bf16[3,128,512]{2,1,0:T(8,128)(2,1)S(1)} %collective-permute-done.18.up_ref, bf16[8,128,512]{2,1,0:T(8,128)(2,1)S(1)} %bitcast.41, ...), custom_call_target="tpu_custom_call" | custom-call | flops 367001600 | bytes 3670016 | tf_op jit(solution)/shard_map/pallas_call | solution.py:250
  117.5 1.2 collective-permute-done.21.up_ref
  118.7 1.2 collective-permute-done.22.down_ref
  119.9 4.5 %shard_map.75 = bf16[8,128,512]{2,1,0:T(8,128)(2,1)S(1)} custom-call(f32[1,512]{1,0:T(1,128)S(1)} %get-tuple-element.119.eigen_ref, f32[14,128,128]{2,1,0:T(8,128)S(1)} %broadcast_in_dim.44.fluid_ref, bf16[3,128,512]{2,1,0:T(8,128)(2,1)S(1)} %collective-permute-done.21.up_ref, bf16[8,128,512]{2,1,0:T(8,128)(2,1)S(1)} %bitcast.42, ...), custom_call_target="tpu_custom_call" | custom-call | flops 367001600 | bytes 3670016 | tf_op jit(solution)/shard_map/pallas_call | solution.py:250
  124.6 2.2 %shard_map.79.refs_2_ = f32[1024,256]{1,0:T(8,128)S(1)} custom-call(s32[4]{0:T(128)S(1)} %pad_add_fusion.1.table, bf16[1024,512]{1,0:T(8,128)(2,1)S(1)} %bitcast.32, bf16[1024,512]{1,0:T(8,128)(2,1)S(1)} %bitcast.37, bf16[1024,512]{1,0:T(8,128)(2,1)S(1)} %collective-permute-done.23.refs_2_, bf16[1024,2048]{1,0:T(8,128)(2,1)S(1)} %copy-done), custom_call_target="tpu_custom_call" | custom-call | flops 1073741824 | bytes 5242880 | tf_op jit(solution)/shard_map/pallas_call | solution.py:306
  127.1 1.6 shard_map.80
  128.7 1.0 collective-permute-start.30
  129.7 3.2 %collective-permute-start.31 = (bf16[1024,128]{1,0:T(8,128)(2,1)S(1)}, bf16[1024,128]{1,0:T(8,128)(2,1)S(1)}, u32[]{:S(2)}, u32[]{:S(2)}) collective-permute-start(bf16[1024,128]{1,0:T(8,128)(2,1)S(1)} %get-tuple-element.112), channel_id=1, source_target_pairs={{0,28},{2,30},{4,24},{6,26},{8,20},{10,22},{12,16},{14,18},{16,12}... | collective-permute-start | bytes 786440 | tf_op jit(solution)/shard_map/ppermute | solution.py:334
  133.0 2.4 %shard_map.76 = (bf16[1024,128]{1,0:T(8,128)(2,1)S(1)}, bf16[1024,128]{1,0:T(8,128)(2,1)S(1)}) custom-call(s32[4]{0:T(128)S(1)} %pad_add_fusion.1.table, bf16[1024,512]{1,0:T(8,128)(2,1)S(1)} %bitcast.33, bf16[1024,512]{1,0:T(8,128)(2,1)S(1)} %bitcast.38, bf16[1024,512]{1,0:T(8,128)(2,1)S(1)} %collective-permute-done.23.refs_2_, ...), custom_call_target="tpu_custom_call" | custom-call | flops 1073741824 | bytes 5242880 | tf_op jit(solution)/shard_map/pallas_call | solution.py:306
  135.4 2.4 %shard_map.77 = (bf16[1024,128]{1,0:T(8,128)(2,1)S(1)}, bf16[1024,128]{1,0:T(8,128)(2,1)S(1)}) custom-call(s32[4]{0:T(128)S(1)} %pad_add_fusion.1.table, bf16[1024,512]{1,0:T(8,128)(2,1)S(1)} %bitcast.34, bf16[1024,512]{1,0:T(8,128)(2,1)S(1)} %bitcast.39, bf16[1024,512]{1,0:T(8,128)(2,1)S(1)} %collective-permute-done.23.refs_2_, ...), custom_call_target="tpu_custom_call" | custom-call | flops 1073741824 | bytes 5242880 | tf_op jit(solution)/shard_map/pallas_call | solution.py:306
  137.9 2.4 %shard_map.78 = (bf16[1024,128]{1,0:T(8,128)(2,1)S(1)}, bf16[1024,128]{1,0:T(8,128)(2,1)S(1)}) custom-call(s32[4]{0:T(128)S(1)} %pad_add_fusion.1.table, bf16[1024,512]{1,0:T(8,128)(2,1)S(1)} %bitcast.35, bf16[1024,512]{1,0:T(8,128)(2,1)S(1)} %bitcast.40, bf16[1024,512]{1,0:T(8,128)(2,1)S(1)} %collective-permute-done.23.refs_2_, ...), custom_call_target="tpu_custom_call" | custom-call | flops 1073741824 | bytes 5242880 | tf_op jit(solution)/shard_map/pallas_call | solution.py:306
  140.6 3.2 %collective-permute-start.26 = (bf16[1024,128]{1,0:T(8,128)(2,1)S(1)}, bf16[1024,128]{1,0:T(8,128)(2,1)S(1)}, u32[]{:S(2)}, u32[]{:S(2)}) collective-permute-start(bf16[1024,128]{1,0:T(8,128)(2,1)S(1)} %get-tuple-element.106), channel_id=1, source_target_pairs={{0,20},{2,22},{4,16},{6,18},{8,28},{10,30},{12,24},{14,26},{16,4},... | collective-permute-start | bytes 786440 | tf_op jit(solution)/shard_map/ppermute | solution.py:334
  143.9 18.4 %collective-permute-start.28 = (bf16[1024,128]{1,0:T(8,128)(2,1)S(1)}, bf16[1024,128]{1,0:T(8,128)(2,1)S(1)}, u32[]{:S(2)}, u32[]{:S(2)}) collective-permute-start(bf16[1024,128]{1,0:T(8,128)(2,1)S(1)} %get-tuple-element.108), channel_id=1, source_target_pairs={{0,12},{2,14},{4,8},{6,10},{8,4},{10,6},{12,0},{14,2},{16,28},{18,... | collective-permute-start | bytes 786440 | tf_op jit(solution)/shard_map/ppermute | solution.py:334
  162.2 1.1 collective-permute-start.29
  163.6 2.2 %shard_map.81.refs_2_ = f32[128,64,128]{2,1,0:T(8,128)} custom-call(s32[2]{0:T(128)S(1)} %pad_add_fusion.4.table, bf16[1024,128]{1,0:T(8,128)(2,1)S(1)} %collective-permute-done.30.refs_0_, bf16[1024,128]{1,0:T(8,128)(2,1)S(1)} %collective-permute-done.31.refs_1_), custom_call_target="tpu_custom_call" | custom-call | flops 262144 | bytes 1572864 | tf_op jit(solution)/shard_map/pallas_call | solution.py:94
  165.7 7.2 %collective-permute-done.29.refs_1_ = bf16[1024,128]{1,0:T(8,128)(2,1)S(1)} collective-permute-done((bf16[1024,128]{1,0:T(8,128)(2,1)S(1)}, bf16[1024,128]{1,0:T(8,128)(2,1)S(1)}, u32[]{:S(2)}, u32[]{:S(2)}) %collective-permute-start.29) | collective-permute-done | bytes 262176 | tf_op jit(solution)/shard_map/ppermute | solution.py:334
  172.9 2.2 %shard_map.82.refs_2_ = f32[128,64,128]{2,1,0:T(8,128)} custom-call(s32[2]{0:T(128)S(1)} %pad_add_fusion.3.table, bf16[1024,128]{1,0:T(8,128)(2,1)S(1)} %get-tuple-element.109.refs_0_, bf16[1024,128]{1,0:T(8,128)(2,1)S(1)} %collective-permute-done.29.refs_1_, f32[128,64,128]{2,1,0:T(8,128)} %shard_map.81.refs_2_), custom_call_target="tpu_custom_call", output_to_operand_aliasing={{}: (3, {})} | custom-call | flops 262144 | bytes 1572864 | tf_op jit(solution)/shard_map/pallas_call | solution.py:94
  175.1 2.2 %shard_map.83.refs_2_ = f32[128,64,128]{2,1,0:T(8,128)} custom-call(s32[2]{0:T(128)S(1)} %get-tuple-element.127.table, bf16[1024,128]{1,0:T(8,128)(2,1)S(1)} %collective-permute-done.27.refs_0_, bf16[1024,128]{1,0:T(8,128)(2,1)S(1)} %collective-permute-done.28.refs_1_, f32[128,64,128]{2,1,0:T(8,128)} %shard_map.82.refs_2_), custom_call_target="tpu_custom_call", output_to_operand_aliasing={{}: (3, {})} | custom-call | flops 262144 | bytes 1572864 | tf_op jit(solution)/shard_map/pallas_call | solution.py:94
  177.3 1.8 collective-permute-done.26.refs_1_
  179.1 2.2 %shard_map.84 = f32[128,64,128]{2,1,0:T(8,128)} custom-call(s32[2]{0:T(128)S(1)} %get-tuple-element.126.table, bf16[1024,128]{1,0:T(8,128)(2,1)S(1)} %collective-permute-done.25.refs_0_, bf16[1024,128]{1,0:T(8,128)(2,1)S(1)} %collective-permute-done.26.refs_1_, f32[128,64,128]{2,1,0:T(8,128)} %shard_map.83.refs_2_), custom_call_target="tpu_custom_call", output_to_operand_aliasing={{}: (3, {})} | custom-call | flops 262144 | bytes 1572864 | tf_op jit(solution)/shard_map/pallas_call | solution.py:94
  (58 shorter events, 2.8 us)
Async XLA Ops:
  0.0 25.5 %copy-start.3 = (bf16[128,2048]{1,0:T(8,128)(2,1)S(1)}, bf16[128,2048]{1,0:T(8,128)(2,1)}, u32[]{:S(2)}) copy-start(bf16[128,2048]{1,0:T(8,128)(2,1)} %refs_0_.1) | copy-start | bytes 1572868
  1.0 17.6 %collective-permute-start = (bf16[64,2048]{1,0:T(8,128)(2,1)S(1)}, bf16[64,2048]{1,0:T(8,128)(2,1)S(1)}, u32[]{:S(2)}, u32[]{:S(2)}) collective-permute-start(bf16[64,2048]{1,0:T(8,128)(2,1)S(1)} %constant_dynamic-slice_fusion), channel_id=1, source_target_pairs={{0,8},{2,10},{4,12},{6,14},{8,0},{10,2},{12,4},{14,6},{16,24},{18,... | collective-permute-start | bytes 786440 | tf_op jit(solution)/shard_map/ppermute | solution.py:334
  4.1 21.4 %collective-permute-start.1 = (bf16[64,2048]{1,0:T(8,128)(2,1)S(1)}, bf16[64,2048]{1,0:T(8,128)(2,1)S(1)}, u32[]{:S(2)}, u32[]{:S(2)}) collective-permute-start(bf16[64,2048]{1,0:T(8,128)(2,1)S(1)} %constant_dynamic-slice_fusion), channel_id=1, source_target_pairs={{0,16},{2,18},{4,20},{6,22},{8,24},{10,26},{12,28},{14,30},{16,0},... | collective-permute-start | bytes 786440 | tf_op jit(solution)/shard_map/ppermute | solution.py:334
  6.7 18.8 %collective-permute-start.2 = (bf16[64,2048]{1,0:T(8,128)(2,1)S(1)}, bf16[64,2048]{1,0:T(8,128)(2,1)S(1)}, u32[]{:S(2)}, u32[]{:S(2)}) collective-permute-start(bf16[64,2048]{1,0:T(8,128)(2,1)S(1)} %constant_dynamic-slice_fusion), channel_id=1, source_target_pairs={{0,24},{2,26},{4,28},{6,30},{8,16},{10,18},{12,20},{14,22},{16,8},... | collective-permute-start | bytes 786440 | tf_op jit(solution)/shard_map/ppermute | solution.py:334
  6.7 18.8 %collective-permute-start.3 = (bf16[128,2048]{1,0:T(8,128)(2,1)}, bf16[128,2048]{1,0:T(8,128)(2,1)S(1)}, u32[]{:S(2)}, u32[]{:S(2)}) collective-permute-start(bf16[128,2048]{1,0:T(8,128)(2,1)} %refs_0_.1), channel_id=1, source_target_pairs={{0,4},{2,6},{4,0},{6,2},{8,12},{10,14},{12,8},{14,10},{16,20},{18,... | collective-permute-start | bytes 1572872 | tf_op jit(solution)/shard_map/ppermute | solution.py:334
  8.5 1.8 %collective-permute-start.4 = (f32[128]{0:T(128)}, f32[128]{0:T(128)S(1)}, u32[]{:S(2)}, u32[]{:S(2)}) collective-permute-start(f32[128]{0:T(128)} %param.8), channel_id=1, source_target_pairs={{0,2},{2,0},{4,6},{6,4},{8,10},{10,8},{12,14},{14,12},{16,18},{18,... | collective-permute-start | bytes 1544 | tf_op jit(solution)/shard_map/ppermute | solution.py:335
  10.3 16.5 %collective-permute-start.5 = (f32[3,128]{1,0:T(4,128)S(1)}, f32[3,128]{1,0:T(4,128)S(1)}, u32[]{:S(2)}, u32[]{:S(2)}) collective-permute-start(f32[3,128]{1,0:T(4,128)S(1)} %get-tuple-element.118), channel_id=1, source_target_pairs={{0,1},{1,0},{2,3},{3,2},{4,5},{5,4},{6,7},{7,6},{8,9},{9,8},{10,11... | collective-permute-start | bytes 4616 | tf_op jit(solution)/shard_map/ppermute | solution.py:369
  18.6 8.2 %collective-permute-start.6 = (f32[3,128]{1,0:T(4,128)S(1)}, f32[3,128]{1,0:T(4,128)S(1)}, u32[]{:S(2)}, u32[]{:S(2)}) collective-permute-start(f32[3,128]{1,0:T(4,128)S(1)} %get-tuple-element.117), channel_id=1, source_target_pairs={{1,0},{0,1},{3,2},{2,3},{5,4},{4,5},{7,6},{6,7},{9,8},{8,9},{11,10... | collective-permute-start | bytes 4616 | tf_op jit(solution)/shard_map/ppermute | solution.py:370
  26.8 23.7 %collective-permute-start.9 = (bf16[1040,128]{1,0:T(8,128)(2,1)S(1)}, bf16[1040,128]{1,0:T(8,128)(2,1)S(1)}, u32[]{:S(2)}, u32[]{:S(2)}) collective-permute-start(bf16[1040,128]{1,0:T(8,128)(2,1)S(1)} %get-tuple-element.71), channel_id=1, source_target_pairs={{0,16},{2,18},{4,20},{6,22},{8,24},{10,26},{12,28},{14,30},{16,0},... | collective-permute-start | bytes 798728 | tf_op jit(solution)/shard_map/ppermute | solution.py:334
  32.7 23.4 %collective-permute-start.10 = (bf16[1040,128]{1,0:T(8,128)(2,1)S(1)}, bf16[1040,128]{1,0:T(8,128)(2,1)S(1)}, u32[]{:S(2)}, u32[]{:S(2)}) collective-permute-start(bf16[1040,128]{1,0:T(8,128)(2,1)S(1)} %get-tuple-element.72), channel_id=1, source_target_pairs={{0,20},{2,22},{4,16},{6,18},{8,28},{10,30},{12,24},{14,26},{16,4},... | collective-permute-start | bytes 798728 | tf_op jit(solution)/shard_map/ppermute | solution.py:334
  33.8 23.6 %collective-permute-start.7 = (bf16[192,2048]{1,0:T(8,128)(2,1)S(1)}, bf16[192,2048]{1,0:T(8,128)(2,1)S(1)}, u32[]{:S(2)}, u32[]{:S(2)}) collective-permute-start(bf16[192,2048]{1,0:T(8,128)(2,1)S(1)} %constant_dynamic-update-slice_fusion), channel_id=1, source_target_pairs={{0,4},{2,6},{4,0},{6,2},{8,12},{10,14},{12,8},{14,10},{16,20},{18,... | collective-permute-start | bytes 2359304 | tf_op jit(solution)/shard_map/ppermute | solution.py:334
  34.3 23.1 %collective-permute-start.8 = (bf16[192,2048]{1,0:T(8,128)(2,1)S(1)}, bf16[192,2048]{1,0:T(8,128)(2,1)S(1)}, u32[]{:S(2)}, u32[]{:S(2)}) collective-permute-start(bf16[192,2048]{1,0:T(8,128)(2,1)S(1)} %constant_dynamic-update-slice_fusion), channel_id=1, source_target_pairs={{0,1},{1,0},{2,3},{3,2},{4,5},{5,4},{6,7},{7,6},{8,9},{9,8},{10,11... | collective-permute-start | bytes 2359304 | tf_op jit(solution)/shard_map/ppermute | solution.py:336
  57.4 0.9 copy-start.1
  58.3 25.4 %collective-permute-start.12 = (bf16[1056,128]{1,0:T(8,128)(2,1)S(1)}, bf16[1056,128]{1,0:T(8,128)(2,1)}, u32[]{:S(2)}, u32[]{:S(2)}) collective-permute-start(bf16[1056,128]{1,0:T(8,128)(2,1)S(1)} %get-tuple-element.81), channel_id=1, source_target_pairs={{0,24},{2,26},{4,28},{6,30},{8,16},{10,18},{12,20},{14,22},{16,8},... | collective-permute-start | bytes 811016 | tf_op jit(solution)/shard_map/ppermute | solution.py:334
  59.6 24.0 %collective-permute-start.13 = (bf16[1056,128]{1,0:T(8,128)(2,1)S(1)}, bf16[1056,128]{1,0:T(8,128)(2,1)}, u32[]{:S(2)}, u32[]{:S(2)}) collective-permute-start(bf16[1056,128]{1,0:T(8,128)(2,1)S(1)} %get-tuple-element.82), channel_id=1, source_target_pairs={{0,28},{2,30},{4,24},{6,26},{8,20},{10,22},{12,16},{14,18},{16,12}... | collective-permute-start | bytes 811016 | tf_op jit(solution)/shard_map/ppermute | solution.py:334
  62.1 10.0 %collective-permute-start.14 = (bf16[1040,128]{1,0:T(8,128)(2,1)}, bf16[1040,128]{1,0:T(8,128)(2,1)}, u32[]{:S(2)}, u32[]{:S(2)}) collective-permute-start(bf16[1040,128]{1,0:T(8,128)(2,1)} %get-tuple-element.83), channel_id=1, source_target_pairs={{0,4},{2,6},{4,0},{6,2},{8,12},{10,14},{12,8},{14,10},{16,20},{18,... | collective-permute-start | bytes 798728 | tf_op jit(solution)/shard_map/ppermute | solution.py:334
  63.6 14.5 %collective-permute-start.15 = (bf16[1040,128]{1,0:T(8,128)(2,1)}, bf16[1040,128]{1,0:T(8,128)(2,1)}, u32[]{:S(2)}, u32[]{:S(2)}) collective-permute-start(bf16[1040,128]{1,0:T(8,128)(2,1)} %get-tuple-element.84), channel_id=1, source_target_pairs={{0,8},{2,10},{4,12},{6,14},{8,0},{10,2},{12,4},{14,6},{16,24},{18,... | collective-permute-start | bytes 798728 | tf_op jit(solution)/shard_map/ppermute | solution.py:334
  63.6 20.1 %collective-permute-start.16 = (bf16[1040,128]{1,0:T(8,128)(2,1)}, bf16[1040,128]{1,0:T(8,128)(2,1)}, u32[]{:S(2)}, u32[]{:S(2)}) collective-permute-start(bf16[1040,128]{1,0:T(8,128)(2,1)} %get-tuple-element.85), channel_id=1, source_target_pairs={{0,12},{2,14},{4,8},{6,10},{8,4},{10,6},{12,0},{14,2},{16,28},{18,... | collective-permute-start | bytes 798728 | tf_op jit(solution)/shard_map/ppermute | solution.py:334
  65.5 1.1 copy-start.2
  72.0 15.0 %collective-permute-start.11 = (bf16[192,2048]{1,0:T(8,128)(2,1)S(1)}, bf16[192,2048]{1,0:T(8,128)(2,1)S(1)}, u32[]{:S(2)}, u32[]{:S(2)}) collective-permute-start(bf16[192,2048]{1,0:T(8,128)(2,1)S(1)} %collective-permute-done.7.refs_0_), channel_id=1, source_target_pairs={{0,1},{1,0},{2,3},{3,2},{4,5},{5,4},{6,7},{7,6},{8,9},{9,8},{10,11... | collective-permute-start | bytes 2359304 | tf_op jit(solution)/shard_map/ppermute | solution.py:336
  91.5 4.5 %collective-permute-start.17 = (f32[1024,512]{1,0:T(8,128)}, f32[1024,512]{1,0:T(8,128)}, u32[]{:S(2)}, u32[]{:S(2)}) collective-permute-start(f32[1024,512]{1,0:T(8,128)} %shard_map.70), channel_id=1, source_target_pairs={{0,2},{2,0},{4,6},{6,4},{8,10},{10,8},{12,14},{14,12},{16,18},{18,... | collective-permute-start | bytes 6291464 | tf_op jit(solution)/shard_map/ppermute | solution.py:335
  95.1 6.0 %collective-permute-start.20 = (f32[1024,512]{1,0:T(8,128)}, f32[1024,512]{1,0:T(8,128)}, u32[]{:S(2)}, u32[]{:S(2)}) collective-permute-start(f32[1024,512]{1,0:T(8,128)} %shard_map.71), channel_id=1, source_target_pairs={{0,2},{2,0},{4,6},{6,4},{8,10},{10,8},{12,14},{14,12},{16,18},{18,... | collective-permute-start | bytes 6291464 | tf_op jit(solution)/shard_map/ppermute | solution.py:335
  99.0 12.0 %collective-permute-start.18 = (bf16[3,128,512]{2,1,0:T(8,128)(2,1)S(1)}, bf16[3,128,512]{2,1,0:T(8,128)(2,1)S(1)}, u32[]{:S(2)}, u32[]{:S(2)}) collective-permute-start(bf16[3,128,512]{2,1,0:T(8,128)(2,1)S(1)} %bitcast.45), channel_id=1, source_target_pairs={{0,4},{2,6},{4,12},{6,14},{12,8},{14,10},{8,16},{10,18},{16,20},{1... | collective-permute-start | bytes 1179656 | tf_op jit(solution)/shard_map/ppermute | solution.py:435
  100.6 12.0 %collective-permute-start.19 = (bf16[3,128,512]{2,1,0:T(8,128)(2,1)S(1)}, bf16[3,128,512]{2,1,0:T(8,128)(2,1)S(1)}, u32[]{:S(2)}, u32[]{:S(2)}) collective-permute-start(bf16[3,128,512]{2,1,0:T(8,128)(2,1)S(1)} %bitcast.43), channel_id=1, source_target_pairs={{4,0},{6,2},{12,4},{14,6},{8,12},{10,14},{16,8},{18,10},{20,16},{2... | collective-permute-start | bytes 1179656 | tf_op jit(solution)/shard_map/ppermute | solution.py:436
  104.1 14.6 %collective-permute-start.21 = (bf16[3,128,512]{2,1,0:T(8,128)(2,1)S(1)}, bf16[3,128,512]{2,1,0:T(8,128)(2,1)S(1)}, u32[]{:S(2)}, u32[]{:S(2)}) collective-permute-start(bf16[3,128,512]{2,1,0:T(8,128)(2,1)S(1)} %bitcast.46), channel_id=1, source_target_pairs={{0,4},{2,6},{4,12},{6,14},{12,8},{14,10},{8,16},{10,18},{16,20},{1... | collective-permute-start | bytes 1179656 | tf_op jit(solution)/shard_map/ppermute | solution.py:435
  105.7 14.2 %collective-permute-start.22 = (bf16[3,128,512]{2,1,0:T(8,128)(2,1)S(1)}, bf16[3,128,512]{2,1,0:T(8,128)(2,1)S(1)}, u32[]{:S(2)}, u32[]{:S(2)}) collective-permute-start(bf16[3,128,512]{2,1,0:T(8,128)(2,1)S(1)} %bitcast.44), channel_id=1, source_target_pairs={{4,0},{6,2},{12,4},{14,6},{8,12},{10,14},{16,8},{18,10},{20,16},{2... | collective-permute-start | bytes 1179656 | tf_op jit(solution)/shard_map/ppermute | solution.py:436
  112.6 12.0 %copy-start = (bf16[1024,2048]{1,0:T(8,128)(2,1)S(1)}, bf16[1024,2048]{1,0:T(8,128)(2,1)}, u32[]{:S(2)}) copy-start(bf16[1024,2048]{1,0:T(8,128)(2,1)} %shard_map.69.b_ref.refs_4_.refs_3_.refs_1_) | copy-start | bytes 12582916
  117.4 7.2 %collective-permute-start.23 = (bf16[1024,512]{1,0:T(8,128)(2,1)S(1)}, bf16[1024,512]{1,0:T(8,128)(2,1)S(1)}, u32[]{:S(2)}, u32[]{:S(2)}) collective-permute-start(bf16[1024,512]{1,0:T(8,128)(2,1)S(1)} %bitcast.31), channel_id=1, source_target_pairs={{0,2},{2,0},{4,6},{6,4},{8,10},{10,8},{12,14},{14,12},{16,18},{18,... | collective-permute-start | bytes 3145736 | tf_op jit(solution)/shard_map/ppermute | solution.py:335
  124.4 2.7 %collective-permute-start.24 = (bf16[1024,512]{1,0:T(8,128)(2,1)S(1)}, bf16[1024,512]{1,0:T(8,128)(2,1)S(1)}, u32[]{:S(2)}, u32[]{:S(2)}) collective-permute-start(bf16[1024,512]{1,0:T(8,128)(2,1)S(1)} %bitcast.36), channel_id=1, source_target_pairs={{0,2},{2,0},{4,6},{6,4},{8,10},{10,8},{12,14},{14,12},{16,18},{18,... | collective-permute-start | bytes 3145736 | tf_op jit(solution)/shard_map/ppermute | solution.py:335
  128.7 15.1 %collective-permute-start.30 = (bf16[1024,128]{1,0:T(8,128)(2,1)S(1)}, bf16[1024,128]{1,0:T(8,128)(2,1)S(1)}, u32[]{:S(2)}, u32[]{:S(2)}) collective-permute-start(bf16[1024,128]{1,0:T(8,128)(2,1)S(1)} %get-tuple-element.111), channel_id=1, source_target_pairs={{0,24},{2,26},{4,28},{6,30},{8,16},{10,18},{12,20},{14,22},{16,8},... | collective-permute-start | bytes 786440 | tf_op jit(solution)/shard_map/ppermute | solution.py:334
  129.7 32.5 %collective-permute-start.31 = (bf16[1024,128]{1,0:T(8,128)(2,1)S(1)}, bf16[1024,128]{1,0:T(8,128)(2,1)S(1)}, u32[]{:S(2)}, u32[]{:S(2)}) collective-permute-start(bf16[1024,128]{1,0:T(8,128)(2,1)S(1)} %get-tuple-element.112), channel_id=1, source_target_pairs={{0,28},{2,30},{4,24},{6,26},{8,20},{10,22},{12,16},{14,18},{16,12}... | collective-permute-start | bytes 786440 | tf_op jit(solution)/shard_map/ppermute | solution.py:334
  140.3 37.0 %collective-permute-start.25 = (bf16[1024,128]{1,0:T(8,128)(2,1)S(1)}, bf16[1024,128]{1,0:T(8,128)(2,1)S(1)}, u32[]{:S(2)}, u32[]{:S(2)}) collective-permute-start(bf16[1024,128]{1,0:T(8,128)(2,1)S(1)} %get-tuple-element.105), channel_id=1, source_target_pairs={{0,16},{2,18},{4,20},{6,22},{8,24},{10,26},{12,28},{14,30},{16,0},... | collective-permute-start | bytes 786440 | tf_op jit(solution)/shard_map/ppermute | solution.py:334
  140.6 38.4 %collective-permute-start.26 = (bf16[1024,128]{1,0:T(8,128)(2,1)S(1)}, bf16[1024,128]{1,0:T(8,128)(2,1)S(1)}, u32[]{:S(2)}, u32[]{:S(2)}) collective-permute-start(bf16[1024,128]{1,0:T(8,128)(2,1)S(1)} %get-tuple-element.106), channel_id=1, source_target_pairs={{0,20},{2,22},{4,16},{6,18},{8,28},{10,30},{12,24},{14,26},{16,4},... | collective-permute-start | bytes 786440 | tf_op jit(solution)/shard_map/ppermute | solution.py:334
  143.9 31.3 %collective-permute-start.27 = (bf16[1024,128]{1,0:T(8,128)(2,1)S(1)}, bf16[1024,128]{1,0:T(8,128)(2,1)S(1)}, u32[]{:S(2)}, u32[]{:S(2)}) collective-permute-start(bf16[1024,128]{1,0:T(8,128)(2,1)S(1)} %get-tuple-element.107), channel_id=1, source_target_pairs={{0,8},{2,10},{4,12},{6,14},{8,0},{10,2},{12,4},{14,6},{16,24},{18,... | collective-permute-start | bytes 786440 | tf_op jit(solution)/shard_map/ppermute | solution.py:334
  143.9 31.2 %collective-permute-start.28 = (bf16[1024,128]{1,0:T(8,128)(2,1)S(1)}, bf16[1024,128]{1,0:T(8,128)(2,1)S(1)}, u32[]{:S(2)}, u32[]{:S(2)}) collective-permute-start(bf16[1024,128]{1,0:T(8,128)(2,1)S(1)} %get-tuple-element.108), channel_id=1, source_target_pairs={{0,12},{2,14},{4,8},{6,10},{8,4},{10,6},{12,0},{14,2},{16,28},{18,... | collective-permute-start | bytes 786440 | tf_op jit(solution)/shard_map/ppermute | solution.py:334
  162.2 10.7 %collective-permute-start.29 = (bf16[1024,128]{1,0:T(8,128)(2,1)S(1)}, bf16[1024,128]{1,0:T(8,128)(2,1)S(1)}, u32[]{:S(2)}, u32[]{:S(2)}) collective-permute-start(bf16[1024,128]{1,0:T(8,128)(2,1)S(1)} %get-tuple-element.110), channel_id=1, source_target_pairs={{0,4},{2,6},{4,0},{6,2},{8,12},{10,14},{12,8},{14,10},{16,20},{18,... | collective-permute-start | bytes 786440 | tf_op jit(solution)/shard_map/ppermute | solution.py:334

commit v5 on v4

--- a/solution.py
+++ b/solution.py
@@ -449,19 +449,13 @@
     pairs = list(range(chips // 2))
     ready = [*solved, *others[:-1]]
     begun = inverse(columns, ready, full, pairs[-1], planes, 0, None, True)
-    ended = inverse(columns, others[-1:], full, pairs[-1], planes, len(ready), begun)
-    home[2 * pairs[-1]], home[2 * pairs[-1] + 1] = ended
-    for i in reversed(pairs[:-1]):
-        home[2 * i], home[2 * i + 1] = inverse(columns, solved + others, full, i, planes)
-    first = [s for i in reversed(pairs[chips // 4 + 1 :]) for s in (2 * i + 1, 2 * i)]
-    second = [s for i in reversed(pairs[: chips // 4 + 1]) for s in (2 * i + 1, 2 * i) if s]
-    held = [home[s] for s in second]
-    sign = core_swap(home[first[0]][:16])
-    for s in first:
-        home[s] = chip_swap(home[s], s)
-    sign, held = lax.optimization_barrier((sign, held))
-    for s, v in zip(second, held):
-        home[s] = chip_swap(v, s)
+    for i in reversed(pairs):
+        if i == pairs[-1]:
+            a, b = inverse(columns, others[-1:], full, i, planes, len(ready), begun)
+        else:
+            a, b = inverse(columns, solved + others, full, i, planes)
+        columns, a, b = lax.optimization_barrier((columns, a, b))
+        home[2 * i], home[2 * i + 1] = a if i == 0 else chip_swap(a, 2 * i), chip_swap(b, 2 * i + 1)
 
     out = None
     for i in [*pairs[chips // 4 + 1 :], *pairs[: chips // 4 + 1]]:

time: 182 us -> 182 us (level)
  no operation moved by 1% of the time
where the time goes in v5:
time: 182 us; the launch traced here: 181 us
  waiting for transfers between devices  61.9 us (34%)
  starting transfers between devices  59.2 us (33%)
  Pallas kernels  53.2 us (29%)
  local copies, waits for them, and re-layouts  3.83 us (2%)
  other arithmetic  2.79 us (2%)
    ppermute x19, waiting for transfers between devices, local(): chip_swap = lambda v, s: lax.ppermute(v, 'wn', flip(s))  50.9 us
    ppermute x19, starting transfers between devices, local(): chip_swap = lambda v, s: lax.ppermute(v, 'wn', flip(s))  49.3 us
    pallas_call x4, Pallas kernels, forward(): pl.pallas_call(forward_body, grid_spec=pltpu.PrefetchScalarGridSpec(num_s...  13 us
    pallas_call x5, Pallas kernels, inverse(): pl.pallas_call(functools.partial(inverse_body, min(cells, 256), skip, bas...  11.1 us
    pallas_call x2, Pallas kernels, sweep(): pl.pallas_call(sweep_body, grid=(modes // lanes,), in_specs=[pl.BlockSpec...  9.01 us
    pallas_call x4, Pallas kernels, place_pair(): pl.pallas_call(place_body, grid_spec=pltpu.PrefetchScalarGridSpec(num_sca...  8.67 us
    pallas_call x1, Pallas kernels, scale(): pl.pallas_call(scale_body, grid_spec=pltpu.PrefetchScalarGridSpec(num_sca...  6.04 us
    ppermute x2, waiting for transfers between devices, local(): up = lax.ppermute(spectral[rows - HALO:], ('wn', 'tile'), onward)  5.92 us
  transfers between devices with their start and end apart: 32, of which 16 were waited for; matrix products, arithmetic and copies ran while one was open for 2% of the time, Pallas kernels for 25%

profile of v5, /device:TPU:0, one launch (start us, length us, event | category | flops | bytes accessed | tf_op | source)
XLA Modules:
  0.0 181.2 jit_solution(10934758167279132307)
XLA Ops:
  0.0 1.0 constant_dynamic-slice_fusion
  1.0 3.1 %collective-permute-start = (bf16[64,2048]{1,0:T(8,128)(2,1)S(1)}, bf16[64,2048]{1,0:T(8,128)(2,1)S(1)}, u32[]{:S(2)}, u32[]{:S(2)}) collective-permute-start(bf16[64,2048]{1,0:T(8,128)(2,1)S(1)} %constant_dynamic-slice_fusion), channel_id=1, source_target_pairs={{0,8},{2,10},{4,12},{6,14},{8,0},{10,2},{12,4},{14,6},{16,24},{18,... | collective-permute-start | bytes 786440 | tf_op jit(solution)/shard_map/ppermute | solution.py:334
  4.1 2.6 %collective-permute-start.1 = (bf16[64,2048]{1,0:T(8,128)(2,1)S(1)}, bf16[64,2048]{1,0:T(8,128)(2,1)S(1)}, u32[]{:S(2)}, u32[]{:S(2)}) collective-permute-start(bf16[64,2048]{1,0:T(8,128)(2,1)S(1)} %constant_dynamic-slice_fusion), channel_id=1, source_target_pairs={{0,16},{2,18},{4,20},{6,22},{8,24},{10,26},{12,28},{14,30},{16,0},... | collective-permute-start | bytes 786440 | tf_op jit(solution)/shard_map/ppermute | solution.py:334
  6.7 1.7 collective-permute-start.3
  8.5 0.8 select_reduce_fusion.1
  9.3 0.8 subtract_convert_fusion
  10.3 1.6 collective-permute-start.5
  11.8 0.7 fusion.3
  12.6 6.0 %shard_map.65 = (bf16[1040,128]{1,0:T(8,128)(2,1)S(1)}, bf16[1040,128]{1,0:T(8,128)(2,1)}, bf16[1040,128]{1,0:T(8,128)(2,1)}, bf16[1040,128]{1,0:T(8,128)(2,1)},...) custom-call(s32[8]{0:T(128)S(1)} %stack.95.table, ...), custom_call_target="tpu_custom_call" | custom-call | flops 1048576 | bytes 6291456 | tf_op jit(solution)/shard_map/pallas_call | solution.py:56
  18.6 0.5 collective-permute-start.6
  19.2 6.3 %collective-permute-done.1.refs_2_ = bf16[64,2048]{1,0:T(8,128)(2,1)S(1)} collective-permute-done((bf16[64,2048]{1,0:T(8,128)(2,1)S(1)}, bf16[64,2048]{1,0:T(8,128)(2,1)S(1)}, u32[]{:S(2)}, u32[]{:S(2)}) %collective-permute-start.1) | collective-permute-done | bytes 262176 | tf_op jit(solution)/shard_map/ppermute | solution.py:334
  25.5 1.3 shard_map.64.refs_2_
  26.8 5.8 %collective-permute-start.9 = (bf16[1040,128]{1,0:T(8,128)(2,1)S(1)}, bf16[1040,128]{1,0:T(8,128)(2,1)S(1)}, u32[]{:S(2)}, u32[]{:S(2)}) collective-permute-start(bf16[1040,128]{1,0:T(8,128)(2,1)S(1)} %get-tuple-element.77), channel_id=1, source_target_pairs={{0,16},{2,18},{4,20},{6,22},{8,24},{10,26},{12,28},{14,30},{16,0},... | collective-permute-start | bytes 798728 | tf_op jit(solution)/shard_map/ppermute | solution.py:334
  32.7 1.0 collective-permute-start.10
  33.8 0.6 collective-permute-start.7
  34.3 1.5 collective-permute-start.8
  35.8 14.7 %collective-permute-done.9.refs_1_ = bf16[1040,128]{1,0:T(8,128)(2,1)S(1)} collective-permute-done((bf16[1040,128]{1,0:T(8,128)(2,1)S(1)}, bf16[1040,128]{1,0:T(8,128)(2,1)S(1)}, u32[]{:S(2)}, u32[]{:S(2)}) %collective-permute-start.9) | collective-permute-done | bytes 266272 | tf_op jit(solution)/shard_map/ppermute | solution.py:334
  50.6 5.5 %collective-permute-done.10.refs_2_ = bf16[1040,128]{1,0:T(8,128)(2,1)S(1)} collective-permute-done((bf16[1040,128]{1,0:T(8,128)(2,1)S(1)}, bf16[1040,128]{1,0:T(8,128)(2,1)S(1)}, u32[]{:S(2)}, u32[]{:S(2)}) %collective-permute-start.10) | collective-permute-done | bytes 266272 | tf_op jit(solution)/shard_map/ppermute | solution.py:334
  56.4 1.0 collective-permute-done.7.refs_0_
  57.4 0.9 copy-done.1
  58.3 1.4 collective-permute-start.12
  59.6 2.4 %collective-permute-start.13 = (bf16[1056,128]{1,0:T(8,128)(2,1)S(1)}, bf16[1056,128]{1,0:T(8,128)(2,1)}, u32[]{:S(2)}, u32[]{:S(2)}) collective-permute-start(bf16[1056,128]{1,0:T(8,128)(2,1)S(1)} %get-tuple-element.88), channel_id=1, source_target_pairs={{0,28},{2,30},{4,24},{6,26},{8,20},{10,22},{12,16},{14,18},{16,12}... | collective-permute-start | bytes 811016 | tf_op jit(solution)/shard_map/ppermute | solution.py:334
  62.1 1.5 collective-permute-start.14
  63.6 2.0 %collective-permute-start.16 = (bf16[1040,128]{1,0:T(8,128)(2,1)}, bf16[1040,128]{1,0:T(8,128)(2,1)}, u32[]{:S(2)}, u32[]{:S(2)}) collective-permute-start(bf16[1040,128]{1,0:T(8,128)(2,1)} %get-tuple-element.91), channel_id=1, source_target_pairs={{0,12},{2,14},{4,8},{6,10},{8,4},{10,6},{12,0},{14,2},{16,28},{18,... | collective-permute-start | bytes 798728 | tf_op jit(solution)/shard_map/ppermute | solution.py:334
  65.5 1.1 copy-done.2
  66.7 1.2 shard_map.68.refs_1_
  67.9 4.2 %collective-permute-done.14.refs_2_ = bf16[1040,128]{1,0:T(8,128)(2,1)} collective-permute-done((bf16[1040,128]{1,0:T(8,128)(2,1)}, bf16[1040,128]{1,0:T(8,128)(2,1)}, u32[]{:S(2)}, u32[]{:S(2)}) %collective-permute-start.14) | collective-permute-done | bytes 266272 | tf_op jit(solution)/shard_map/ppermute | solution.py:334
  72.0 1.5 collective-permute-start.11
  73.5 4.6 %collective-permute-done.15.refs_3_ = bf16[1040,128]{1,0:T(8,128)(2,1)} collective-permute-done((bf16[1040,128]{1,0:T(8,128)(2,1)}, bf16[1040,128]{1,0:T(8,128)(2,1)}, u32[]{:S(2)}, u32[]{:S(2)}) %collective-permute-start.15) | collective-permute-done | bytes 266272 | tf_op jit(solution)/shard_map/ppermute | solution.py:334
  78.1 5.6 %collective-permute-done.16.refs_4_ = bf16[1040,128]{1,0:T(8,128)(2,1)} collective-permute-done((bf16[1040,128]{1,0:T(8,128)(2,1)}, bf16[1040,128]{1,0:T(8,128)(2,1)}, u32[]{:S(2)}, u32[]{:S(2)}) %collective-permute-start.16) | collective-permute-done | bytes 266272 | tf_op jit(solution)/shard_map/ppermute | solution.py:334
  83.6 1.8 shard_map.67
  85.4 1.6 collective-permute-done.11.refs_0_
  87.1 0.9 shard_map.69.b_ref.refs_3_.refs_1_.refs_4_
  88.0 3.6 %shard_map.70 = f32[1024,512]{1,0:T(8,128)} custom-call(s32[1]{0:T(128)} %bitcast.20.table, bf16[1024,1024]{1,0:T(8,128)(2,1)S(1)} %get-tuple-element.99.x_ref, bf16[1024,2048]{1,0:T(8,128)(2,1)} %shard_map.69.b_ref.refs_3_.refs_1_.refs_4_), custom_call_target="tpu_custom_call" | custom-call | flops 1073741824 | bytes 5242880 | tf_op jit(solution)/shard_map/pallas_call | solution.py:198
  91.5 3.6 %shard_map.71 = f32[1024,512]{1,0:T(8,128)} custom-call(s32[1]{0:T(128)} %bitcast.19.table, bf16[1024,1024]{1,0:T(8,128)(2,1)S(1)} %get-tuple-element.99.x_ref, bf16[1024,2048]{1,0:T(8,128)(2,1)} %shard_map.69.b_ref.refs_3_.refs_1_.refs_4_), custom_call_target="tpu_custom_call" | custom-call | flops 1073741824 | bytes 5242880 | tf_op jit(solution)/shard_map/pallas_call | solution.py:198
  95.1 0.5 collective-permute-start.18
  96.0 2.9 %shard_map.72 = bf16[1024,512]{1,0:T(8,128)(2,1)S(1)} custom-call(s32[1]{0:T(128)} %bitcast.18.table, bf16[1024,1024]{1,0:T(8,128)(2,1)S(1)} %get-tuple-element.99.x_ref, bf16[1024,2048]{1,0:T(8,128)(2,1)} %shard_map.69.b_ref.refs_3_.refs_1_.refs_4_, f32[1024,512]{1,0:T(8,128)} %collective-permute-done.17.refs_0_), custom_call_target="tpu_custom_call" | custom-call | flops 1073741824 | bytes 5242880 | tf_op jit(solution)/shard_map/pallas_call | solution.py:198
  99.0 1.6 collective-permute-start.22
  100.6 0.5 collective-permute-start.23
  101.1 2.9 %shard_map.73 = bf16[1024,512]{1,0:T(8,128)(2,1)S(1)} custom-call(s32[1]{0:T(128)} %bitcast.17.table, bf16[1024,1024]{1,0:T(8,128)(2,1)S(1)} %get-tuple-element.99.x_ref, bf16[1024,2048]{1,0:T(8,128)(2,1)} %shard_map.69.b_ref.refs_3_.refs_1_.refs_4_, f32[1024,512]{1,0:T(8,128)} %collective-permute-done.18.refs_0_), custom_call_target="tpu_custom_call" | custom-call | flops 1073741824 | bytes 5242880 | tf_op jit(solution)/shard_map/pallas_call | solution.py:198
  104.1 1.6 collective-permute-start.19
  105.7 0.5 collective-permute-start.20
  106.3 4.7 %collective-permute-done.22.up_ref = bf16[3,128,512]{2,1,0:T(8,128)(2,1)S(1)} collective-permute-done((bf16[3,128,512]{2,1,0:T(8,128)(2,1)S(1)}, bf16[3,128,512]{2,1,0:T(8,128)(2,1)S(1)}, u32[]{:S(2)}, u32[]{:S(2)}) %collective-permute-start.22) | collective-permute-done | bytes 393248 | tf_op jit(solution)/shard_map/ppermute | solution.py:435
  111.0 1.6 collective-permute-done.23.down_ref
  112.9 4.5 %shard_map.75 = bf16[8,128,512]{2,1,0:T(8,128)(2,1)S(1)} custom-call(f32[1,512]{1,0:T(1,128)S(1)} %get-tuple-element.131.eigen_ref, f32[14,128,128]{2,1,0:T(8,128)S(1)} %broadcast_in_dim.44.fluid_ref, bf16[3,128,512]{2,1,0:T(8,128)(2,1)S(1)} %collective-permute-done.22.up_ref, bf16[8,128,512]{2,1,0:T(8,128)(2,1)S(1)} %bitcast.41, ...), custom_call_target="tpu_custom_call" | custom-call | flops 367001600 | bytes 3670016 | tf_op jit(solution)/shard_map/pallas_call | solution.py:250
  117.5 1.2 collective-permute-done.19.up_ref
  118.7 1.2 collective-permute-done.20.down_ref
  119.9 4.5 %shard_map.74 = bf16[8,128,512]{2,1,0:T(8,128)(2,1)S(1)} custom-call(f32[1,512]{1,0:T(1,128)S(1)} %get-tuple-element.132.eigen_ref, f32[14,128,128]{2,1,0:T(8,128)S(1)} %broadcast_in_dim.44.fluid_ref, bf16[3,128,512]{2,1,0:T(8,128)(2,1)S(1)} %collective-permute-done.19.up_ref, bf16[8,128,512]{2,1,0:T(8,128)(2,1)S(1)} %bitcast.42, ...), custom_call_target="tpu_custom_call" | custom-call | flops 367001600 | bytes 3670016 | tf_op jit(solution)/shard_map/pallas_call | solution.py:250
  124.6 2.2 %shard_map.76.refs_2_ = f32[1024,256]{1,0:T(8,128)S(1)} custom-call(s32[4]{0:T(128)S(1)} %pad_add_fusion.1.table, bf16[1024,512]{1,0:T(8,128)(2,1)S(1)} %bitcast.32, bf16[1024,512]{1,0:T(8,128)(2,1)S(1)} %bitcast.37, bf16[1024,512]{1,0:T(8,128)(2,1)S(1)} %collective-permute-done.24.refs_2_, bf16[1024,2048]{1,0:T(8,128)(2,1)S(1)} %copy-done), custom_call_target="tpu_custom_call" | custom-call | flops 1073741824 | bytes 5242880 | tf_op jit(solution)/shard_map/pallas_call | solution.py:306
  127.1 1.6 shard_map.77
  128.7 1.0 collective-permute-start.30
  129.7 3.2 %collective-permute-start.31 = (bf16[1024,128]{1,0:T(8,128)(2,1)S(1)}, bf16[1024,128]{1,0:T(8,128)(2,1)S(1)}, u32[]{:S(2)}, u32[]{:S(2)}) collective-permute-start(bf16[1024,128]{1,0:T(8,128)(2,1)S(1)} %get-tuple-element.124), channel_id=1, source_target_pairs={{0,28},{2,30},{4,24},{6,26},{8,20},{10,22},{12,16},{14,18},{16,12}... | collective-permute-start | bytes 786440 | tf_op jit(solution)/shard_map/ppermute | solution.py:334
  133.0 2.4 %shard_map.78 = (bf16[1024,128]{1,0:T(8,128)(2,1)S(1)}, bf16[1024,128]{1,0:T(8,128)(2,1)S(1)}) custom-call(s32[4]{0:T(128)S(1)} %pad_add_fusion.1.table, bf16[1024,512]{1,0:T(8,128)(2,1)S(1)} %bitcast.33, bf16[1024,512]{1,0:T(8,128)(2,1)S(1)} %bitcast.38, bf16[1024,512]{1,0:T(8,128)(2,1)S(1)} %collective-permute-done.24.refs_2_, ...), custom_call_target="tpu_custom_call" | custom-call | flops 1073741824 | bytes 5242880 | tf_op jit(solution)/shard_map/pallas_call | solution.py:306
  135.7 3.2 %collective-permute-start.26 = (bf16[1024,128]{1,0:T(8,128)(2,1)S(1)}, bf16[1024,128]{1,0:T(8,128)(2,1)S(1)}, u32[]{:S(2)}, u32[]{:S(2)}) collective-permute-start(bf16[1024,128]{1,0:T(8,128)(2,1)S(1)} %get-tuple-element.112), channel_id=1, source_target_pairs={{0,20},{2,22},{4,16},{6,18},{8,28},{10,30},{12,24},{14,26},{16,4},... | collective-permute-start | bytes 786440 | tf_op jit(solution)/shard_map/ppermute | solution.py:334
  139.0 2.4 %shard_map.79 = (bf16[1024,128]{1,0:T(8,128)(2,1)S(1)}, bf16[1024,128]{1,0:T(8,128)(2,1)S(1)}) custom-call(s32[4]{0:T(128)S(1)} %pad_add_fusion.1.table, bf16[1024,512]{1,0:T(8,128)(2,1)S(1)} %bitcast.34, bf16[1024,512]{1,0:T(8,128)(2,1)S(1)} %bitcast.39, bf16[1024,512]{1,0:T(8,128)(2,1)S(1)} %collective-permute-done.24.refs_2_, ...), custom_call_target="tpu_custom_call" | custom-call | flops 1073741824 | bytes 5242880 | tf_op jit(solution)/shard_map/pallas_call | solution.py:306
  141.5 2.4 %shard_map.80 = (bf16[1024,128]{1,0:T(8,128)(2,1)S(1)}, bf16[1024,128]{1,0:T(8,128)(2,1)S(1)}) custom-call(s32[4]{0:T(128)S(1)} %pad_add_fusion.1.table, bf16[1024,512]{1,0:T(8,128)(2,1)S(1)} %bitcast.35, bf16[1024,512]{1,0:T(8,128)(2,1)S(1)} %bitcast.40, bf16[1024,512]{1,0:T(8,128)(2,1)S(1)} %collective-permute-done.24.refs_2_, ...), custom_call_target="tpu_custom_call" | custom-call | flops 1073741824 | bytes 5242880 | tf_op jit(solution)/shard_map/pallas_call | solution.py:306
  143.9 18.3 %collective-permute-start.28 = (bf16[1024,128]{1,0:T(8,128)(2,1)S(1)}, bf16[1024,128]{1,0:T(8,128)(2,1)S(1)}, u32[]{:S(2)}, u32[]{:S(2)}) collective-permute-start(bf16[1024,128]{1,0:T(8,128)(2,1)S(1)} %get-tuple-element.117), channel_id=1, source_target_pairs={{0,12},{2,14},{4,8},{6,10},{8,4},{10,6},{12,0},{14,2},{16,28},{18,... | collective-permute-start | bytes 786440 | tf_op jit(solution)/shard_map/ppermute | solution.py:334
  162.2 1.1 collective-permute-start.29
  163.6 2.2 %shard_map.81.refs_2_ = f32[128,64,128]{2,1,0:T(8,128)} custom-call(s32[2]{0:T(128)S(1)} %pad_add_fusion.4.table, bf16[1024,128]{1,0:T(8,128)(2,1)S(1)} %collective-permute-done.30.refs_0_, bf16[1024,128]{1,0:T(8,128)(2,1)S(1)} %collective-permute-done.31.refs_1_), custom_call_target="tpu_custom_call" | custom-call | flops 262144 | bytes 1572864 | tf_op jit(solution)/shard_map/pallas_call | solution.py:94
  165.7 7.2 %collective-permute-done.29.refs_1_ = bf16[1024,128]{1,0:T(8,128)(2,1)S(1)} collective-permute-done((bf16[1024,128]{1,0:T(8,128)(2,1)S(1)}, bf16[1024,128]{1,0:T(8,128)(2,1)S(1)}, u32[]{:S(2)}, u32[]{:S(2)}) %collective-permute-start.29) | collective-permute-done | bytes 262176 | tf_op jit(solution)/shard_map/ppermute | solution.py:334
  172.9 2.2 %shard_map.82.refs_2_ = f32[128,64,128]{2,1,0:T(8,128)} custom-call(s32[2]{0:T(128)S(1)} %pad_add_fusion.3.table, bf16[1024,128]{1,0:T(8,128)(2,1)S(1)} %get-tuple-element.121.refs_0_, bf16[1024,128]{1,0:T(8,128)(2,1)S(1)} %collective-permute-done.29.refs_1_, f32[128,64,128]{2,1,0:T(8,128)} %shard_map.81.refs_2_), custom_call_target="tpu_custom_call", output_to_operand_aliasing={{}: (3, {})} | custom-call | flops 262144 | bytes 1572864 | tf_op jit(solution)/shard_map/pallas_call | solution.py:94
  175.1 2.2 %shard_map.83.refs_2_ = f32[128,64,128]{2,1,0:T(8,128)} custom-call(s32[2]{0:T(128)S(1)} %get-tuple-element.139.table, bf16[1024,128]{1,0:T(8,128)(2,1)S(1)} %collective-permute-done.27.refs_0_, bf16[1024,128]{1,0:T(8,128)(2,1)S(1)} %collective-permute-done.28.refs_1_, f32[128,64,128]{2,1,0:T(8,128)} %shard_map.82.refs_2_), custom_call_target="tpu_custom_call", output_to_operand_aliasing={{}: (3, {})} | custom-call | flops 262144 | bytes 1572864 | tf_op jit(solution)/shard_map/pallas_call | solution.py:94
  177.3 1.8 collective-permute-done.26.refs_1_
  179.1 2.2 %shard_map.84 = f32[128,64,128]{2,1,0:T(8,128)} custom-call(s32[2]{0:T(128)S(1)} %get-tuple-element.138.table, bf16[1024,128]{1,0:T(8,128)(2,1)S(1)} %collective-permute-done.25.refs_0_, bf16[1024,128]{1,0:T(8,128)(2,1)S(1)} %collective-permute-done.26.refs_1_, f32[128,64,128]{2,1,0:T(8,128)} %shard_map.83.refs_2_), custom_call_target="tpu_custom_call", output_to_operand_aliasing={{}: (3, {})} | custom-call | flops 262144 | bytes 1572864 | tf_op jit(solution)/shard_map/pallas_call | solution.py:94
  (58 shorter events, 2.9 us)
Async XLA Ops:
  0.0 25.5 %copy-start.3 = (bf16[128,2048]{1,0:T(8,128)(2,1)S(1)}, bf16[128,2048]{1,0:T(8,128)(2,1)}, u32[]{:S(2)}) copy-start(bf16[128,2048]{1,0:T(8,128)(2,1)} %refs_0_.1) | copy-start | bytes 1572868
  1.0 17.6 %collective-permute-start = (bf16[64,2048]{1,0:T(8,128)(2,1)S(1)}, bf16[64,2048]{1,0:T(8,128)(2,1)S(1)}, u32[]{:S(2)}, u32[]{:S(2)}) collective-permute-start(bf16[64,2048]{1,0:T(8,128)(2,1)S(1)} %constant_dynamic-slice_fusion), channel_id=1, source_target_pairs={{0,8},{2,10},{4,12},{6,14},{8,0},{10,2},{12,4},{14,6},{16,24},{18,... | collective-permute-start | bytes 786440 | tf_op jit(solution)/shard_map/ppermute | solution.py:334
  4.1 21.4 %collective-permute-start.1 = (bf16[64,2048]{1,0:T(8,128)(2,1)S(1)}, bf16[64,2048]{1,0:T(8,128)(2,1)S(1)}, u32[]{:S(2)}, u32[]{:S(2)}) collective-permute-start(bf16[64,2048]{1,0:T(8,128)(2,1)S(1)} %constant_dynamic-slice_fusion), channel_id=1, source_target_pairs={{0,16},{2,18},{4,20},{6,22},{8,24},{10,26},{12,28},{14,30},{16,0},... | collective-permute-start | bytes 786440 | tf_op jit(solution)/shard_map/ppermute | solution.py:334
  6.7 18.8 %collective-permute-start.2 = (bf16[64,2048]{1,0:T(8,128)(2,1)S(1)}, bf16[64,2048]{1,0:T(8,128)(2,1)S(1)}, u32[]{:S(2)}, u32[]{:S(2)}) collective-permute-start(bf16[64,2048]{1,0:T(8,128)(2,1)S(1)} %constant_dynamic-slice_fusion), channel_id=1, source_target_pairs={{0,24},{2,26},{4,28},{6,30},{8,16},{10,18},{12,20},{14,22},{16,8},... | collective-permute-start | bytes 786440 | tf_op jit(solution)/shard_map/ppermute | solution.py:334
  6.7 18.8 %collective-permute-start.3 = (bf16[128,2048]{1,0:T(8,128)(2,1)}, bf16[128,2048]{1,0:T(8,128)(2,1)S(1)}, u32[]{:S(2)}, u32[]{:S(2)}) collective-permute-start(bf16[128,2048]{1,0:T(8,128)(2,1)} %refs_0_.1), channel_id=1, source_target_pairs={{0,4},{2,6},{4,0},{6,2},{8,12},{10,14},{12,8},{14,10},{16,20},{18,... | collective-permute-start | bytes 1572872 | tf_op jit(solution)/shard_map/ppermute | solution.py:334
  8.5 1.8 %collective-permute-start.4 = (f32[128]{0:T(128)}, f32[128]{0:T(128)S(1)}, u32[]{:S(2)}, u32[]{:S(2)}) collective-permute-start(f32[128]{0:T(128)} %param.8), channel_id=1, source_target_pairs={{0,2},{2,0},{4,6},{6,4},{8,10},{10,8},{12,14},{14,12},{16,18},{18,... | collective-permute-start | bytes 1544 | tf_op jit(solution)/shard_map/ppermute | solution.py:335
  10.3 16.5 %collective-permute-start.5 = (f32[3,128]{1,0:T(4,128)S(1)}, f32[3,128]{1,0:T(4,128)S(1)}, u32[]{:S(2)}, u32[]{:S(2)}) collective-permute-start(f32[3,128]{1,0:T(4,128)S(1)} %get-tuple-element.130), channel_id=1, source_target_pairs={{0,1},{1,0},{2,3},{3,2},{4,5},{5,4},{6,7},{7,6},{8,9},{9,8},{10,11... | collective-permute-start | bytes 4616 | tf_op jit(solution)/shard_map/ppermute | solution.py:369
  18.6 8.2 %collective-permute-start.6 = (f32[3,128]{1,0:T(4,128)S(1)}, f32[3,128]{1,0:T(4,128)S(1)}, u32[]{:S(2)}, u32[]{:S(2)}) collective-permute-start(f32[3,128]{1,0:T(4,128)S(1)} %get-tuple-element.129), channel_id=1, source_target_pairs={{1,0},{0,1},{3,2},{2,3},{5,4},{4,5},{7,6},{6,7},{9,8},{8,9},{11,10... | collective-permute-start | bytes 4616 | tf_op jit(solution)/shard_map/ppermute | solution.py:370
  26.8 23.7 %collective-permute-start.9 = (bf16[1040,128]{1,0:T(8,128)(2,1)S(1)}, bf16[1040,128]{1,0:T(8,128)(2,1)S(1)}, u32[]{:S(2)}, u32[]{:S(2)}) collective-permute-start(bf16[1040,128]{1,0:T(8,128)(2,1)S(1)} %get-tuple-element.77), channel_id=1, source_target_pairs={{0,16},{2,18},{4,20},{6,22},{8,24},{10,26},{12,28},{14,30},{16,0},... | collective-permute-start | bytes 798728 | tf_op jit(solution)/shard_map/ppermute | solution.py:334
  32.7 23.4 %collective-permute-start.10 = (bf16[1040,128]{1,0:T(8,128)(2,1)S(1)}, bf16[1040,128]{1,0:T(8,128)(2,1)S(1)}, u32[]{:S(2)}, u32[]{:S(2)}) collective-permute-start(bf16[1040,128]{1,0:T(8,128)(2,1)S(1)} %get-tuple-element.78), channel_id=1, source_target_pairs={{0,20},{2,22},{4,16},{6,18},{8,28},{10,30},{12,24},{14,26},{16,4},... | collective-permute-start | bytes 798728 | tf_op jit(solution)/shard_map/ppermute | solution.py:334
  33.8 23.6 %collective-permute-start.7 = (bf16[192,2048]{1,0:T(8,128)(2,1)S(1)}, bf16[192,2048]{1,0:T(8,128)(2,1)S(1)}, u32[]{:S(2)}, u32[]{:S(2)}) collective-permute-start(bf16[192,2048]{1,0:T(8,128)(2,1)S(1)} %constant_dynamic-update-slice_fusion), channel_id=1, source_target_pairs={{0,4},{2,6},{4,0},{6,2},{8,12},{10,14},{12,8},{14,10},{16,20},{18,... | collective-permute-start | bytes 2359304 | tf_op jit(solution)/shard_map/ppermute | solution.py:334
  34.3 23.1 %collective-permute-start.8 = (bf16[192,2048]{1,0:T(8,128)(2,1)S(1)}, bf16[192,2048]{1,0:T(8,128)(2,1)S(1)}, u32[]{:S(2)}, u32[]{:S(2)}) collective-permute-start(bf16[192,2048]{1,0:T(8,128)(2,1)S(1)} %constant_dynamic-update-slice_fusion), channel_id=1, source_target_pairs={{0,1},{1,0},{2,3},{3,2},{4,5},{5,4},{6,7},{7,6},{8,9},{9,8},{10,11... | collective-permute-start | bytes 2359304 | tf_op jit(solution)/shard_map/ppermute | solution.py:336
  57.4 0.9 copy-start.1
  58.3 25.4 %collective-permute-start.12 = (bf16[1056,128]{1,0:T(8,128)(2,1)S(1)}, bf16[1056,128]{1,0:T(8,128)(2,1)}, u32[]{:S(2)}, u32[]{:S(2)}) collective-permute-start(bf16[1056,128]{1,0:T(8,128)(2,1)S(1)} %get-tuple-element.87), channel_id=1, source_target_pairs={{0,24},{2,26},{4,28},{6,30},{8,16},{10,18},{12,20},{14,22},{16,8},... | collective-permute-start | bytes 811016 | tf_op jit(solution)/shard_map/ppermute | solution.py:334
  59.6 24.0 %collective-permute-start.13 = (bf16[1056,128]{1,0:T(8,128)(2,1)S(1)}, bf16[1056,128]{1,0:T(8,128)(2,1)}, u32[]{:S(2)}, u32[]{:S(2)}) collective-permute-start(bf16[1056,128]{1,0:T(8,128)(2,1)S(1)} %get-tuple-element.88), channel_id=1, source_target_pairs={{0,28},{2,30},{4,24},{6,26},{8,20},{10,22},{12,16},{14,18},{16,12}... | collective-permute-start | bytes 811016 | tf_op jit(solution)/shard_map/ppermute | solution.py:334
  62.1 10.0 %collective-permute-start.14 = (bf16[1040,128]{1,0:T(8,128)(2,1)}, bf16[1040,128]{1,0:T(8,128)(2,1)}, u32[]{:S(2)}, u32[]{:S(2)}) collective-permute-start(bf16[1040,128]{1,0:T(8,128)(2,1)} %get-tuple-element.89), channel_id=1, source_target_pairs={{0,4},{2,6},{4,0},{6,2},{8,12},{10,14},{12,8},{14,10},{16,20},{18,... | collective-permute-start | bytes 798728 | tf_op jit(solution)/shard_map/ppermute | solution.py:334
  63.6 14.5 %collective-permute-start.15 = (bf16[1040,128]{1,0:T(8,128)(2,1)}, bf16[1040,128]{1,0:T(8,128)(2,1)}, u32[]{:S(2)}, u32[]{:S(2)}) collective-permute-start(bf16[1040,128]{1,0:T(8,128)(2,1)} %get-tuple-element.90), channel_id=1, source_target_pairs={{0,8},{2,10},{4,12},{6,14},{8,0},{10,2},{12,4},{14,6},{16,24},{18,... | collective-permute-start | bytes 798728 | tf_op jit(solution)/shard_map/ppermute | solution.py:334
  63.6 20.1 %collective-permute-start.16 = (bf16[1040,128]{1,0:T(8,128)(2,1)}, bf16[1040,128]{1,0:T(8,128)(2,1)}, u32[]{:S(2)}, u32[]{:S(2)}) collective-permute-start(bf16[1040,128]{1,0:T(8,128)(2,1)} %get-tuple-element.91), channel_id=1, source_target_pairs={{0,12},{2,14},{4,8},{6,10},{8,4},{10,6},{12,0},{14,2},{16,28},{18,... | collective-permute-start | bytes 798728 | tf_op jit(solution)/shard_map/ppermute | solution.py:334
  65.5 1.1 copy-start.2
  72.0 15.0 %collective-permute-start.11 = (bf16[192,2048]{1,0:T(8,128)(2,1)S(1)}, bf16[192,2048]{1,0:T(8,128)(2,1)S(1)}, u32[]{:S(2)}, u32[]{:S(2)}) collective-permute-start(bf16[192,2048]{1,0:T(8,128)(2,1)S(1)} %collective-permute-done.7.refs_0_), channel_id=1, source_target_pairs={{0,1},{1,0},{2,3},{3,2},{4,5},{5,4},{6,7},{7,6},{8,9},{9,8},{10,11... | collective-permute-start | bytes 2359304 | tf_op jit(solution)/shard_map/ppermute | solution.py:336
  91.5 4.5 %collective-permute-start.17 = (f32[1024,512]{1,0:T(8,128)}, f32[1024,512]{1,0:T(8,128)}, u32[]{:S(2)}, u32[]{:S(2)}) collective-permute-start(f32[1024,512]{1,0:T(8,128)} %shard_map.70), channel_id=1, source_target_pairs={{0,2},{2,0},{4,6},{6,4},{8,10},{10,8},{12,14},{14,12},{16,18},{18,... | collective-permute-start | bytes 6291464 | tf_op jit(solution)/shard_map/ppermute | solution.py:335
  95.1 6.0 %collective-permute-start.18 = (f32[1024,512]{1,0:T(8,128)}, f32[1024,512]{1,0:T(8,128)}, u32[]{:S(2)}, u32[]{:S(2)}) collective-permute-start(f32[1024,512]{1,0:T(8,128)} %shard_map.71), channel_id=1, source_target_pairs={{0,2},{2,0},{4,6},{6,4},{8,10},{10,8},{12,14},{14,12},{16,18},{18,... | collective-permute-start | bytes 6291464 | tf_op jit(solution)/shard_map/ppermute | solution.py:335
  99.0 12.0 %collective-permute-start.22 = (bf16[3,128,512]{2,1,0:T(8,128)(2,1)S(1)}, bf16[3,128,512]{2,1,0:T(8,128)(2,1)S(1)}, u32[]{:S(2)}, u32[]{:S(2)}) collective-permute-start(bf16[3,128,512]{2,1,0:T(8,128)(2,1)S(1)} %bitcast.45), channel_id=1, source_target_pairs={{0,4},{2,6},{4,12},{6,14},{12,8},{14,10},{8,16},{10,18},{16,20},{1... | collective-permute-start | bytes 1179656 | tf_op jit(solution)/shard_map/ppermute | solution.py:435
  100.6 12.0 %collective-permute-start.23 = (bf16[3,128,512]{2,1,0:T(8,128)(2,1)S(1)}, bf16[3,128,512]{2,1,0:T(8,128)(2,1)S(1)}, u32[]{:S(2)}, u32[]{:S(2)}) collective-permute-start(bf16[3,128,512]{2,1,0:T(8,128)(2,1)S(1)} %bitcast.43), channel_id=1, source_target_pairs={{4,0},{6,2},{12,4},{14,6},{8,12},{10,14},{16,8},{18,10},{20,16},{2... | collective-permute-start | bytes 1179656 | tf_op jit(solution)/shard_map/ppermute | solution.py:436
  104.1 14.6 %collective-permute-start.19 = (bf16[3,128,512]{2,1,0:T(8,128)(2,1)S(1)}, bf16[3,128,512]{2,1,0:T(8,128)(2,1)S(1)}, u32[]{:S(2)}, u32[]{:S(2)}) collective-permute-start(bf16[3,128,512]{2,1,0:T(8,128)(2,1)S(1)} %bitcast.46), channel_id=1, source_target_pairs={{0,4},{2,6},{4,12},{6,14},{12,8},{14,10},{8,16},{10,18},{16,20},{1... | collective-permute-start | bytes 1179656 | tf_op jit(solution)/shard_map/ppermute | solution.py:435
  105.7 14.2 %collective-permute-start.20 = (bf16[3,128,512]{2,1,0:T(8,128)(2,1)S(1)}, bf16[3,128,512]{2,1,0:T(8,128)(2,1)S(1)}, u32[]{:S(2)}, u32[]{:S(2)}) collective-permute-start(bf16[3,128,512]{2,1,0:T(8,128)(2,1)S(1)} %bitcast.44), channel_id=1, source_target_pairs={{4,0},{6,2},{12,4},{14,6},{8,12},{10,14},{16,8},{18,10},{20,16},{2... | collective-permute-start | bytes 1179656 | tf_op jit(solution)/shard_map/ppermute | solution.py:436
  106.3 18.3 %copy-start = (bf16[1024,2048]{1,0:T(8,128)(2,1)S(1)}, bf16[1024,2048]{1,0:T(8,128)(2,1)}, u32[]{:S(2)}) copy-start(bf16[1024,2048]{1,0:T(8,128)(2,1)} %shard_map.69.b_ref.refs_3_.refs_1_.refs_4_) | copy-start | bytes 12582916
  117.4 7.2 %collective-permute-start.24 = (bf16[1024,512]{1,0:T(8,128)(2,1)S(1)}, bf16[1024,512]{1,0:T(8,128)(2,1)S(1)}, u32[]{:S(2)}, u32[]{:S(2)}) collective-permute-start(bf16[1024,512]{1,0:T(8,128)(2,1)S(1)} %bitcast.31), channel_id=1, source_target_pairs={{0,2},{2,0},{4,6},{6,4},{8,10},{10,8},{12,14},{14,12},{16,18},{18,... | collective-permute-start | bytes 3145736 | tf_op jit(solution)/shard_map/ppermute | solution.py:335
  124.4 2.7 %collective-permute-start.21 = (bf16[1024,512]{1,0:T(8,128)(2,1)S(1)}, bf16[1024,512]{1,0:T(8,128)(2,1)S(1)}, u32[]{:S(2)}, u32[]{:S(2)}) collective-permute-start(bf16[1024,512]{1,0:T(8,128)(2,1)S(1)} %bitcast.36), channel_id=1, source_target_pairs={{0,2},{2,0},{4,6},{6,4},{8,10},{10,8},{12,14},{14,12},{16,18},{18,... | collective-permute-start | bytes 3145736 | tf_op jit(solution)/shard_map/ppermute | solution.py:335
  128.7 15.2 %collective-permute-start.30 = (bf16[1024,128]{1,0:T(8,128)(2,1)S(1)}, bf16[1024,128]{1,0:T(8,128)(2,1)S(1)}, u32[]{:S(2)}, u32[]{:S(2)}) collective-permute-start(bf16[1024,128]{1,0:T(8,128)(2,1)S(1)} %get-tuple-element.123), channel_id=1, source_target_pairs={{0,24},{2,26},{4,28},{6,30},{8,16},{10,18},{12,20},{14,22},{16,8},... | collective-permute-start | bytes 786440 | tf_op jit(solution)/shard_map/ppermute | solution.py:334
  129.7 32.5 %collective-permute-start.31 = (bf16[1024,128]{1,0:T(8,128)(2,1)S(1)}, bf16[1024,128]{1,0:T(8,128)(2,1)S(1)}, u32[]{:S(2)}, u32[]{:S(2)}) collective-permute-start(bf16[1024,128]{1,0:T(8,128)(2,1)S(1)} %get-tuple-element.124), channel_id=1, source_target_pairs={{0,28},{2,30},{4,24},{6,26},{8,20},{10,22},{12,16},{14,18},{16,12}... | collective-permute-start | bytes 786440 | tf_op jit(solution)/shard_map/ppermute | solution.py:334
  135.4 41.9 %collective-permute-start.25 = (bf16[1024,128]{1,0:T(8,128)(2,1)S(1)}, bf16[1024,128]{1,0:T(8,128)(2,1)S(1)}, u32[]{:S(2)}, u32[]{:S(2)}) collective-permute-start(bf16[1024,128]{1,0:T(8,128)(2,1)S(1)} %get-tuple-element.111), channel_id=1, source_target_pairs={{0,16},{2,18},{4,20},{6,22},{8,24},{10,26},{12,28},{14,30},{16,0},... | collective-permute-start | bytes 786440 | tf_op jit(solution)/shard_map/ppermute | solution.py:334
  135.7 43.3 %collective-permute-start.26 = (bf16[1024,128]{1,0:T(8,128)(2,1)S(1)}, bf16[1024,128]{1,0:T(8,128)(2,1)S(1)}, u32[]{:S(2)}, u32[]{:S(2)}) collective-permute-start(bf16[1024,128]{1,0:T(8,128)(2,1)S(1)} %get-tuple-element.112), channel_id=1, source_target_pairs={{0,20},{2,22},{4,16},{6,18},{8,28},{10,30},{12,24},{14,26},{16,4},... | collective-permute-start | bytes 786440 | tf_op jit(solution)/shard_map/ppermute | solution.py:334
  141.4 33.7 %collective-permute-start.27 = (bf16[1024,128]{1,0:T(8,128)(2,1)S(1)}, bf16[1024,128]{1,0:T(8,128)(2,1)S(1)}, u32[]{:S(2)}, u32[]{:S(2)}) collective-permute-start(bf16[1024,128]{1,0:T(8,128)(2,1)S(1)} %get-tuple-element.116), channel_id=1, source_target_pairs={{0,8},{2,10},{4,12},{6,14},{8,0},{10,2},{12,4},{14,6},{16,24},{18,... | collective-permute-start | bytes 786440 | tf_op jit(solution)/shard_map/ppermute | solution.py:334
  143.9 31.2 %collective-permute-start.28 = (bf16[1024,128]{1,0:T(8,128)(2,1)S(1)}, bf16[1024,128]{1,0:T(8,128)(2,1)S(1)}, u32[]{:S(2)}, u32[]{:S(2)}) collective-permute-start(bf16[1024,128]{1,0:T(8,128)(2,1)S(1)} %get-tuple-element.117), channel_id=1, source_target_pairs={{0,12},{2,14},{4,8},{6,10},{8,4},{10,6},{12,0},{14,2},{16,28},{18,... | collective-permute-start | bytes 786440 | tf_op jit(solution)/shard_map/ppermute | solution.py:334
  162.2 10.7 %collective-permute-start.29 = (bf16[1024,128]{1,0:T(8,128)(2,1)S(1)}, bf16[1024,128]{1,0:T(8,128)(2,1)S(1)}, u32[]{:S(2)}, u32[]{:S(2)}) collective-permute-start(bf16[1024,128]{1,0:T(8,128)(2,1)S(1)} %get-tuple-element.122), channel_id=1, source_target_pairs={{0,4},{2,6},{4,0},{6,2},{8,12},{10,14},{12,8},{14,10},{16,20},{18,... | collective-permute-start | bytes 786440 | tf_op jit(solution)/shard_map/ppermute | solution.py:334

commit v6 on v4

--- a/solution.py
+++ b/solution.py
@@ -389,13 +389,13 @@
 
     held = jnp.concatenate(column)
     over_y, over_x = chip_swap(held, 1), tile_swap(held)
-    evens = list(range(far, far + far // 2))
+    evens = [*range(far, far + far // 2), 2]
     x = gather([send[0], *[chip_swap(send[s], s) for s in evens]], [0, *evens], cells, chips, None, LATE)
     over_y, over_x, x, send = lax.optimization_barrier((over_y, over_x, x, send))
 
     corner = tile_swap(over_y)
     full = join(i32(odd), [over_y, over_x], (("mine", odds[1:]), ("other", ids)), planes, chips, full, small)
-    last, nearby = list(range(far + far // 2, chips)), list(range(1, far))
+    last, nearby = list(range(far + far // 2, chips)), [1, *range(3, far)]
     final = [chip_swap(send[s], s) for s in last]
     close = [chip_swap(send[s], s) for s in nearby]
     x = gather([*final, *close], [*last, *nearby], cells, chips, x, LATE)

time: 182 us -> 180 us (0.989)
  waiting for transfers between devices: 61.9 us -> 58.1 us
  starting transfers between devices: 59.2 us -> 61.2 us
    ppermute x2, waiting for transfers between devices: 2.79 us -> 7.5 us  [local(): down = lax.ppermute(spectral[:HALO], ('wn', 'tile'), backward)]
    ppermute x2, waiting for transfers between devices: 5.93 us -> 1.99 us  [local(): up = lax.ppermute(spectral[rows - HALO:], ('wn', 'tile'), onward)]
    ppermute x2, starting transfers between devices: 3.14 us -> 6.4 us  [local(): up = lax.ppermute(spectral[rows - HALO:], ('wn', 'tile'), onward)]
    ppermute x19, waiting for transfers between devices: 50.9 us -> 47.9 us  [local(): chip_swap = lambda v, s: lax.ppermute(v, 'wn', flip(s))]
  transfers between devices with their start and end apart: 32 -> 32, of which waited for: 16 -> 12; matrix products, arithmetic and copies ran while one was open for 2% -> 2% of each run, Pallas kernels for 25% -> 25%
where the time goes in v6:
time: 180 us; the launch traced here: 179 us
  starting transfers between devices  61.2 us (34%)
  waiting for transfers between devices  58.1 us (32%)
  Pallas kernels  53 us (29%)
  local copies, waits for them, and re-layouts  3.83 us (2%)
  other arithmetic  2.79 us (2%)
    ppermute x19, starting transfers between devices, local(): chip_swap = lambda v, s: lax.ppermute(v, 'wn', flip(s))  48.6 us
    ppermute x19, waiting for transfers between devices, local(): chip_swap = lambda v, s: lax.ppermute(v, 'wn', flip(s))  47.9 us
    pallas_call x4, Pallas kernels, forward(): pl.pallas_call(forward_body, grid_spec=pltpu.PrefetchScalarGridSpec(num_s...  13 us
    pallas_call x5, Pallas kernels, inverse(): pl.pallas_call(functools.partial(inverse_body, min(cells, 256), skip, bas...  11.1 us
    pallas_call x2, Pallas kernels, sweep(): pl.pallas_call(sweep_body, grid=(modes // lanes,), in_specs=[pl.BlockSpec...  9.01 us
    pallas_call x4, Pallas kernels, place_pair(): pl.pallas_call(place_body, grid_spec=pltpu.PrefetchScalarGridSpec(num_sca...  8.65 us
    ppermute x2, waiting for transfers between devices, local(): down = lax.ppermute(spectral[:HALO], ('wn', 'tile'), backward)  7.5 us
    ppermute x2, starting transfers between devices, local(): up = lax.ppermute(spectral[rows - HALO:], ('wn', 'tile'), onward)  6.4 us
  transfers between devices with their start and end apart: 32, of which 12 were waited for; matrix products, arithmetic and copies ran while one was open for 2% of the time, Pallas kernels for 25%

profile of v6, /device:TPU:0, one launch (start us, length us, event | category | flops | bytes accessed | tf_op | source)
XLA Modules:
  0.0 179.2 jit_solution(8553388766224563180)
XLA Ops:
  0.0 1.0 constant_dynamic-slice_fusion
  1.0 3.1 %collective-permute-start = (bf16[64,2048]{1,0:T(8,128)(2,1)S(1)}, bf16[64,2048]{1,0:T(8,128)(2,1)S(1)}, u32[]{:S(2)}, u32[]{:S(2)}) collective-permute-start(bf16[64,2048]{1,0:T(8,128)(2,1)S(1)} %constant_dynamic-slice_fusion), channel_id=1, source_target_pairs={{0,8},{2,10},{4,12},{6,14},{8,0},{10,2},{12,4},{14,6},{16,24},{18,... | collective-permute-start | bytes 786440 | tf_op jit(solution)/shard_map/ppermute | solution.py:334
  4.1 2.6 %collective-permute-start.1 = (bf16[64,2048]{1,0:T(8,128)(2,1)S(1)}, bf16[64,2048]{1,0:T(8,128)(2,1)S(1)}, u32[]{:S(2)}, u32[]{:S(2)}) collective-permute-start(bf16[64,2048]{1,0:T(8,128)(2,1)S(1)} %constant_dynamic-slice_fusion), channel_id=1, source_target_pairs={{0,16},{2,18},{4,20},{6,22},{8,24},{10,26},{12,28},{14,30},{16,0},... | collective-permute-start | bytes 786440 | tf_op jit(solution)/shard_map/ppermute | solution.py:334
  6.7 1.7 collective-permute-start.3
  8.5 0.8 select_reduce_fusion.1
  9.2 0.1 copy.15.w_ref
  9.3 0.8 subtract_convert_fusion
  10.3 1.6 collective-permute-start.5
  11.8 0.7 fusion.3
  12.6 5.9 %shard_map.65 = (bf16[1040,128]{1,0:T(8,128)(2,1)S(1)}, bf16[1040,128]{1,0:T(8,128)(2,1)}, bf16[1040,128]{1,0:T(8,128)(2,1)S(1)}, bf16[1040,128]{1,0:T(8,128)(2,...) custom-call(s32[8]{0:T(128)S(1)} %stack.95.table, ...), custom_call_target="tpu_custom_call" | custom-call | flops 1048576 | bytes 6291456 | tf_op jit(solution)/shard_map/pallas_call | solution.py:56
  18.5 0.5 collective-permute-start.6
  19.0 6.5 %collective-permute-done.1.refs_2_ = bf16[64,2048]{1,0:T(8,128)(2,1)S(1)} collective-permute-done((bf16[64,2048]{1,0:T(8,128)(2,1)S(1)}, bf16[64,2048]{1,0:T(8,128)(2,1)S(1)}, u32[]{:S(2)}, u32[]{:S(2)}) %collective-permute-start.1) | collective-permute-done | bytes 262176 | tf_op jit(solution)/shard_map/ppermute | solution.py:334
  25.5 1.3 shard_map.64.refs_2_
  26.8 5.8 %collective-permute-start.9 = (bf16[1040,128]{1,0:T(8,128)(2,1)S(1)}, bf16[1040,128]{1,0:T(8,128)(2,1)S(1)}, u32[]{:S(2)}, u32[]{:S(2)}) collective-permute-start(bf16[1040,128]{1,0:T(8,128)(2,1)S(1)} %get-tuple-element.70), channel_id=1, source_target_pairs={{0,16},{2,18},{4,20},{6,22},{8,24},{10,26},{12,28},{14,30},{16,0},... | collective-permute-start | bytes 798728 | tf_op jit(solution)/shard_map/ppermute | solution.py:334
  32.7 1.0 collective-permute-start.10
  33.7 1.8 %collective-permute-start.11 = (bf16[1040,128]{1,0:T(8,128)(2,1)S(1)}, bf16[1040,128]{1,0:T(8,128)(2,1)S(1)}, u32[]{:S(2)}, u32[]{:S(2)}) collective-permute-start(bf16[1040,128]{1,0:T(8,128)(2,1)S(1)} %get-tuple-element.72), channel_id=1, source_target_pairs={{0,8},{2,10},{4,12},{6,14},{8,0},{10,2},{12,4},{14,6},{16,24},{18,... | collective-permute-start | bytes 798728 | tf_op jit(solution)/shard_map/ppermute | solution.py:334
  35.6 0.6 collective-permute-start.7
  36.2 1.5 collective-permute-start.8
  37.7 12.9 %collective-permute-done.9.refs_1_ = bf16[1040,128]{1,0:T(8,128)(2,1)S(1)} collective-permute-done((bf16[1040,128]{1,0:T(8,128)(2,1)S(1)}, bf16[1040,128]{1,0:T(8,128)(2,1)S(1)}, u32[]{:S(2)}, u32[]{:S(2)}) %collective-permute-start.9) | collective-permute-done | bytes 266272 | tf_op jit(solution)/shard_map/ppermute | solution.py:334
  50.6 5.5 %collective-permute-done.10.refs_2_ = bf16[1040,128]{1,0:T(8,128)(2,1)S(1)} collective-permute-done((bf16[1040,128]{1,0:T(8,128)(2,1)S(1)}, bf16[1040,128]{1,0:T(8,128)(2,1)S(1)}, u32[]{:S(2)}, u32[]{:S(2)}) %collective-permute-start.10) | collective-permute-done | bytes 266272 | tf_op jit(solution)/shard_map/ppermute | solution.py:334
  56.1 0.4 shard_map.66
  56.5 2.2 %collective-permute-done.7.refs_0_ = bf16[192,2048]{1,0:T(8,128)(2,1)S(1)} collective-permute-done((bf16[192,2048]{1,0:T(8,128)(2,1)S(1)}, bf16[192,2048]{1,0:T(8,128)(2,1)S(1)}, u32[]{:S(2)}, u32[]{:S(2)}) %collective-permute-start.7) | collective-permute-done | bytes 786464 | tf_op jit(solution)/shard_map/ppermute | solution.py:334
  58.7 0.9 copy-done.1
  59.6 2.5 %collective-permute-start.13 = (bf16[1056,128]{1,0:T(8,128)(2,1)S(1)}, bf16[1056,128]{1,0:T(8,128)(2,1)}, u32[]{:S(2)}, u32[]{:S(2)}) collective-permute-start(bf16[1056,128]{1,0:T(8,128)(2,1)S(1)} %get-tuple-element.80), channel_id=1, source_target_pairs={{0,24},{2,26},{4,28},{6,30},{8,16},{10,18},{12,20},{14,22},{16,8},... | collective-permute-start | bytes 811016 | tf_op jit(solution)/shard_map/ppermute | solution.py:334
  62.0 1.3 collective-permute-start.14
  63.3 1.5 collective-permute-start.15
  64.9 1.5 collective-permute-start.12
  66.3 1.1 copy-done.2
  67.5 1.2 shard_map.68.refs_1_
  68.7 10.9 %collective-permute-done.15.refs_2_ = bf16[1040,128]{1,0:T(8,128)(2,1)} collective-permute-done((bf16[1040,128]{1,0:T(8,128)(2,1)}, bf16[1040,128]{1,0:T(8,128)(2,1)}, u32[]{:S(2)}, u32[]{:S(2)}) %collective-permute-start.15) | collective-permute-done | bytes 266272 | tf_op jit(solution)/shard_map/ppermute | solution.py:334
  79.5 1.6 shard_map.67
  81.1 0.9 shard_map.69.b_ref.refs_4_.refs_3_.refs_1_
  82.1 3.6 %shard_map.70 = f32[1024,512]{1,0:T(8,128)} custom-call(s32[1]{0:T(128)} %bitcast.19.table, bf16[1024,1024]{1,0:T(8,128)(2,1)S(1)} %get-tuple-element.91.x_ref, bf16[1024,2048]{1,0:T(8,128)(2,1)} %shard_map.69.b_ref.refs_4_.refs_3_.refs_1_), custom_call_target="tpu_custom_call" | custom-call | flops 1073741824 | bytes 5242880 | tf_op jit(solution)/shard_map/pallas_call | solution.py:198
  85.6 3.6 %shard_map.71 = f32[1024,512]{1,0:T(8,128)} custom-call(s32[1]{0:T(128)} %bitcast.18.table, bf16[1024,1024]{1,0:T(8,128)(2,1)S(1)} %get-tuple-element.91.x_ref, bf16[1024,2048]{1,0:T(8,128)(2,1)} %shard_map.69.b_ref.refs_4_.refs_3_.refs_1_), custom_call_target="tpu_custom_call" | custom-call | flops 1073741824 | bytes 5242880 | tf_op jit(solution)/shard_map/pallas_call | solution.py:198
  89.2 0.5 collective-permute-start.20
  89.9 0.3 collective-permute-done.17.refs_0_
  90.1 2.9 %shard_map.72 = bf16[1024,512]{1,0:T(8,128)(2,1)S(1)} custom-call(s32[1]{0:T(128)} %bitcast.17.table, bf16[1024,1024]{1,0:T(8,128)(2,1)S(1)} %get-tuple-element.91.x_ref, bf16[1024,2048]{1,0:T(8,128)(2,1)} %shard_map.69.b_ref.refs_4_.refs_3_.refs_1_, f32[1024,512]{1,0:T(8,128)} %collective-permute-done.17.refs_0_), custom_call_target="tpu_custom_call" | custom-call | flops 1073741824 | bytes 5242880 | tf_op jit(solution)/shard_map/pallas_call | solution.py:198
  93.1 1.6 collective-permute-start.18
  94.7 0.5 collective-permute-start.19
  95.2 2.9 %shard_map.74 = bf16[1024,512]{1,0:T(8,128)(2,1)S(1)} custom-call(s32[1]{0:T(128)} %bitcast.24.table, bf16[1024,1024]{1,0:T(8,128)(2,1)S(1)} %get-tuple-element.91.x_ref, bf16[1024,2048]{1,0:T(8,128)(2,1)} %shard_map.69.b_ref.refs_4_.refs_3_.refs_1_, f32[1024,512]{1,0:T(8,128)} %collective-permute-done.20.refs_0_), custom_call_target="tpu_custom_call" | custom-call | flops 1073741824 | bytes 5242880 | tf_op jit(solution)/shard_map/pallas_call | solution.py:198
  98.2 4.8 %collective-permute-start.21 = (bf16[3,128,512]{2,1,0:T(8,128)(2,1)S(1)}, bf16[3,128,512]{2,1,0:T(8,128)(2,1)S(1)}, u32[]{:S(2)}, u32[]{:S(2)}) collective-permute-start(bf16[3,128,512]{2,1,0:T(8,128)(2,1)S(1)} %bitcast.46), channel_id=1, source_target_pairs={{0,4},{2,6},{4,12},{6,14},{12,8},{14,10},{8,16},{10,18},{16,20},{1... | collective-permute-start | bytes 1179656 | tf_op jit(solution)/shard_map/ppermute | solution.py:435
  103.0 0.1 select_reduce_fusion
  103.1 2.0 %collective-permute-done.18.up_ref = bf16[3,128,512]{2,1,0:T(8,128)(2,1)S(1)} collective-permute-done((bf16[3,128,512]{2,1,0:T(8,128)(2,1)S(1)}, bf16[3,128,512]{2,1,0:T(8,128)(2,1)S(1)}, u32[]{:S(2)}, u32[]{:S(2)}) %collective-permute-start.18) | collective-permute-done | bytes 393248 | tf_op jit(solution)/shard_map/ppermute | solution.py:435
  105.1 4.8 %collective-permute-done.19.down_ref = bf16[3,128,512]{2,1,0:T(8,128)(2,1)S(1)} collective-permute-done((bf16[3,128,512]{2,1,0:T(8,128)(2,1)S(1)}, bf16[3,128,512]{2,1,0:T(8,128)(2,1)S(1)}, u32[]{:S(2)}, u32[]{:S(2)}) %collective-permute-start.19) | collective-permute-done | bytes 393248 | tf_op jit(solution)/shard_map/ppermute | solution.py:436
  109.9 0.3 broadcast_in_dim.44.fluid_ref
  110.2 4.5 %shard_map.73 = bf16[8,128,512]{2,1,0:T(8,128)(2,1)S(1)} custom-call(f32[1,512]{1,0:T(1,128)S(1)} %get-tuple-element.118.eigen_ref, f32[14,128,128]{2,1,0:T(8,128)S(1)} %broadcast_in_dim.44.fluid_ref, bf16[3,128,512]{2,1,0:T(8,128)(2,1)S(1)} %collective-permute-done.18.up_ref, bf16[8,128,512]{2,1,0:T(8,128)(2,1)S(1)} %bitcast.41, ...), custom_call_target="tpu_custom_call" | custom-call | flops 367001600 | bytes 3670016 | tf_op jit(solution)/shard_map/pallas_call | solution.py:250
  114.8 2.7 %collective-permute-done.22.down_ref = bf16[3,128,512]{2,1,0:T(8,128)(2,1)S(1)} collective-permute-done((bf16[3,128,512]{2,1,0:T(8,128)(2,1)S(1)}, bf16[3,128,512]{2,1,0:T(8,128)(2,1)S(1)}, u32[]{:S(2)}, u32[]{:S(2)}) %collective-permute-start.22) | collective-permute-done | bytes 393248 | tf_op jit(solution)/shard_map/ppermute | solution.py:436
  117.5 4.5 %shard_map.75 = bf16[8,128,512]{2,1,0:T(8,128)(2,1)S(1)} custom-call(f32[1,512]{1,0:T(1,128)S(1)} %get-tuple-element.117.eigen_ref, f32[14,128,128]{2,1,0:T(8,128)S(1)} %broadcast_in_dim.44.fluid_ref, bf16[3,128,512]{2,1,0:T(8,128)(2,1)S(1)} %collective-permute-done.21.up_ref, bf16[8,128,512]{2,1,0:T(8,128)(2,1)S(1)} %bitcast.42, ...), custom_call_target="tpu_custom_call" | custom-call | flops 367001600 | bytes 3670016 | tf_op jit(solution)/shard_map/pallas_call | solution.py:250
  122.2 2.2 %shard_map.79.refs_2_ = f32[1024,256]{1,0:T(8,128)S(1)} custom-call(s32[4]{0:T(128)S(1)} %pad_add_fusion.1.table, bf16[1024,512]{1,0:T(8,128)(2,1)S(1)} %bitcast.32, bf16[1024,512]{1,0:T(8,128)(2,1)S(1)} %bitcast.37, bf16[1024,512]{1,0:T(8,128)(2,1)S(1)} %collective-permute-done.23.refs_2_, bf16[1024,2048]{1,0:T(8,128)(2,1)S(1)} %copy-done), custom_call_target="tpu_custom_call" | custom-call | flops 1073741824 | bytes 5242880 | tf_op jit(solution)/shard_map/pallas_call | solution.py:306
  124.4 0.4 collective-permute-done.24.refs_3_.refs_0_
  124.8 1.6 shard_map.80
  126.5 5.0 %collective-permute-start.31 = (bf16[1024,128]{1,0:T(8,128)(2,1)S(1)}, bf16[1024,128]{1,0:T(8,128)(2,1)S(1)}, u32[]{:S(2)}, u32[]{:S(2)}) collective-permute-start(bf16[1024,128]{1,0:T(8,128)(2,1)S(1)} %get-tuple-element.110), channel_id=1, source_target_pairs={{0,28},{2,30},{4,24},{6,26},{8,20},{10,22},{12,16},{14,18},{16,12}... | collective-permute-start | bytes 786440 | tf_op jit(solution)/shard_map/ppermute | solution.py:334
  131.4 2.4 %shard_map.76 = (bf16[1024,128]{1,0:T(8,128)(2,1)S(1)}, bf16[1024,128]{1,0:T(8,128)(2,1)S(1)}) custom-call(s32[4]{0:T(128)S(1)} %pad_add_fusion.1.table, bf16[1024,512]{1,0:T(8,128)(2,1)S(1)} %bitcast.33, bf16[1024,512]{1,0:T(8,128)(2,1)S(1)} %bitcast.38, bf16[1024,512]{1,0:T(8,128)(2,1)S(1)} %collective-permute-done.23.refs_2_, ...), custom_call_target="tpu_custom_call" | custom-call | flops 1073741824 | bytes 5242880 | tf_op jit(solution)/shard_map/pallas_call | solution.py:306
  133.9 2.4 %shard_map.77 = (bf16[1024,128]{1,0:T(8,128)(2,1)S(1)}, bf16[1024,128]{1,0:T(8,128)(2,1)S(1)}) custom-call(s32[4]{0:T(128)S(1)} %pad_add_fusion.1.table, bf16[1024,512]{1,0:T(8,128)(2,1)S(1)} %bitcast.34, bf16[1024,512]{1,0:T(8,128)(2,1)S(1)} %bitcast.39, bf16[1024,512]{1,0:T(8,128)(2,1)S(1)} %collective-permute-done.23.refs_2_, ...), custom_call_target="tpu_custom_call" | custom-call | flops 1073741824 | bytes 5242880 | tf_op jit(solution)/shard_map/pallas_call | solution.py:306
  136.3 2.4 %shard_map.78 = (bf16[1024,128]{1,0:T(8,128)(2,1)S(1)}, bf16[1024,128]{1,0:T(8,128)(2,1)S(1)}) custom-call(s32[4]{0:T(128)S(1)} %pad_add_fusion.1.table, bf16[1024,512]{1,0:T(8,128)(2,1)S(1)} %bitcast.35, bf16[1024,512]{1,0:T(8,128)(2,1)S(1)} %bitcast.40, bf16[1024,512]{1,0:T(8,128)(2,1)S(1)} %collective-permute-done.23.refs_2_, ...), custom_call_target="tpu_custom_call" | custom-call | flops 1073741824 | bytes 5242880 | tf_op jit(solution)/shard_map/pallas_call | solution.py:306
  138.9 2.6 %collective-permute-start.26 = (bf16[1024,128]{1,0:T(8,128)(2,1)S(1)}, bf16[1024,128]{1,0:T(8,128)(2,1)S(1)}, u32[]{:S(2)}, u32[]{:S(2)}) collective-permute-start(bf16[1024,128]{1,0:T(8,128)(2,1)S(1)} %get-tuple-element.104), channel_id=1, source_target_pairs={{0,20},{2,22},{4,16},{6,18},{8,28},{10,30},{12,24},{14,26},{16,4},... | collective-permute-start | bytes 786440 | tf_op jit(solution)/shard_map/ppermute | solution.py:334
  141.5 18.3 %collective-permute-start.28 = (bf16[1024,128]{1,0:T(8,128)(2,1)S(1)}, bf16[1024,128]{1,0:T(8,128)(2,1)S(1)}, u32[]{:S(2)}, u32[]{:S(2)}) collective-permute-start(bf16[1024,128]{1,0:T(8,128)(2,1)S(1)} %get-tuple-element.106), channel_id=1, source_target_pairs={{0,12},{2,14},{4,8},{6,10},{8,4},{10,6},{12,0},{14,2},{16,28},{18,... | collective-permute-start | bytes 786440 | tf_op jit(solution)/shard_map/ppermute | solution.py:334
  159.8 0.6 collective-permute-start.29
  160.6 2.2 %shard_map.81.refs_2_ = f32[128,64,128]{2,1,0:T(8,128)} custom-call(s32[2]{0:T(128)S(1)} %pad_add_fusion.4.table, bf16[1024,128]{1,0:T(8,128)(2,1)S(1)} %collective-permute-done.30.refs_0_, bf16[1024,128]{1,0:T(8,128)(2,1)S(1)} %collective-permute-done.31.refs_1_), custom_call_target="tpu_custom_call" | custom-call | flops 262144 | bytes 1572864 | tf_op jit(solution)/shard_map/pallas_call | solution.py:94
  162.7 7.6 %collective-permute-done.29.refs_1_ = bf16[1024,128]{1,0:T(8,128)(2,1)S(1)} collective-permute-done((bf16[1024,128]{1,0:T(8,128)(2,1)S(1)}, bf16[1024,128]{1,0:T(8,128)(2,1)S(1)}, u32[]{:S(2)}, u32[]{:S(2)}) %collective-permute-start.29) | collective-permute-done | bytes 262176 | tf_op jit(solution)/shard_map/ppermute | solution.py:334
  170.3 2.2 %shard_map.82.refs_2_ = f32[128,64,128]{2,1,0:T(8,128)} custom-call(s32[2]{0:T(128)S(1)} %pad_add_fusion.3.table, bf16[1024,128]{1,0:T(8,128)(2,1)S(1)} %get-tuple-element.107.refs_0_, bf16[1024,128]{1,0:T(8,128)(2,1)S(1)} %collective-permute-done.29.refs_1_, f32[128,64,128]{2,1,0:T(8,128)} %shard_map.81.refs_2_), custom_call_target="tpu_custom_call", output_to_operand_aliasing={{}: (3, {})} | custom-call | flops 262144 | bytes 1572864 | tf_op jit(solution)/shard_map/pallas_call | solution.py:94
  172.5 2.2 %shard_map.83.refs_2_ = f32[128,64,128]{2,1,0:T(8,128)} custom-call(s32[2]{0:T(128)S(1)} %get-tuple-element.125.table, bf16[1024,128]{1,0:T(8,128)(2,1)S(1)} %collective-permute-done.27.refs_0_, bf16[1024,128]{1,0:T(8,128)(2,1)S(1)} %collective-permute-done.28.refs_1_, f32[128,64,128]{2,1,0:T(8,128)} %shard_map.82.refs_2_), custom_call_target="tpu_custom_call", output_to_operand_aliasing={{}: (3, {})} | custom-call | flops 262144 | bytes 1572864 | tf_op jit(solution)/shard_map/pallas_call | solution.py:94
  174.7 2.4 %collective-permute-done.26.refs_1_ = bf16[1024,128]{1,0:T(8,128)(2,1)S(1)} collective-permute-done((bf16[1024,128]{1,0:T(8,128)(2,1)S(1)}, bf16[1024,128]{1,0:T(8,128)(2,1)S(1)}, u32[]{:S(2)}, u32[]{:S(2)}) %collective-permute-start.26) | collective-permute-done | bytes 262176 | tf_op jit(solution)/shard_map/ppermute | solution.py:334
  177.1 2.2 %shard_map.84 = f32[128,64,128]{2,1,0:T(8,128)} custom-call(s32[2]{0:T(128)S(1)} %get-tuple-element.124.table, bf16[1024,128]{1,0:T(8,128)(2,1)S(1)} %collective-permute-done.25.refs_0_, bf16[1024,128]{1,0:T(8,128)(2,1)S(1)} %collective-permute-done.26.refs_1_, f32[128,64,128]{2,1,0:T(8,128)} %shard_map.83.refs_2_), custom_call_target="tpu_custom_call", output_to_operand_aliasing={{}: (3, {})} | custom-call | flops 262144 | bytes 1572864 | tf_op jit(solution)/shard_map/pallas_call | solution.py:94
  (58 shorter events, 1.2 us)
Async XLA Ops:
  0.0 25.5 %copy-start.3 = (bf16[128,2048]{1,0:T(8,128)(2,1)S(1)}, bf16[128,2048]{1,0:T(8,128)(2,1)}, u32[]{:S(2)}) copy-start(bf16[128,2048]{1,0:T(8,128)(2,1)} %refs_0_.1) | copy-start | bytes 1572868
  1.0 17.5 %collective-permute-start = (bf16[64,2048]{1,0:T(8,128)(2,1)S(1)}, bf16[64,2048]{1,0:T(8,128)(2,1)S(1)}, u32[]{:S(2)}, u32[]{:S(2)}) collective-permute-start(bf16[64,2048]{1,0:T(8,128)(2,1)S(1)} %constant_dynamic-slice_fusion), channel_id=1, source_target_pairs={{0,8},{2,10},{4,12},{6,14},{8,0},{10,2},{12,4},{14,6},{16,24},{18,... | collective-permute-start | bytes 786440 | tf_op jit(solution)/shard_map/ppermute | solution.py:334
  4.1 21.4 %collective-permute-start.1 = (bf16[64,2048]{1,0:T(8,128)(2,1)S(1)}, bf16[64,2048]{1,0:T(8,128)(2,1)S(1)}, u32[]{:S(2)}, u32[]{:S(2)}) collective-permute-start(bf16[64,2048]{1,0:T(8,128)(2,1)S(1)} %constant_dynamic-slice_fusion), channel_id=1, source_target_pairs={{0,16},{2,18},{4,20},{6,22},{8,24},{10,26},{12,28},{14,30},{16,0},... | collective-permute-start | bytes 786440 | tf_op jit(solution)/shard_map/ppermute | solution.py:334
  6.7 18.8 %collective-permute-start.2 = (bf16[64,2048]{1,0:T(8,128)(2,1)S(1)}, bf16[64,2048]{1,0:T(8,128)(2,1)S(1)}, u32[]{:S(2)}, u32[]{:S(2)}) collective-permute-start(bf16[64,2048]{1,0:T(8,128)(2,1)S(1)} %constant_dynamic-slice_fusion), channel_id=1, source_target_pairs={{0,24},{2,26},{4,28},{6,30},{8,16},{10,18},{12,20},{14,22},{16,8},... | collective-permute-start | bytes 786440 | tf_op jit(solution)/shard_map/ppermute | solution.py:334
  6.7 18.8 %collective-permute-start.3 = (bf16[128,2048]{1,0:T(8,128)(2,1)}, bf16[128,2048]{1,0:T(8,128)(2,1)S(1)}, u32[]{:S(2)}, u32[]{:S(2)}) collective-permute-start(bf16[128,2048]{1,0:T(8,128)(2,1)} %refs_0_.1), channel_id=1, source_target_pairs={{0,4},{2,6},{4,0},{6,2},{8,12},{10,14},{12,8},{14,10},{16,20},{18,... | collective-permute-start | bytes 1572872 | tf_op jit(solution)/shard_map/ppermute | solution.py:334
  8.5 1.8 %collective-permute-start.4 = (f32[128]{0:T(128)}, f32[128]{0:T(128)S(1)}, u32[]{:S(2)}, u32[]{:S(2)}) collective-permute-start(f32[128]{0:T(128)} %param.8), channel_id=1, source_target_pairs={{0,2},{2,0},{4,6},{6,4},{8,10},{10,8},{12,14},{14,12},{16,18},{18,... | collective-permute-start | bytes 1544 | tf_op jit(solution)/shard_map/ppermute | solution.py:335
  10.3 16.5 %collective-permute-start.5 = (f32[3,128]{1,0:T(4,128)S(1)}, f32[3,128]{1,0:T(4,128)S(1)}, u32[]{:S(2)}, u32[]{:S(2)}) collective-permute-start(f32[3,128]{1,0:T(4,128)S(1)} %get-tuple-element.116), channel_id=1, source_target_pairs={{0,1},{1,0},{2,3},{3,2},{4,5},{5,4},{6,7},{7,6},{8,9},{9,8},{10,11... | collective-permute-start | bytes 4616 | tf_op jit(solution)/shard_map/ppermute | solution.py:369
  18.5 8.3 %collective-permute-start.6 = (f32[3,128]{1,0:T(4,128)S(1)}, f32[3,128]{1,0:T(4,128)S(1)}, u32[]{:S(2)}, u32[]{:S(2)}) collective-permute-start(f32[3,128]{1,0:T(4,128)S(1)} %get-tuple-element.115), channel_id=1, source_target_pairs={{1,0},{0,1},{3,2},{2,3},{5,4},{4,5},{7,6},{6,7},{9,8},{8,9},{11,10... | collective-permute-start | bytes 4616 | tf_op jit(solution)/shard_map/ppermute | solution.py:370
  26.8 23.7 %collective-permute-start.9 = (bf16[1040,128]{1,0:T(8,128)(2,1)S(1)}, bf16[1040,128]{1,0:T(8,128)(2,1)S(1)}, u32[]{:S(2)}, u32[]{:S(2)}) collective-permute-start(bf16[1040,128]{1,0:T(8,128)(2,1)S(1)} %get-tuple-element.70), channel_id=1, source_target_pairs={{0,16},{2,18},{4,20},{6,22},{8,24},{10,26},{12,28},{14,30},{16,0},... | collective-permute-start | bytes 798728 | tf_op jit(solution)/shard_map/ppermute | solution.py:334
  32.7 23.4 %collective-permute-start.10 = (bf16[1040,128]{1,0:T(8,128)(2,1)S(1)}, bf16[1040,128]{1,0:T(8,128)(2,1)S(1)}, u32[]{:S(2)}, u32[]{:S(2)}) collective-permute-start(bf16[1040,128]{1,0:T(8,128)(2,1)S(1)} %get-tuple-element.71), channel_id=1, source_target_pairs={{0,20},{2,22},{4,16},{6,18},{8,28},{10,30},{12,24},{14,26},{16,4},... | collective-permute-start | bytes 798728 | tf_op jit(solution)/shard_map/ppermute | solution.py:334
  33.7 22.4 %collective-permute-start.11 = (bf16[1040,128]{1,0:T(8,128)(2,1)S(1)}, bf16[1040,128]{1,0:T(8,128)(2,1)S(1)}, u32[]{:S(2)}, u32[]{:S(2)}) collective-permute-start(bf16[1040,128]{1,0:T(8,128)(2,1)S(1)} %get-tuple-element.72), channel_id=1, source_target_pairs={{0,8},{2,10},{4,12},{6,14},{8,0},{10,2},{12,4},{14,6},{16,24},{18,... | collective-permute-start | bytes 798728 | tf_op jit(solution)/shard_map/ppermute | solution.py:334
  35.6 23.1 %collective-permute-start.7 = (bf16[192,2048]{1,0:T(8,128)(2,1)S(1)}, bf16[192,2048]{1,0:T(8,128)(2,1)S(1)}, u32[]{:S(2)}, u32[]{:S(2)}) collective-permute-start(bf16[192,2048]{1,0:T(8,128)(2,1)S(1)} %constant_dynamic-update-slice_fusion), channel_id=1, source_target_pairs={{0,4},{2,6},{4,0},{6,2},{8,12},{10,14},{12,8},{14,10},{16,20},{18,... | collective-permute-start | bytes 2359304 | tf_op jit(solution)/shard_map/ppermute | solution.py:334
  36.2 22.5 %collective-permute-start.8 = (bf16[192,2048]{1,0:T(8,128)(2,1)S(1)}, bf16[192,2048]{1,0:T(8,128)(2,1)S(1)}, u32[]{:S(2)}, u32[]{:S(2)}) collective-permute-start(bf16[192,2048]{1,0:T(8,128)(2,1)S(1)} %constant_dynamic-update-slice_fusion), channel_id=1, source_target_pairs={{0,1},{1,0},{2,3},{3,2},{4,5},{5,4},{6,7},{7,6},{8,9},{9,8},{10,11... | collective-permute-start | bytes 2359304 | tf_op jit(solution)/shard_map/ppermute | solution.py:336
  58.7 0.9 copy-start.1
  59.6 20.0 %collective-permute-start.13 = (bf16[1056,128]{1,0:T(8,128)(2,1)S(1)}, bf16[1056,128]{1,0:T(8,128)(2,1)}, u32[]{:S(2)}, u32[]{:S(2)}) collective-permute-start(bf16[1056,128]{1,0:T(8,128)(2,1)S(1)} %get-tuple-element.80), channel_id=1, source_target_pairs={{0,24},{2,26},{4,28},{6,30},{8,16},{10,18},{12,20},{14,22},{16,8},... | collective-permute-start | bytes 811016 | tf_op jit(solution)/shard_map/ppermute | solution.py:334
  62.0 17.5 %collective-permute-start.14 = (bf16[1056,128]{1,0:T(8,128)(2,1)S(1)}, bf16[1056,128]{1,0:T(8,128)(2,1)}, u32[]{:S(2)}, u32[]{:S(2)}) collective-permute-start(bf16[1056,128]{1,0:T(8,128)(2,1)S(1)} %get-tuple-element.81), channel_id=1, source_target_pairs={{0,28},{2,30},{4,24},{6,26},{8,20},{10,22},{12,16},{14,18},{16,12}... | collective-permute-start | bytes 811016 | tf_op jit(solution)/shard_map/ppermute | solution.py:334
  63.3 16.2 %collective-permute-start.15 = (bf16[1040,128]{1,0:T(8,128)(2,1)}, bf16[1040,128]{1,0:T(8,128)(2,1)}, u32[]{:S(2)}, u32[]{:S(2)}) collective-permute-start(bf16[1040,128]{1,0:T(8,128)(2,1)} %get-tuple-element.82), channel_id=1, source_target_pairs={{0,4},{2,6},{4,0},{6,2},{8,12},{10,14},{12,8},{14,10},{16,20},{18,... | collective-permute-start | bytes 798728 | tf_op jit(solution)/shard_map/ppermute | solution.py:334
  64.8 14.7 %collective-permute-start.16 = (bf16[1040,128]{1,0:T(8,128)(2,1)}, bf16[1040,128]{1,0:T(8,128)(2,1)}, u32[]{:S(2)}, u32[]{:S(2)}) collective-permute-start(bf16[1040,128]{1,0:T(8,128)(2,1)} %get-tuple-element.83), channel_id=1, source_target_pairs={{0,12},{2,14},{4,8},{6,10},{8,4},{10,6},{12,0},{14,2},{16,28},{18,... | collective-permute-start | bytes 798728 | tf_op jit(solution)/shard_map/ppermute | solution.py:334
  64.9 16.3 %collective-permute-start.12 = (bf16[192,2048]{1,0:T(8,128)(2,1)S(1)}, bf16[192,2048]{1,0:T(8,128)(2,1)S(1)}, u32[]{:S(2)}, u32[]{:S(2)}) collective-permute-start(bf16[192,2048]{1,0:T(8,128)(2,1)S(1)} %collective-permute-done.7.refs_0_), channel_id=1, source_target_pairs={{0,1},{1,0},{2,3},{3,2},{4,5},{5,4},{6,7},{7,6},{8,9},{9,8},{10,11... | collective-permute-start | bytes 2359304 | tf_op jit(solution)/shard_map/ppermute | solution.py:336
  66.3 1.1 copy-start.2
  85.6 4.5 %collective-permute-start.17 = (f32[1024,512]{1,0:T(8,128)}, f32[1024,512]{1,0:T(8,128)}, u32[]{:S(2)}, u32[]{:S(2)}) collective-permute-start(f32[1024,512]{1,0:T(8,128)} %shard_map.70), channel_id=1, source_target_pairs={{0,2},{2,0},{4,6},{6,4},{8,10},{10,8},{12,14},{14,12},{16,18},{18,... | collective-permute-start | bytes 6291464 | tf_op jit(solution)/shard_map/ppermute | solution.py:335
  89.2 6.0 %collective-permute-start.20 = (f32[1024,512]{1,0:T(8,128)}, f32[1024,512]{1,0:T(8,128)}, u32[]{:S(2)}, u32[]{:S(2)}) collective-permute-start(f32[1024,512]{1,0:T(8,128)} %shard_map.71), channel_id=1, source_target_pairs={{0,2},{2,0},{4,6},{6,4},{8,10},{10,8},{12,14},{14,12},{16,18},{18,... | collective-permute-start | bytes 6291464 | tf_op jit(solution)/shard_map/ppermute | solution.py:335
  93.1 12.0 %collective-permute-start.18 = (bf16[3,128,512]{2,1,0:T(8,128)(2,1)S(1)}, bf16[3,128,512]{2,1,0:T(8,128)(2,1)S(1)}, u32[]{:S(2)}, u32[]{:S(2)}) collective-permute-start(bf16[3,128,512]{2,1,0:T(8,128)(2,1)S(1)} %bitcast.45), channel_id=1, source_target_pairs={{0,4},{2,6},{4,12},{6,14},{12,8},{14,10},{8,16},{10,18},{16,20},{1... | collective-permute-start | bytes 1179656 | tf_op jit(solution)/shard_map/ppermute | solution.py:435
  94.7 15.2 %collective-permute-start.19 = (bf16[3,128,512]{2,1,0:T(8,128)(2,1)S(1)}, bf16[3,128,512]{2,1,0:T(8,128)(2,1)S(1)}, u32[]{:S(2)}, u32[]{:S(2)}) collective-permute-start(bf16[3,128,512]{2,1,0:T(8,128)(2,1)S(1)} %bitcast.43), channel_id=1, source_target_pairs={{4,0},{6,2},{12,4},{14,6},{8,12},{10,14},{16,8},{18,10},{20,16},{2... | collective-permute-start | bytes 1179656 | tf_op jit(solution)/shard_map/ppermute | solution.py:436
  98.2 16.6 %collective-permute-start.21 = (bf16[3,128,512]{2,1,0:T(8,128)(2,1)S(1)}, bf16[3,128,512]{2,1,0:T(8,128)(2,1)S(1)}, u32[]{:S(2)}, u32[]{:S(2)}) collective-permute-start(bf16[3,128,512]{2,1,0:T(8,128)(2,1)S(1)} %bitcast.46), channel_id=1, source_target_pairs={{0,4},{2,6},{4,12},{6,14},{12,8},{14,10},{8,16},{10,18},{16,20},{1... | collective-permute-start | bytes 1179656 | tf_op jit(solution)/shard_map/ppermute | solution.py:435
  103.0 14.5 %collective-permute-start.22 = (bf16[3,128,512]{2,1,0:T(8,128)(2,1)S(1)}, bf16[3,128,512]{2,1,0:T(8,128)(2,1)S(1)}, u32[]{:S(2)}, u32[]{:S(2)}) collective-permute-start(bf16[3,128,512]{2,1,0:T(8,128)(2,1)S(1)} %bitcast.44), channel_id=1, source_target_pairs={{4,0},{6,2},{12,4},{14,6},{8,12},{10,14},{16,8},{18,10},{20,16},{2... | collective-permute-start | bytes 1179656 | tf_op jit(solution)/shard_map/ppermute | solution.py:436
  109.9 12.3 %copy-start = (bf16[1024,2048]{1,0:T(8,128)(2,1)S(1)}, bf16[1024,2048]{1,0:T(8,128)(2,1)}, u32[]{:S(2)}) copy-start(bf16[1024,2048]{1,0:T(8,128)(2,1)} %shard_map.69.b_ref.refs_4_.refs_3_.refs_1_) | copy-start | bytes 12582916
  114.7 7.5 %collective-permute-start.23 = (bf16[1024,512]{1,0:T(8,128)(2,1)S(1)}, bf16[1024,512]{1,0:T(8,128)(2,1)S(1)}, u32[]{:S(2)}, u32[]{:S(2)}) collective-permute-start(bf16[1024,512]{1,0:T(8,128)(2,1)S(1)} %bitcast.31), channel_id=1, source_target_pairs={{0,2},{2,0},{4,6},{6,4},{8,10},{10,8},{12,14},{14,12},{16,18},{18,... | collective-permute-start | bytes 3145736 | tf_op jit(solution)/shard_map/ppermute | solution.py:335
  122.0 2.7 %collective-permute-start.24 = (bf16[1024,512]{1,0:T(8,128)(2,1)S(1)}, bf16[1024,512]{1,0:T(8,128)(2,1)S(1)}, u32[]{:S(2)}, u32[]{:S(2)}) collective-permute-start(bf16[1024,512]{1,0:T(8,128)(2,1)S(1)} %bitcast.36), channel_id=1, source_target_pairs={{0,2},{2,0},{4,6},{6,4},{8,10},{10,8},{12,14},{14,12},{16,18},{18,... | collective-permute-start | bytes 3145736 | tf_op jit(solution)/shard_map/ppermute | solution.py:335
  126.4 15.1 %collective-permute-start.30 = (bf16[1024,128]{1,0:T(8,128)(2,1)S(1)}, bf16[1024,128]{1,0:T(8,128)(2,1)S(1)}, u32[]{:S(2)}, u32[]{:S(2)}) collective-permute-start(bf16[1024,128]{1,0:T(8,128)(2,1)S(1)} %get-tuple-element.109), channel_id=1, source_target_pairs={{0,24},{2,26},{4,28},{6,30},{8,16},{10,18},{12,20},{14,22},{16,8},... | collective-permute-start | bytes 786440 | tf_op jit(solution)/shard_map/ppermute | solution.py:334
  126.5 33.3 %collective-permute-start.31 = (bf16[1024,128]{1,0:T(8,128)(2,1)S(1)}, bf16[1024,128]{1,0:T(8,128)(2,1)S(1)}, u32[]{:S(2)}, u32[]{:S(2)}) collective-permute-start(bf16[1024,128]{1,0:T(8,128)(2,1)S(1)} %get-tuple-element.110), channel_id=1, source_target_pairs={{0,28},{2,30},{4,24},{6,26},{8,20},{10,22},{12,16},{14,18},{16,12}... | collective-permute-start | bytes 786440 | tf_op jit(solution)/shard_map/ppermute | solution.py:334
  138.8 35.9 %collective-permute-start.25 = (bf16[1024,128]{1,0:T(8,128)(2,1)S(1)}, bf16[1024,128]{1,0:T(8,128)(2,1)S(1)}, u32[]{:S(2)}, u32[]{:S(2)}) collective-permute-start(bf16[1024,128]{1,0:T(8,128)(2,1)S(1)} %get-tuple-element.103), channel_id=1, source_target_pairs={{0,16},{2,18},{4,20},{6,22},{8,24},{10,26},{12,28},{14,30},{16,0},... | collective-permute-start | bytes 786440 | tf_op jit(solution)/shard_map/ppermute | solution.py:334
  138.9 38.2 %collective-permute-start.26 = (bf16[1024,128]{1,0:T(8,128)(2,1)S(1)}, bf16[1024,128]{1,0:T(8,128)(2,1)S(1)}, u32[]{:S(2)}, u32[]{:S(2)}) collective-permute-start(bf16[1024,128]{1,0:T(8,128)(2,1)S(1)} %get-tuple-element.104), channel_id=1, source_target_pairs={{0,20},{2,22},{4,16},{6,18},{8,28},{10,30},{12,24},{14,26},{16,4},... | collective-permute-start | bytes 786440 | tf_op jit(solution)/shard_map/ppermute | solution.py:334
  141.5 31.0 %collective-permute-start.27 = (bf16[1024,128]{1,0:T(8,128)(2,1)S(1)}, bf16[1024,128]{1,0:T(8,128)(2,1)S(1)}, u32[]{:S(2)}, u32[]{:S(2)}) collective-permute-start(bf16[1024,128]{1,0:T(8,128)(2,1)S(1)} %get-tuple-element.105), channel_id=1, source_target_pairs={{0,8},{2,10},{4,12},{6,14},{8,0},{10,2},{12,4},{14,6},{16,24},{18,... | collective-permute-start | bytes 786440 | tf_op jit(solution)/shard_map/ppermute | solution.py:334
  141.5 31.0 %collective-permute-start.28 = (bf16[1024,128]{1,0:T(8,128)(2,1)S(1)}, bf16[1024,128]{1,0:T(8,128)(2,1)S(1)}, u32[]{:S(2)}, u32[]{:S(2)}) collective-permute-start(bf16[1024,128]{1,0:T(8,128)(2,1)S(1)} %get-tuple-element.106), channel_id=1, source_target_pairs={{0,12},{2,14},{4,8},{6,10},{8,4},{10,6},{12,0},{14,2},{16,28},{18,... | collective-permute-start | bytes 786440 | tf_op jit(solution)/shard_map/ppermute | solution.py:334
  159.8 10.5 %collective-permute-start.29 = (bf16[1024,128]{1,0:T(8,128)(2,1)S(1)}, bf16[1024,128]{1,0:T(8,128)(2,1)S(1)}, u32[]{:S(2)}, u32[]{:S(2)}) collective-permute-start(bf16[1024,128]{1,0:T(8,128)(2,1)S(1)} %get-tuple-element.108), channel_id=1, source_target_pairs={{0,4},{2,6},{4,0},{6,2},{8,12},{10,14},{12,8},{14,10},{16,20},{18,... | collective-permute-start | bytes 786440 | tf_op jit(solution)/shard_map/ppermute | solution.py:334
